TPU v7x, 32 devices: a whole 2x2x4 slice. The times are simulated.
32 devices in a mesh: groups: 2 (over x), nodes: 16 (over z, y, core).
Axes of the slice: x: 2, y: 2, z: 4, core: 2. Of those that a mesh axis runs over, the one named last changes fastest.
Arguments:
- node_feats: bfloat16 [8192, 256], P(('groups', 'nodes')), parts along dimension 0, may hold values from -6 to 6
- norm_gain: float32 [256], replicated, may hold values from 0.1 to 1.9
- w_query: bfloat16 [256, 256], replicated, may hold values from -0.375 to 0.375
- w_key: bfloat16 [256, 256], replicated, may hold values from -0.375 to 0.375
- w_value: bfloat16 [256, 256], replicated, may hold values from -0.375 to 0.375
- w_out: bfloat16 [256, 256], replicated, may hold values from -0.375 to 0.375
- cotangent: bfloat16 [8192, 256], P(('groups', 'nodes')), parts along dimension 0, may hold values from -6 to 6
- edge_dst: int32 [1536, 128], P(('groups', 'nodes')), parts along dimension 0, may hold values from 0 to 255
- edge_src: int32 [1536, 128], P(('groups', 'nodes')), parts along dimension 0, may hold values from 0 to 319, as said below
- edge_mask: int32 [1536, 128], P(('groups', 'nodes')), parts along dimension 0, may hold values from 0 to 1, as said below
- send_rows: int32 [32, 16, 4], P(('groups', 'nodes')), parts along dimension 0, may hold values from 0 to 255
Outputs:
- output: bfloat16 [8192, 256], P(('groups', 'nodes')), parts along dimension 0
- grad_feats: float32 [8192, 256], P(('groups', 'nodes')), parts along dimension 0
- grad_gain: float32 [512], P('groups'), parts along dimension 0
- grad_query: float32 [512, 256], P('groups'), parts along dimension 0
- grad_key: float32 [512, 256], P('groups'), parts along dimension 0
- grad_value: float32 [512, 256], P('groups'), parts along dimension 0
- grad_out: float32 [512, 256], P('groups'), parts along dimension 0
There are 2 independent parts, one for each index of `groups`. A program takes and returns all parts, laid end to end along the dimension named above; an argument that names none is the same for every part. Nothing has to cross between parts.
Inputs may be any that keep to these rules, and one draw needn't show every extreme that they name: `edge_src`: an index below 256 is a row of the same partition; 256 + s * 4 + c is slot c of the rows that partition s sends to this one. `edge_mask`: within each partition the edges fill its 48 blocks from the front; on at least one partition every slot holds an edge. `send_rows`: entry [s, p, c] is the row of partition s that it sends to partition p in slot c.
All inputs are finite; a program needn't handle non-finite values.
Results may differ from a plain program's by a relative error of at most 0.012.
Values may be sent and summed in bfloat16 or wider, within the bound.
No kernel may reach another device: no remote copies, remote signals or barrier semaphores. Data moves between devices by JAX's collectives and lax.ppermute only.
A program may use at most 64 MiB of HBM per device.

v0:
```python
import math

import jax
import jax.numpy as jnp
from jax import lax
from jax.sharding import PartitionSpec as P

HEADS = 8


def layer_norm(feats, norm_gain):
    average = jnp.mean(feats, axis=1, keepdims=True)
    centered = feats - average
    variance = jnp.mean(centered * centered, axis=1, keepdims=True)
    return centered * lax.rsqrt(variance + 1e-05) * norm_gain


def head_table(features, head_count):
    head_size = features // head_count
    column = jnp.arange(features, dtype=jnp.int32)[:, None] // head_size
    return (column == jnp.arange(head_count, dtype=jnp.int32)[None, :]).astype(jnp.float32)


def block_terms(query_rows, pair_rows, validity, head_map):
    features = query_rows.shape[1]
    head_size = features // head_map.shape[1]
    highest = lax.Precision.HIGHEST
    key_rows = pair_rows[:, :features]
    value_rows = pair_rows[:, features:]
    logits = jnp.dot(query_rows * key_rows, head_map, precision=highest) / math.sqrt(head_size)
    weight = jnp.exp(5.0 * jnp.tanh(logits / 5.0)) * validity[:, None]
    numerator = jnp.dot(weight, head_map.T, precision=highest) * value_rows
    return (numerator, weight)


def on_device(
    node_feats,
    norm_gain,
    w_query,
    w_key,
    w_value,
    w_out,
    cotangent,
    edge_dst,
    edge_src,
    edge_mask,
    send_rows,
):
    row_count, features = node_feats.shape
    peer_count = send_rows.shape[1]
    slot_count = send_rows.shape[2]
    highest = lax.Precision.HIGHEST
    head_map = head_table(features, HEADS)
    feats32 = node_feats.astype(jnp.float32)
    normed = layer_norm(feats32, norm_gain).astype(jnp.bfloat16)
    w_pair = jnp.concatenate([w_key, w_value], axis=1)
    queries = jnp.dot(normed, w_query, preferred_element_type=jnp.float32).astype(jnp.bfloat16)
    key_val = jnp.dot(normed, w_pair, preferred_element_type=jnp.float32).astype(jnp.bfloat16)
    send_index = send_rows[0].reshape(-1)
    outgoing = key_val[send_index].reshape(peer_count, slot_count, 2 * features)
    arrived = lax.all_to_all(outgoing, "nodes", split_axis=0, concat_axis=0, tiled=True)
    remote = arrived.reshape(-1, 2 * features)
    pair32 = key_val.astype(jnp.float32)
    table32 = jnp.concatenate([pair32, remote.astype(jnp.float32)], axis=0)
    query32 = queries.astype(jnp.float32)
    edge_step = 8 * 128
    target_all = edge_dst.reshape(-1, edge_step)
    source_all = edge_src.reshape(-1, edge_step)
    valid_all = edge_mask.reshape(-1, edge_step).astype(jnp.float32)
    turn_count = target_all.shape[0]
    unit_mask = jnp.ones((row_count,), jnp.float32)
    num_self, den_self = block_terms(query32, pair32, unit_mask, head_map)

    def forward_step(turn_index, running):
        numerator, denominator = running
        targets = target_all[turn_index]
        sources = source_all[turn_index]
        num_part, den_part = block_terms(
            query32[targets], table32[sources], valid_all[turn_index], head_map
        )
        return (numerator.at[targets].add(num_part), denominator.at[targets].add(den_part))

    numerator, denominator = lax.fori_loop(0, turn_count, forward_step, (num_self, den_self))
    den_wide = jnp.dot(denominator, head_map.T, precision=highest)
    attended32 = numerator / den_wide
    attended = attended32.astype(jnp.bfloat16)
    output = (feats32 + jnp.dot(attended, w_out, preferred_element_type=jnp.float32)).astype(
        jnp.bfloat16
    )
    grad_out = jnp.dot(attended.T, cotangent, preferred_element_type=jnp.float32)
    d_attended = (
        jnp.dot(cotangent, w_out.T, preferred_element_type=jnp.float32)
        .astype(jnp.bfloat16)
        .astype(jnp.float32)
    )
    d_num = d_attended / den_wide
    d_den = -jnp.dot(d_attended * attended32, head_map, precision=highest) / denominator

    def self_terms(query_rows, pair_rows):
        return block_terms(query_rows, pair_rows, unit_mask, head_map)

    _, pullback = jax.vjp(self_terms, query32, pair32)
    dq_self, dpair_self = pullback((d_num, d_den))
    dpair_start = jnp.concatenate(
        [dpair_self, jnp.zeros((peer_count * slot_count, 2 * features), jnp.float32)], axis=0
    )

    def backward_step(turn_index, running):
        dq_acc, dpair_acc = running
        targets = target_all[turn_index]
        sources = source_all[turn_index]
        validity = valid_all[turn_index]

        def edge_terms(query_rows, pair_rows):
            return block_terms(query_rows, pair_rows, validity, head_map)

        _, pull_edges = jax.vjp(edge_terms, query32[targets], table32[sources])
        dq_rows, dpair_rows = pull_edges((d_num[targets], d_den[targets]))
        return (dq_acc.at[targets].add(dq_rows), dpair_acc.at[sources].add(dpair_rows))

    dq_acc, dpair_acc = lax.fori_loop(0, turn_count, backward_step, (dq_self, dpair_start))
    dq_low = dq_acc.astype(jnp.bfloat16)
    normed32 = normed.astype(jnp.float32)
    w_pair32 = w_pair.astype(jnp.float32)
    grad_query = jnp.dot(normed.T, dq_low, preferred_element_type=jnp.float32)
    d_normed = jnp.dot(dq_low, w_query.T, preferred_element_type=jnp.float32)
    returned = lax.all_to_all(
        dpair_acc[row_count:].reshape(peer_count, slot_count, 2 * features).astype(jnp.bfloat16),
        "nodes",
        split_axis=0,
        concat_axis=0,
        tiled=True,
    ).astype(jnp.float32)
    dpair_local = dpair_acc[:row_count].at[send_index].add(returned.reshape(-1, 2 * features))
    grad_pair = jnp.dot(normed32.T, dpair_local, precision=highest)
    d_normed = d_normed + jnp.dot(dpair_local, w_pair32.T, precision=highest)
    grad_key = grad_pair[:, :features]
    grad_value = grad_pair[:, features:]
    _, pull_norm = jax.vjp(layer_norm, feats32, norm_gain)
    dx_norm, gain_term = pull_norm(d_normed)
    grad_feats = cotangent.astype(jnp.float32) + dx_norm
    totals = lax.psum((gain_term, grad_query, grad_key, grad_value, grad_out), "nodes")
    return (output, grad_feats, totals[0], totals[1], totals[2], totals[3], totals[4])


def solution(mesh):
    in_specs = (
        P(("groups", "nodes"), None),
        P(),
        P(),
        P(),
        P(),
        P(),
        P(("groups", "nodes"), None),
        P(("groups", "nodes"), None),
        P(("groups", "nodes"), None),
        P(("groups", "nodes"), None),
        P(("groups", "nodes"), None, None),
    )
    out_specs = (
        P(("groups", "nodes"), None),
        P(("groups", "nodes"), None),
        P("groups"),
        P("groups", None),
        P("groups", None),
        P("groups", None),
        P("groups", None),
    )
    return jax.shard_map(
        on_device, mesh=mesh, in_specs=in_specs, out_specs=out_specs, check_vma=False
    )
```

profile of v0, /device:TPU:1, one launch (start us, length us, event | category | flops | bytes accessed | tf_op | source)
XLA Modules:
  0.0 560.4 jit_solution(1865772341581998561)
XLA Ops:
  15.4 7.3 %all-to-all-start = ((bf16[16,4,512]{2,1,0:T(4,128)(2,1)}), bf16[16,4,512]{2,1,0:T(4,128)(2,1)S(1)}, u32[]{:S(2)}, u32[]{:S(2)}) async-start(bf16[16,4,512]{2,1,0:T(4,128)(2,1)} %reshape.287), calls=%async_computation | async-start | bytes 131072 | tf_op jit(solution)/shard_map/all_to_all | solution.py:61
  28.9 151.4 %while.39 = (s32[]{:T(128)}, f32[256,256]{1,0:T(8,128)S(1)}, f32[256,8]{1,0:T(8,128)S(1)}, s32[6,1024]{1,0:T(8,128)S(1)}, f32[256,256]{1,0:T(8,128)S(1)}, /*inde...) while((s32[]{:T(128)}, f32[256,256]{1,0:T(8,128)S(1)}, ...), condition=%wide.region_5.6_spmd.clone.clone, body=%wide.region_2.5_spmd.clone.clone.sunk | while | flops 51167232 | bytes 22313104 | solution.py:83
  41.7 6.2 %scatter_fusion = f32[256,256]{1,0:T(8,128)S(1)} fusion(f32[256,256]{1,0:T(8,128)S(1)} %get-tuple-element.876, s32[1024]{0:T(1024)S(1)} %bitcast.51, f32[1024,256]{1,0:T(8,128)S(1)} %convolution_multiply_fusion.7), kind=kCustom, calls=%fused_computation.7.clone.clone.1 | custom fusion | flops 262144 | bytes 3149824 | tf_op jit(solution)/shard_map/while/body/eval_jaxpr/scatter-add | solution.py:81
  48.1 6.1 %scatter_fusion.1 = f32[256,8]{1,0:T(8,128)S(1)} fusion(f32[256,8]{1,0:T(8,128)S(1)} %get-tuple-element.877, s32[1024]{0:T(1024)S(1)} %bitcast.52, f32[1024,8]{1,0:T(8,128)S(1)} %copy.35), kind=kCustom, calls=%fused_computation.8.clone.clone.1 | custom fusion | flops 8192 | bytes 102400 | tf_op jit(solution)/shard_map/while/body/eval_jaxpr/scatter-add | solution.py:81
  58.5 4.9 gather_fusion.1
  66.9 6.2 %scatter_fusion = f32[256,256]{1,0:T(8,128)S(1)} fusion(f32[256,256]{1,0:T(8,128)S(1)} %get-tuple-element.876, s32[1024]{0:T(1024)S(1)} %bitcast.51, f32[1024,256]{1,0:T(8,128)S(1)} %convolution_multiply_fusion.7), kind=kCustom, calls=%fused_computation.7.clone.clone.1 | custom fusion | flops 262144 | bytes 3149824 | tf_op jit(solution)/shard_map/while/body/eval_jaxpr/scatter-add | solution.py:81
  73.3 6.1 %scatter_fusion.1 = f32[256,8]{1,0:T(8,128)S(1)} fusion(f32[256,8]{1,0:T(8,128)S(1)} %get-tuple-element.877, s32[1024]{0:T(1024)S(1)} %bitcast.52, f32[1024,8]{1,0:T(8,128)S(1)} %copy.35), kind=kCustom, calls=%fused_computation.8.clone.clone.1 | custom fusion | flops 8192 | bytes 102400 | tf_op jit(solution)/shard_map/while/body/eval_jaxpr/scatter-add | solution.py:81
  92.1 6.2 %scatter_fusion = f32[256,256]{1,0:T(8,128)S(1)} fusion(f32[256,256]{1,0:T(8,128)S(1)} %get-tuple-element.876, s32[1024]{0:T(1024)S(1)} %bitcast.51, f32[1024,256]{1,0:T(8,128)S(1)} %convolution_multiply_fusion.7), kind=kCustom, calls=%fused_computation.7.clone.clone.1 | custom fusion | flops 262144 | bytes 3149824 | tf_op jit(solution)/shard_map/while/body/eval_jaxpr/scatter-add | solution.py:81
  98.5 6.1 %scatter_fusion.1 = f32[256,8]{1,0:T(8,128)S(1)} fusion(f32[256,8]{1,0:T(8,128)S(1)} %get-tuple-element.877, s32[1024]{0:T(1024)S(1)} %bitcast.52, f32[1024,8]{1,0:T(8,128)S(1)} %copy.35), kind=kCustom, calls=%fused_computation.8.clone.clone.1 | custom fusion | flops 8192 | bytes 102400 | tf_op jit(solution)/shard_map/while/body/eval_jaxpr/scatter-add | solution.py:81
  117.4 6.2 %scatter_fusion = f32[256,256]{1,0:T(8,128)S(1)} fusion(f32[256,256]{1,0:T(8,128)S(1)} %get-tuple-element.876, s32[1024]{0:T(1024)S(1)} %bitcast.51, f32[1024,256]{1,0:T(8,128)S(1)} %convolution_multiply_fusion.7), kind=kCustom, calls=%fused_computation.7.clone.clone.1 | custom fusion | flops 262144 | bytes 3149824 | tf_op jit(solution)/shard_map/while/body/eval_jaxpr/scatter-add | solution.py:81
  123.8 6.1 %scatter_fusion.1 = f32[256,8]{1,0:T(8,128)S(1)} fusion(f32[256,8]{1,0:T(8,128)S(1)} %get-tuple-element.877, s32[1024]{0:T(1024)S(1)} %bitcast.52, f32[1024,8]{1,0:T(8,128)S(1)} %copy.35), kind=kCustom, calls=%fused_computation.8.clone.clone.1 | custom fusion | flops 8192 | bytes 102400 | tf_op jit(solution)/shard_map/while/body/eval_jaxpr/scatter-add | solution.py:81
  134.2 4.9 gather_fusion.1
  142.6 6.2 %scatter_fusion = f32[256,256]{1,0:T(8,128)S(1)} fusion(f32[256,256]{1,0:T(8,128)S(1)} %get-tuple-element.876, s32[1024]{0:T(1024)S(1)} %bitcast.51, f32[1024,256]{1,0:T(8,128)S(1)} %convolution_multiply_fusion.7), kind=kCustom, calls=%fused_computation.7.clone.clone.1 | custom fusion | flops 262144 | bytes 3149824 | tf_op jit(solution)/shard_map/while/body/eval_jaxpr/scatter-add | solution.py:81
  149.0 6.1 %scatter_fusion.1 = f32[256,8]{1,0:T(8,128)S(1)} fusion(f32[256,8]{1,0:T(8,128)S(1)} %get-tuple-element.877, s32[1024]{0:T(1024)S(1)} %bitcast.52, f32[1024,8]{1,0:T(8,128)S(1)} %copy.35), kind=kCustom, calls=%fused_computation.8.clone.clone.1 | custom fusion | flops 8192 | bytes 102400 | tf_op jit(solution)/shard_map/while/body/eval_jaxpr/scatter-add | solution.py:81
  159.4 4.9 gather_fusion.1
  167.8 6.2 %scatter_fusion = f32[256,256]{1,0:T(8,128)S(1)} fusion(f32[256,256]{1,0:T(8,128)S(1)} %get-tuple-element.876, s32[1024]{0:T(1024)S(1)} %bitcast.51, f32[1024,256]{1,0:T(8,128)S(1)} %convolution_multiply_fusion.7), kind=kCustom, calls=%fused_computation.7.clone.clone.1 | custom fusion | flops 262144 | bytes 3149824 | tf_op jit(solution)/shard_map/while/body/eval_jaxpr/scatter-add | solution.py:81
  174.2 6.1 %scatter_fusion.1 = f32[256,8]{1,0:T(8,128)S(1)} fusion(f32[256,8]{1,0:T(8,128)S(1)} %get-tuple-element.877, s32[1024]{0:T(1024)S(1)} %bitcast.52, f32[1024,8]{1,0:T(8,128)S(1)} %copy.35), kind=kCustom, calls=%fused_computation.8.clone.clone.1 | custom fusion | flops 8192 | bytes 102400 | tf_op jit(solution)/shard_map/while/body/eval_jaxpr/scatter-add | solution.py:81
  185.7 252.3 %while.40 = (s32[]{:T(128)}, f32[256,256]{1,0:T(8,128)S(1)}, f32[320,512]{1,0:T(8,128)}, s32[6,1024]{1,0:T(8,128)}, f32[256,8]{1,0:T(8,128)S(1)}, /*index=5*/f32...) while((s32[]{:T(128)}, f32[256,256]{1,0:T(8,128)S(1)}, ...), condition=%wide.region_9.10_spmd.clone.clone, body=%wide.region_6.9_spmd.clone.clone.sunk | while | flops 103415808 | bytes 35918532 | solution.py:121
  209.5 6.9 %scatter_custom_fusion.21 = f32[256,256]{1,0:T(8,128)S(1)} fusion(f32[256,256]{1,0:T(8,128)S(1)} %get-tuple-element.909, s32[1024]{0:T(1024)S(1)} %bitcast.59, f32[1024,256]{1,0:T(8,128)} %get-tuple-element.863, f32[1024,512]{1,0:T(8,128)} %gather_fusion.5), kind=kCustom, calls=%fused_computation.45.clone.1 | custom fusion | flops 524288 | bytes 2359296 | tf_op jit(solution)/shard_map/while/body/eval_jaxpr/scatter-add | solution.py:119
  218.5 9.2 %scatter_custom_fusion.22 = f32[320,512]{1,0:T(8,128)} fusion(f32[320,512]{1,0:T(8,128)} %get-tuple-element.910, s32[1024]{0:T(1024)S(1)} %bitcast.57, f32[1024,256]{1,0:T(8,128)} %get-tuple-element.864, f32[]{:T(128)} %constant.222.clone.1..sunk, f32[1024,256]{1,0:T(8,128)} %convolution_multiply_fusion.8), kind=kCustom, calls=%fused_computation.31.clone.1 | custom fusion | flops 1048576 | bytes 2753024 | tf_op jit(solution)/shard_map/while/body/eval_jaxpr/scatter-add | solution.py:119
  251.6 6.9 %scatter_custom_fusion.21 = f32[256,256]{1,0:T(8,128)S(1)} fusion(f32[256,256]{1,0:T(8,128)S(1)} %get-tuple-element.909, s32[1024]{0:T(1024)S(1)} %bitcast.59, f32[1024,256]{1,0:T(8,128)} %get-tuple-element.863, f32[1024,512]{1,0:T(8,128)} %gather_fusion.5), kind=kCustom, calls=%fused_computation.45.clone.1 | custom fusion | flops 524288 | bytes 2359296 | tf_op jit(solution)/shard_map/while/body/eval_jaxpr/scatter-add | solution.py:119
  260.6 9.2 %scatter_custom_fusion.22 = f32[320,512]{1,0:T(8,128)} fusion(f32[320,512]{1,0:T(8,128)} %get-tuple-element.910, s32[1024]{0:T(1024)S(1)} %bitcast.57, f32[1024,256]{1,0:T(8,128)} %get-tuple-element.864, f32[]{:T(128)} %constant.222.clone.1..sunk, f32[1024,256]{1,0:T(8,128)} %convolution_multiply_fusion.8), kind=kCustom, calls=%fused_computation.31.clone.1 | custom fusion | flops 1048576 | bytes 2753024 | tf_op jit(solution)/shard_map/while/body/eval_jaxpr/scatter-add | solution.py:119
  293.6 6.9 %scatter_custom_fusion.21 = f32[256,256]{1,0:T(8,128)S(1)} fusion(f32[256,256]{1,0:T(8,128)S(1)} %get-tuple-element.909, s32[1024]{0:T(1024)S(1)} %bitcast.59, f32[1024,256]{1,0:T(8,128)} %get-tuple-element.863, f32[1024,512]{1,0:T(8,128)} %gather_fusion.5), kind=kCustom, calls=%fused_computation.45.clone.1 | custom fusion | flops 524288 | bytes 2359296 | tf_op jit(solution)/shard_map/while/body/eval_jaxpr/scatter-add | solution.py:119
  302.6 9.2 %scatter_custom_fusion.22 = f32[320,512]{1,0:T(8,128)} fusion(f32[320,512]{1,0:T(8,128)} %get-tuple-element.910, s32[1024]{0:T(1024)S(1)} %bitcast.57, f32[1024,256]{1,0:T(8,128)} %get-tuple-element.864, f32[]{:T(128)} %constant.222.clone.1..sunk, f32[1024,256]{1,0:T(8,128)} %convolution_multiply_fusion.8), kind=kCustom, calls=%fused_computation.31.clone.1 | custom fusion | flops 1048576 | bytes 2753024 | tf_op jit(solution)/shard_map/while/body/eval_jaxpr/scatter-add | solution.py:119
  335.7 6.9 %scatter_custom_fusion.21 = f32[256,256]{1,0:T(8,128)S(1)} fusion(f32[256,256]{1,0:T(8,128)S(1)} %get-tuple-element.909, s32[1024]{0:T(1024)S(1)} %bitcast.59, f32[1024,256]{1,0:T(8,128)} %get-tuple-element.863, f32[1024,512]{1,0:T(8,128)} %gather_fusion.5), kind=kCustom, calls=%fused_computation.45.clone.1 | custom fusion | flops 524288 | bytes 2359296 | tf_op jit(solution)/shard_map/while/body/eval_jaxpr/scatter-add | solution.py:119
  344.7 9.2 %scatter_custom_fusion.22 = f32[320,512]{1,0:T(8,128)} fusion(f32[320,512]{1,0:T(8,128)} %get-tuple-element.910, s32[1024]{0:T(1024)S(1)} %bitcast.57, f32[1024,256]{1,0:T(8,128)} %get-tuple-element.864, f32[]{:T(128)} %constant.222.clone.1..sunk, f32[1024,256]{1,0:T(8,128)} %convolution_multiply_fusion.8), kind=kCustom, calls=%fused_computation.31.clone.1 | custom fusion | flops 1048576 | bytes 2753024 | tf_op jit(solution)/shard_map/while/body/eval_jaxpr/scatter-add | solution.py:119
  377.7 6.9 %scatter_custom_fusion.21 = f32[256,256]{1,0:T(8,128)S(1)} fusion(f32[256,256]{1,0:T(8,128)S(1)} %get-tuple-element.909, s32[1024]{0:T(1024)S(1)} %bitcast.59, f32[1024,256]{1,0:T(8,128)} %get-tuple-element.863, f32[1024,512]{1,0:T(8,128)} %gather_fusion.5), kind=kCustom, calls=%fused_computation.45.clone.1 | custom fusion | flops 524288 | bytes 2359296 | tf_op jit(solution)/shard_map/while/body/eval_jaxpr/scatter-add | solution.py:119
  386.7 9.2 %scatter_custom_fusion.22 = f32[320,512]{1,0:T(8,128)} fusion(f32[320,512]{1,0:T(8,128)} %get-tuple-element.910, s32[1024]{0:T(1024)S(1)} %bitcast.57, f32[1024,256]{1,0:T(8,128)} %get-tuple-element.864, f32[]{:T(128)} %constant.222.clone.1..sunk, f32[1024,256]{1,0:T(8,128)} %convolution_multiply_fusion.8), kind=kCustom, calls=%fused_computation.31.clone.1 | custom fusion | flops 1048576 | bytes 2753024 | tf_op jit(solution)/shard_map/while/body/eval_jaxpr/scatter-add | solution.py:119
  419.8 6.9 %scatter_custom_fusion.21 = f32[256,256]{1,0:T(8,128)S(1)} fusion(f32[256,256]{1,0:T(8,128)S(1)} %get-tuple-element.909, s32[1024]{0:T(1024)S(1)} %bitcast.59, f32[1024,256]{1,0:T(8,128)} %get-tuple-element.863, f32[1024,512]{1,0:T(8,128)} %gather_fusion.5), kind=kCustom, calls=%fused_computation.45.clone.1 | custom fusion | flops 524288 | bytes 2359296 | tf_op jit(solution)/shard_map/while/body/eval_jaxpr/scatter-add | solution.py:119
  428.8 9.2 %scatter_custom_fusion.22 = f32[320,512]{1,0:T(8,128)} fusion(f32[320,512]{1,0:T(8,128)} %get-tuple-element.910, s32[1024]{0:T(1024)S(1)} %bitcast.57, f32[1024,256]{1,0:T(8,128)} %get-tuple-element.864, f32[]{:T(128)} %constant.222.clone.1..sunk, f32[1024,256]{1,0:T(8,128)} %convolution_multiply_fusion.8), kind=kCustom, calls=%fused_computation.31.clone.1 | custom fusion | flops 1048576 | bytes 2753024 | tf_op jit(solution)/shard_map/while/body/eval_jaxpr/scatter-add | solution.py:119
  456.4 30.7 %psum.35 = f32[256]{0:T(256)} all-reduce(f32[256]{0:T(256)S(1)} %get-tuple-element.664), channel_id=1, replica_groups=mesh['groups'=2,'nodes'=16] {'nodes'}, use_global_device_ids=true, to_apply=%region_14.15 | all-reduce | flops 256 | bytes 2048 | tf_op jit(solution)/shard_map/psum | solution.py:142
  488.1 58.9 %all-reduce.8.cloned.1.call-done = (f32[256,256]{1,0:T(8,128)}, f32[256,256]{1,0:T(8,128)}, f32[256,256]{1,0:T(8,128)}, f32[256,256]{1,0:T(8,128)}) async-done(((f32[256,256]{1,0:T(8,128)}, f32[256,256]{1,0:T(8,128)}, f32[256,256]{1,0:T(8,128)}, f32[256,256]{1,0:T(8,128)}), (f32[256,256]{1,0:T(8,128)}, f32[256,256]{1,0:T(8,128)}, f32[256,256]{1,0:T(8,128)}, ...) | async-done | bytes 1048592 | tf_op jit(solution)/shard_map/psum | solution.py:142
  (271 shorter events, 262.7 us)
Async XLA Ops:
  7.2 173.6 %copy-start = (bf16[256,256]{1,0:T(8,128)(2,1)S(1)}, bf16[256,256]{1,0:T(8,128)(2,1)}, u32[]{:S(2)}) copy-start(bf16[256,256]{1,0:T(8,128)(2,1)} %param.20) | copy-start | bytes 393220
  7.2 15.6 %copy-start.4 = (bf16[256,256]{1,0:T(8,128)(2,1)S(1)}, bf16[256,256]{1,0:T(8,128)(2,1)}, u32[]{:S(2)}) copy-start(bf16[256,256]{1,0:T(8,128)(2,1)} %param.15) | copy-start | bytes 393220
  7.2 15.6 %copy-start.16 = (f32[256]{0:T(256)S(1)}, f32[256]{0:T(256)}, u32[]{:S(2)}) copy-start(f32[256]{0:T(256)} %param.16) | copy-start | bytes 3076
  7.2 15.6 %copy-start.9 = (bf16[256,256]{1,0:T(8,128)(2,1)S(1)}, bf16[256,256]{1,0:T(8,128)(2,1)}, u32[]{:S(2)}) copy-start(bf16[256,256]{1,0:T(8,128)(2,1)} %param.17) | copy-start | bytes 393220
  7.2 16.3 %copy-start.20 = (s32[48,128]{1,0:T(8,128)S(1)}, s32[48,128]{1,0:T(8,128)}, u32[]{:S(2)}) copy-start(s32[48,128]{1,0:T(8,128)} %param.22) | copy-start | bytes 73732
  7.2 16.4 %copy-start.21 = (s32[48,128]{1,0:T(8,128)S(1)}, s32[48,128]{1,0:T(8,128)}, u32[]{:S(2)}) copy-start(s32[48,128]{1,0:T(8,128)} %param.23) | copy-start | bytes 73732
  7.2 17.0 %copy-start.22 = (s32[48,128]{1,0:T(8,128)S(1)}, s32[48,128]{1,0:T(8,128)}, u32[]{:S(2)}) copy-start(s32[48,128]{1,0:T(8,128)} %param.24) | copy-start | bytes 73732
  9.3 14.9 %copy-start.14 = (f32[256]{0:T(256)}, f32[256]{0:T(256)S(1)}, u32[]{:S(2)}) copy-start(f32[256]{0:T(256)S(1)} %broadcast_multiply_fusion) | copy-start | bytes 3076
  11.0 13.2 %copy-start.18 = (f32[256]{0:T(256)}, f32[256]{0:T(256)S(1)}, u32[]{:S(2)}) copy-start(f32[256]{0:T(256)S(1)} %fusion.80) | copy-start | bytes 3076
  11.8 11.2 %copy-start.25 = (s32[64]{0:T(128)}, s32[64]{0:T(128)S(1)}, u32[]{:S(2)}) copy-start(s32[64]{0:T(128)S(1)} %fusion.81) | copy-start | bytes 772
  12.8 12.5 %copy-start.6 = (bf16[256,512]{1,0:T(8,128)(2,1)}, bf16[256,512]{1,0:T(8,128)(2,1)S(1)}, u32[]{:S(2)}) copy-start(bf16[256,512]{1,0:T(8,128)(2,1)S(1)} %constant_dynamic-update-slice_fusion) | copy-start | bytes 786436
  15.4 13.4 %all-to-all-start = ((bf16[16,4,512]{2,1,0:T(4,128)(2,1)}), bf16[16,4,512]{2,1,0:T(4,128)(2,1)S(1)}, u32[]{:S(2)}, u32[]{:S(2)}) async-start(bf16[16,4,512]{2,1,0:T(4,128)(2,1)} %reshape.287), calls=%async_computation | async-start | bytes 131072 | tf_op jit(solution)/shard_map/all_to_all | solution.py:61
  28.9 152.8 %copy-start.11 = (bf16[256,256]{1,0:T(8,128)(2,1)S(1)}, bf16[256,256]{1,0:T(8,128)(2,1)}, u32[]{:S(2)}) copy-start(bf16[256,256]{1,0:T(8,128)(2,1)} %param.21) | copy-start | bytes 393220
  202.6 3.5 copy-start.1
  202.6 4.6 copy-start.2
  244.6 3.5 copy-start.1
  244.6 4.6 copy-start.2
  286.6 3.5 copy-start.1
  286.6 4.6 copy-start.2
  328.7 3.5 copy-start.1
  328.7 4.6 copy-start.2
  370.7 3.5 copy-start.1
  370.7 4.6 copy-start.2
  412.8 4.6 copy-start.2
  438.0 8.9 %copy-start.15 = (f32[256]{0:T(256)S(1)}, f32[256]{0:T(256)}, u32[]{:S(2)}) copy-start(f32[256]{0:T(256)} %copy-done.14) | copy-start | bytes 3076
  438.0 8.9 %copy-start.17 = (f32[256]{0:T(256)S(1)}, f32[256]{0:T(256)}, u32[]{:S(2)}) copy-start(f32[256]{0:T(256)} %param.16) | copy-start | bytes 3076
  438.0 8.9 %copy-start.19 = (f32[256]{0:T(256)S(1)}, f32[256]{0:T(256)}, u32[]{:S(2)}) copy-start(f32[256]{0:T(256)} %copy-done.18) | copy-start | bytes 3076
  438.0 10.0 %copy-start.10 = (bf16[256,256]{1,0:T(8,128)(2,1)S(1)}, bf16[256,256]{1,0:T(8,128)(2,1)}, u32[]{:S(2)}) copy-start(bf16[256,256]{1,0:T(8,128)(2,1)} %param.17) | copy-start | bytes 393220
  438.0 15.0 %copy-start.26 = (s32[64]{0:T(128)S(1)}, s32[64]{0:T(128)}, u32[]{:S(2)}) copy-start(s32[64]{0:T(128)} %copy-done.25) | copy-start | bytes 772
  442.6 10.4 %all-to-all-start.1 = ((bf16[16,4,512]{2,1,0:T(4,128)(2,1)}), bf16[16,4,512]{2,1,0:T(4,128)(2,1)S(1)}, u32[]{:S(2)}, u32[]{:S(2)}) async-start(bf16[16,4,512]{2,1,0:T(4,128)(2,1)} %convert_element_type.85), calls=%async_computation.1 | async-start | bytes 131072 | tf_op jit(solution)/shard_map/all_to_all | solution.py:127
  446.9 100.1 %all-reduce.8.cloned.1.call-start = ((), (), s32[]{:S(2)}) async-start(), calls=%async_computation.2 | async-start | bytes 2097152 | tf_op jit(solution)/shard_map/psum | solution.py:142
  448.0 6.8 %copy-start.7 = (bf16[256,512]{1,0:T(8,128)(2,1)S(1)}, bf16[256,512]{1,0:T(8,128)(2,1)}, u32[]{:S(2)}) copy-start(bf16[256,512]{1,0:T(8,128)(2,1)} %copy-done.6) | copy-start | bytes 786436
  (13 other events, 30.0 us)
Sparse Core Ops, SparseCore 0:
  456.3 90.5 all-reduce.7
where the time goes:
time: 564 us; the launch traced here: 560 us
  other arithmetic  185 us (33%)
  local copies, waits for them, and re-layouts  169 us (30%)
  matrix products  81.7 us (14%)
  waiting for transfers between devices  67.2 us (12%)
  blocking collectives  30.7 us (5%)
  between operations  14.5 us (3%)
  starting transfers between devices  11.6 us (2%)
    psum x1, waiting for transfers between devices, on_device(): lax.psum((gain_term, grad_query, grad_key, grad_value, grad_out), 'nodes')  58.9 us
    gather x12, local copies, waits for them, and re-layouts, backward_step(): _, pull_edges = jax.vjp(edge_terms, query32[targets], table32[sources])  57.4 us
    scatter-add x6, other arithmetic, backward_step(): dpair_acc.at[sources].add(dpair_rows)  55.4 us
    dot_general x20, matrix products, block_terms(): jnp.dot(query_rows * key_rows, head_map, precision=highest)  46.7 us
    scatter-add x6, other arithmetic, backward_step(): dq_acc.at[targets].add(dq_rows)  41.5 us
    gather x18, local copies, waits for them, and re-layouts, backward_step(): dq_rows, dpair_rows = pull_edges((d_num[targets], d_den[targets]))  38.6 us
    scatter-add x6, other arithmetic, forward_step(): numerator.at[targets].add(num_part)  37 us
    scatter-add x6, other arithmetic, forward_step(): denominator.at[targets].add(den_part)  36.6 us
  transfers between devices with their start and end apart: 3, of which 3 were waited for; matrix products, arithmetic and copies ran while one was open for 1% of the time, Pallas kernels for 0%

commit v1 on v0

v1 whole, which is shorter than its diff:
```python
import functools
import math

import jax
import jax.numpy as jnp
from jax import lax
from jax.experimental import pallas as pl
from jax.experimental.pallas import tpu as pltpu
from jax.sharding import PartitionSpec as P

HEADS = 8
EPS = 1e-05
F32 = jnp.float32
BF16 = jnp.bfloat16
VMEM = pl.BlockSpec(memory_space=pltpu.VMEM)
SMEM = pl.BlockSpec(memory_space=pltpu.SMEM)
LIMIT = 40 * 1024 * 1024


def up(n, m):
    return -(-n // m) * m


def dot(a, b):
    return jnp.dot(a, b, preferred_element_type=F32)


def dot_t(a, b):
    return lax.dot_general(a, b, (((1,), (1,)), ((), ())), preferred_element_type=F32)


def standardize(x):
    centered = x - jnp.mean(x, axis=1, keepdims=True)
    rstd = lax.rsqrt(jnp.mean(centered * centered, axis=1, keepdims=True) + EPS)
    return centered * rstd, rstd


def pick_kernel(send_ref, feats_ref, out_ref, wide, picked):
    peers, slots = send_ref.shape
    wide[...] = feats_ref[...].astype(F32)

    def one_peer(peer, carry):
        for slot in range(slots):
            picked[pl.ds(peer * slots + slot, 1), :] = wide[pl.ds(send_ref[peer, slot], 1), :]
        return carry

    lax.fori_loop(0, peers, one_peer, 0)
    out_ref[...] = picked[...].astype(BF16)


def local_kernel(
    x_ref, gain_ref, wq_ref, wk_ref, wv_ref, wo_ref, cot_ref, dst_ref, src_ref, mask_ref,
    q_ref, k_ref, v_ref, qt_ref, normt_ref, datt_ref, count_ref,
):
    rows = x_ref.shape[0]
    width = count_ref.shape[1]
    xhat, _ = standardize(x_ref[...].astype(F32))
    normed = (xhat * gain_ref[...]).astype(BF16)
    q = dot(normed, wq_ref[...]).astype(BF16)
    q_ref[...] = q
    qt_ref[...] = q.T
    normt_ref[...] = normed.T
    k_ref[...] = dot(normed, wk_ref[...]).astype(BF16)
    v_ref[...] = dot(normed, wv_ref[...]).astype(BF16)
    datt_ref[...] = dot_t(cot_ref[...], wo_ref[...]).astype(BF16)
    row_id = lax.broadcasted_iota(jnp.int32, (rows, width), 0)
    col_id = lax.broadcasted_iota(jnp.int32, (rows, width), 1)
    count_ref[...] = (row_id == col_id).astype(F32)
    group = 8
    edge = 128
    dst_id = lax.broadcasted_iota(jnp.int32, (rows, edge), 0)
    src_id = lax.broadcasted_iota(jnp.int32, (width, edge), 0)

    def step(i, carry):
        base = pl.multiple_of(i * group, group)
        dst = dst_ref[pl.ds(base, group), :]
        src = jnp.where(mask_ref[pl.ds(base, group), :] > 0, src_ref[pl.ds(base, group), :], -1)
        hot_dst = jnp.concatenate(
            [(dst_id == dst[j : j + 1]).astype(F32).astype(BF16) for j in range(group)], axis=1
        )
        hot_src = jnp.concatenate(
            [(src_id == src[j : j + 1]).astype(F32).astype(BF16) for j in range(group)], axis=1
        )
        count_ref[...] += dot_t(hot_dst, hot_src)
        return carry

    lax.fori_loop(0, dst_ref.shape[0] // group, step, 0)


def attend_kernel(
    x_ref, far_ref, gain_ref, wq_ref, wk_ref, wv_ref, wo_ref, cot_ref,
    q_ref, k_ref, v_ref, qt_ref, normt_ref, datt_ref, count_ref,
    out_ref, gf_ref, pay_ref, w_scr, g_scr, dkt_scr, dvt_scr,
):
    rows, feats = x_ref.shape
    far = far_ref.shape[0]
    width = count_ref.shape[1]
    head = feats // HEADS
    peers, block, _ = pay_ref.shape
    slots = far // peers
    pad = width - rows - far
    far_x = far_ref[...].astype(F32)
    if pad:
        far_x = jnp.concatenate([far_x, jnp.zeros((pad, feats), F32)], axis=0)
    x = x_ref[...].astype(F32)
    gain = gain_ref[...]
    far_hat, far_rstd = standardize(far_x)
    far_normed = (far_hat * gain).astype(BF16)
    keys = jnp.concatenate([k_ref[...], dot(far_normed, wk_ref[...]).astype(BF16)], axis=0)
    values = jnp.concatenate([v_ref[...], dot(far_normed, wv_ref[...]).astype(BF16)], axis=0)
    lane = lax.broadcasted_iota(jnp.int32, (1, feats), 1)
    masks = [(lane >= h * head) & (lane < (h + 1) * head) for h in range(HEADS)]
    hots = [m.astype(F32).astype(BF16) for m in masks]
    queries = q_ref[...]
    count = count_ref[...]
    num = jnp.zeros((rows, feats), F32)
    den = jnp.zeros((rows, feats), F32)
    for h in range(HEADS):
        score = dot_t(queries * hots[h], keys)
        t = jnp.tanh(score * (0.2 / math.sqrt(head)))
        w = count * jnp.exp(5.0 * t)
        wb = w.astype(BF16)
        w_scr[h] = wb
        g_scr[h] = w * (1.0 - t * t) * (1.0 / math.sqrt(head))
        num = num + dot(wb, values * hots[h])
        den = den + dot(wb, jnp.broadcast_to(hots[h], (width, feats)))
    rden = 1.0 / den
    att32 = num * rden
    att = att32.astype(BF16)
    out_ref[...] = (x + dot(att, wo_ref[...])).astype(BF16)
    grad_out = dot(att.T, cot_ref[...])
    dnum = (datt_ref[...].astype(F32) * rden).astype(BF16)
    dnum_t = dnum.T
    prod = dnum.astype(F32) * att32
    qt = qt_ref[...]
    dq = jnp.zeros((rows, feats), F32)
    for h in range(HEADS):
        z = jnp.sum(jnp.where(masks[h], prod, 0.0), axis=1, keepdims=True)
        ds = (g_scr[h] * (dot_t(dnum * hots[h], values) - z)).astype(BF16)
        dq = dq + dot(ds, keys * hots[h])
        at = slice(h * head, (h + 1) * head)
        dkt_scr[at, :] = dot(qt[at, :], ds)
        dvt_scr[at, :] = dot(dnum_t[at, :], w_scr[h])
    dq = dq.astype(BF16)
    dkt = dkt_scr[...].astype(BF16)
    dvt = dvt_scr[...].astype(BF16)
    norm_t = jnp.concatenate([normt_ref[...], far_normed.T], axis=1)
    grad_query = dot(normt_ref[...], dq)
    grad_key = dot_t(norm_t, dkt)
    grad_value = dot_t(norm_t, dvt)
    d_normed = (dot(wk_ref[...], dkt) + dot(wv_ref[...], dvt)).T
    near = d_normed[:rows] + dot_t(dq, wq_ref[...])
    away = d_normed[rows:]
    hat, rstd = standardize(x)

    def pull(d, xhat, scale):
        g = d * gain
        mean_g = jnp.mean(g, axis=1, keepdims=True)
        mean_gx = jnp.mean(g * xhat, axis=1, keepdims=True)
        return scale * (g - mean_g - xhat * mean_gx)

    gf_ref[...] = cot_ref[...].astype(F32) + pull(near, hat, rstd)
    away_dx = pull(away, far_hat, far_rstd)
    gain_sum = jnp.sum(near * hat, axis=0, keepdims=True) + jnp.sum(
        away * far_hat, axis=0, keepdims=True
    )
    grads = jnp.concatenate([grad_query, grad_key, grad_value, grad_out], axis=0)
    share = grads.shape[0] // peers
    blank = jnp.zeros((block - share - slots - 1, feats), F32)
    for p in range(peers):
        pay_ref[p] = jnp.concatenate(
            [
                grads[p * share : (p + 1) * share],
                away_dx[p * slots : (p + 1) * slots],
                gain_sum,
                blank,
            ],
            axis=0,
        ).astype(BF16)


def reduce_kernel(got_ref, share_ref):
    peers, share, _ = share_ref.shape
    total = jnp.zeros(share_ref.shape[1:], F32)
    for p in range(peers):
        total = total + got_ref[p].astype(F32)[:share]
    share_ref[...] = jnp.broadcast_to(total.astype(BF16)[None], share_ref.shape)


def finish_kernel(share, send_ref, gf_ref, got_ref, feats_ref, gain_ref):
    peers, slots = send_ref.shape
    feats_ref[...] = gf_ref[...]
    gain = jnp.zeros(gain_ref.shape, F32)
    for p in range(peers):
        got = got_ref[p].astype(F32)
        gain = gain + got[share + slots : share + slots + 1]
        for slot in range(slots):
            at = pl.ds(send_ref[p, slot], 1)
            feats_ref[at, :] += got[share + slot : share + slot + 1]
    gain_ref[...] = gain


def spread_kernel(got_ref, *out_refs):
    rows = out_refs[0].shape[0]
    peers, share, feats = got_ref.shape
    whole = got_ref[...].astype(F32).reshape(peers * share, feats)
    for i, out_ref in enumerate(out_refs):
        out_ref[...] = whole[i * rows : (i + 1) * rows]


def call(kernel, out_shape, n_in, scratch=(), smem=(), cost=None):
    return pl.pallas_call(
        kernel,
        out_shape=out_shape,
        in_specs=[SMEM if i in smem else VMEM for i in range(n_in)],
        out_specs=jax.tree.map(lambda _: VMEM, out_shape),
        scratch_shapes=list(scratch),
        compiler_params=pltpu.CompilerParams(vmem_limit_bytes=LIMIT),
        cost_estimate=cost,
    )


def on_device(
    node_feats, norm_gain, w_query, w_key, w_value, w_out, cotangent,
    edge_dst, edge_src, edge_mask, send_rows,
):
    rows, feats = node_feats.shape
    peers, slots = send_rows.shape[1:]
    far = peers * slots
    width = rows + up(far, 128)
    share = 4 * feats // peers
    block = up(share + slots + 1, 16)
    gain = norm_gain.reshape(1, feats)
    send = send_rows[0]

    def like(shape, dtype):
        return jax.ShapeDtypeStruct(shape, dtype)

    picked = call(
        pick_kernel,
        like((far, feats), BF16),
        2,
        (pltpu.VMEM((rows, feats), F32), pltpu.VMEM((far, feats), F32)),
        smem=(0,),
    )(send, node_feats)
    arrived = lax.all_to_all(
        picked.reshape(peers, slots, feats), "nodes", split_axis=0, concat_axis=0, tiled=True
    ).reshape(far, feats)
    square = like((rows, feats), BF16)
    cost = pl.CostEstimate(flops=2_000_000_000, bytes_accessed=2_000_000, transcendentals=0)
    near = call(
        local_kernel,
        (square, square, square, like((feats, rows), BF16), like((feats, rows), BF16), square,
         like((rows, width), F32)),
        10,
        cost=cost,
    )(node_feats, gain, w_query, w_key, w_value, w_out, cotangent, edge_dst, edge_src, edge_mask)
    output, gf, payload = call(
        attend_kernel,
        (square, like((rows, feats), F32), like((peers, block, feats), BF16)),
        15,
        (
            pltpu.VMEM((HEADS, rows, width), BF16),
            pltpu.VMEM((HEADS, rows, width), F32),
            pltpu.VMEM((feats, width), F32),
            pltpu.VMEM((feats, width), F32),
        ),
    )(node_feats, arrived, gain, w_query, w_key, w_value, w_out, cotangent, *near)
    got = lax.all_to_all(payload, "nodes", split_axis=0, concat_axis=0, tiled=True)
    shares = call(reduce_kernel, like((peers, share, feats), BF16), 1)(got)
    whole = lax.all_to_all(shares, "nodes", split_axis=0, concat_axis=0, tiled=True)
    grad_feats, grad_gain = call(
        functools.partial(finish_kernel, share),
        (like((rows, feats), F32), like((1, feats), F32)),
        3,
        smem=(0,),
    )(send, gf, got)
    grads = call(spread_kernel, (like((feats, feats), F32),) * 4, 1)(whole)
    return (output, grad_feats, grad_gain.reshape(feats), *grads)


def solution(mesh):
    nodes = P(("groups", "nodes"), None)
    in_specs = (
        nodes, P(), P(), P(), P(), P(), nodes, nodes, nodes, nodes,
        P(("groups", "nodes"), None, None),
    )
    out_specs = (nodes, nodes, P("groups")) + (P("groups", None),) * 4
    return jax.shard_map(
        on_device, mesh=mesh, in_specs=in_specs, out_specs=out_specs, check_vma=False
    )
```

time: 564 us -> 71.9 us (0.13)
  other arithmetic: 185 us -> 0 us
  local copies, waits for them, and re-layouts: 169 us -> 8.07 us
  matrix products: 81.7 us -> 0 us
  waiting for transfers between devices: 67.2 us -> 12.5 us
  Pallas kernels: 0 us -> 14.5 us
  between operations: 14.5 us -> 0.74 us
  blocking collectives: 30.7 us -> 23.9 us
    scatter-add x25 -> x0, other arithmetic: 172 us -> none  [the longest x6 55.4 us: backward_step(): dpair_acc.at[sources].add(dpair_rows)]
    gather x43 -> x0, local copies, waits for them, and re-layouts: 147 us -> none  [the longest x12 57.4 us: backward_step(): _, pull_edges = jax.vjp(edge_terms, query32[targets], table32[sources])]
    dot_general x51 -> x0, matrix products: 81.7 us -> none  [the longest x20 46.7 us: block_terms(): jnp.dot(query_rows * key_rows, head_map, precision=highest)]
    psum x1 -> x0, waiting for transfers between devices: 58.9 us -> none  [on_device(): lax.psum((gain_term, grad_query, grad_key, grad_value, grad_out), 'nodes')]
    psum x1 -> x0, blocking collectives: 30.7 us -> none  [on_device(): lax.psum((gain_term, grad_query, grad_key, grad_value, grad_out), 'nodes')]
    all_to_all x0 -> x1, blocking collectives: none -> 23.9 us  [on_device(): lax.all_to_all(payload, 'nodes', split_axis=0, concat_axis=0, tiled=True)]
    pallas_call x0 -> x6, Pallas kernels: none -> 14.5 us  [the longest x1 6.68 us: on_device(): call(attend_kernel, (square, like((rows, feats), F32), like((peers, block...]
    select_n x14 -> x0, other arithmetic: 9.44 us -> none  [the longest x6 4.73 us: backward_step(): _, pull_edges = jax.vjp(edge_terms, query32[targets], table32[sources])]
  transfers between devices with their start and end apart: 3 -> 2, of which waited for: 3 -> 1; matrix products, arithmetic and copies ran while one was open for 1% -> 0% of each run, Pallas kernels for 0% -> 7%
where the time goes in v1:
time: 71.9 us; the launch traced here: 70.9 us
  blocking collectives  23.9 us (33%)
  Pallas kernels  14.5 us (20%)
  waiting for transfers between devices  12.5 us (17%)
  starting transfers between devices  11 us (15%)
  local copies, waits for them, and re-layouts  8.07 us (11%)
  between operations  0.74 us (1%)
    all_to_all x1, blocking collectives, on_device(): lax.all_to_all(payload, 'nodes', split_axis=0, concat_axis=0, tiled=True)  23.9 us
    all_to_all x1, waiting for transfers between devices, on_device(): lax.all_to_all(shares, 'nodes', split_axis=0, concat_axis=0, tiled=True)  12.5 us
    all_to_all x1, starting transfers between devices, on_device(): lax.all_to_all(picked.reshape(peers, slots, feats), 'nodes', split_axis=0...  7.48 us
    pallas_call x1, Pallas kernels, on_device(): call(attend_kernel, (square, like((rows, feats), F32), like((peers, block...  6.68 us
    unnamed x30, local copies, waits for them, and re-layouts  6.66 us
    all_to_all x1, starting transfers between devices, on_device(): lax.all_to_all(shares, 'nodes', split_axis=0, concat_axis=0, tiled=True)  3.55 us
    pallas_call x1, Pallas kernels, on_device(): call(local_kernel, (square, square, square, like((feats, rows), BF16), li...  3.36 us
    pallas_call x1, Pallas kernels, on_device(): call(functools.partial(finish_kernel, share), (like((rows, feats), F32),...  1.61 us
  transfers between devices with their start and end apart: 2, of which 1 were waited for; matrix products, arithmetic and copies ran while one was open for 0% of the time, Pallas kernels for 7%

profile of v1, /device:TPU:1, one launch (start us, length us, event | category | flops | bytes accessed | tf_op | source)
XLA Modules:
  0.0 70.9 jit_solution(6851661514856161654)
XLA Ops:
  0.6 0.8 %copy.18.send_ref = s32[16,4]{1,0:T(8,128)S(1)} copy(s32[16,4]{0,1:T(4,128)} %bitcast.5) | data formatting | bytes 512 | tf_op jit(solution)/shard_map/squeeze | solution.py:234
  1.4 0.0 copy-start
  1.4 0.9 %copy-done = bf16[256,256]{1,0:T(8,128)(2,1)S(1)} copy-done((bf16[256,256]{1,0:T(8,128)(2,1)S(1)}, bf16[256,256]{1,0:T(8,128)(2,1)}, u32[]{:S(2)}) %copy-start) | copy-done | bytes 131096
  2.3 0.0 copy-start.1
  2.3 0.0 copy-start.2
  2.3 1.0 %shard_map.162 = bf16[64,256]{1,0:T(8,128)(2,1)S(1)} custom-call(s32[16,4]{1,0:T(8,128)S(1)} %copy.18.send_ref, bf16[256,256]{1,0:T(8,128)(2,1)S(1)} %copy-done), custom_call_target="tpu_custom_call" | custom-call | tf_op jit(solution)/shard_map/pallas_call | solution.py:239
  3.3 0.6 reshape.26
  3.9 0.0 copy-start.12
  3.9 7.5 %all-to-all-start = ((bf16[16,4,256]{2,1,0:T(4,128)(2,1)}), bf16[16,4,256]{2,1,0:T(4,128)(2,1)S(1)}, u32[]{:S(2)}, u32[]{:S(2)}) async-start(bf16[16,4,256]{2,1,0:T(4,128)(2,1)} %reshape.26), calls=%async_computation | async-start | bytes 65536 | tf_op jit(solution)/shard_map/all_to_all | solution.py:246
  11.4 0.0 copy-done.1
  11.4 0.0 copy-done.2
  11.4 0.0 copy-done.12
  11.4 0.6 copy-done.11
  12.1 0.9 %copy-done.3 = bf16[256,256]{1,0:T(8,128)(2,1)S(1)} copy-done((bf16[256,256]{1,0:T(8,128)(2,1)S(1)}, bf16[256,256]{1,0:T(8,128)(2,1)}, u32[]{:S(2)}) %copy-start.3) | copy-done | bytes 131096
  13.0 0.9 %copy-done.5 = bf16[256,256]{1,0:T(8,128)(2,1)S(1)} copy-done((bf16[256,256]{1,0:T(8,128)(2,1)S(1)}, bf16[256,256]{1,0:T(8,128)(2,1)}, u32[]{:S(2)}) %copy-start.5) | copy-done | bytes 131096
  13.9 0.9 %copy-done.7 = bf16[256,256]{1,0:T(8,128)(2,1)S(1)} copy-done((bf16[256,256]{1,0:T(8,128)(2,1)S(1)}, bf16[256,256]{1,0:T(8,128)(2,1)}, u32[]{:S(2)}) %copy-start.7) | copy-done | bytes 131096
  14.8 0.9 %copy-done.9 = bf16[256,256]{1,0:T(8,128)(2,1)S(1)} copy-done((bf16[256,256]{1,0:T(8,128)(2,1)S(1)}, bf16[256,256]{1,0:T(8,128)(2,1)}, u32[]{:S(2)}) %copy-start.9) | copy-done | bytes 131096
  15.7 0.7 %copy-done.13 = s32[48,128]{1,0:T(8,128)S(1)} copy-done((s32[48,128]{1,0:T(8,128)S(1)}, s32[48,128]{1,0:T(8,128)}, u32[]{:S(2)}) %copy-start.13) | copy-done | bytes 24600
  16.4 0.7 %copy-done.14 = s32[48,128]{1,0:T(8,128)S(1)} copy-done((s32[48,128]{1,0:T(8,128)S(1)}, s32[48,128]{1,0:T(8,128)}, u32[]{:S(2)}) %copy-start.14) | copy-done | bytes 24600
  17.2 3.4 %shard_map.163 = (bf16[256,256]{1,0:T(8,128)(2,1)S(1)}, bf16[256,256]{1,0:T(8,128)(2,1)S(1)}, bf16[256,256]{1,0:T(8,128)(2,1)S(1)}, bf16[256,256]{1,0:T(8,128)(2...) custom-call(bf16[256,256]{1,0:T(8,128)(2,1)S(1)} %copy-done.1, ...), custom_call_target="tpu_custom_call" | custom-call | flops 2000000000 | bytes 2000000 | tf_op jit(solution)/shard_map/pallas_call | solution.py:251
  20.6 0.0 all-to-all-done
  20.6 0.0 copy-done.4
  20.6 0.0 copy-done.6
  20.6 0.0 copy-done.8
  20.6 0.0 copy-done.10
  20.6 6.7 %shard_map.164 = (bf16[256,256]{1,0:T(8,128)(2,1)}, f32[256,256]{1,0:T(8,128)S(1)}, bf16[16,80,256]{2,1,0:T(8,128)(2,1)S(1)}) custom-call(bf16[256,256]{1,0:T(8,128)(2,1)S(1)} %copy-done.1, bf16[64,256]{1,0:T(8,128)(2,1)S(1)} %reshape.27.far_ref, f32[1,256]{1,0:T(1,128)S(1)} %bitcast.4, bf16[256,256]{1,0:T(8,128)(2,1)S(1)} %copy-done.2, ...), custom_call_target="tpu_custom_call" | custom-call | tf_op jit(solution)/shard_map/pallas_call | solution.py:258
  27.3 23.9 %all_to_all.15.got_ref = bf16[16,80,256]{2,1,0:T(8,128)(2,1)S(1)} all-to-all(bf16[16,80,256]{2,1,0:T(8,128)(2,1)S(1)} %get-tuple-element.32), channel_id=1, replica_groups=mesh['groups'=2,'nodes'=16] {'nodes'}, dimensions={0} | all-to-all | bytes 1310720 | tf_op jit(solution)/shard_map/all_to_all | solution.py:269
  51.2 0.9 %shard_map.166 = bf16[16,64,256]{2,1,0:T(8,128)(2,1)} custom-call(bf16[16,80,256]{2,1,0:T(8,128)(2,1)S(1)} %all_to_all.15.got_ref), custom_call_target="tpu_custom_call" | custom-call | tf_op jit(solution)/shard_map/pallas_call | solution.py:270
  52.1 3.6 %all-to-all-start.2 = ((bf16[16,64,256]{2,1,0:T(8,128)(2,1)}), bf16[16,64,256]{2,1,0:T(8,128)(2,1)S(1)}, u32[]{:S(2)}, u32[]{:S(2)}) async-start(bf16[16,64,256]{2,1,0:T(8,128)(2,1)} %shard_map.166), calls=%async_computation.2 | async-start | bytes 1048576 | tf_op jit(solution)/shard_map/all_to_all | solution.py:271
  55.7 1.6 %shard_map.165 = (f32[256,256]{1,0:T(8,128)}, f32[1,256]{1,0:T(1,128)}) custom-call(s32[16,4]{1,0:T(8,128)S(1)} %copy.18.send_ref, f32[256,256]{1,0:T(8,128)S(1)} %get-tuple-element.31.gf_ref, bf16[16,80,256]{2,1,0:T(8,128)(2,1)S(1)} %all_to_all.15.got_ref), custom_call_target="tpu_custom_call" | custom-call | tf_op jit(solution)/shard_map/pallas_call | solution.py:272
  57.3 12.5 %all-to-all-done.2.got_ref = bf16[16,64,256]{2,1,0:T(8,128)(2,1)S(1)} async-done(((bf16[16,64,256]{2,1,0:T(8,128)(2,1)}), bf16[16,64,256]{2,1,0:T(8,128)(2,1)S(1)}, u32[]{:S(2)}, u32[]{:S(2)}) %all-to-all-start.2) | async-done | bytes 524320 | tf_op jit(solution)/shard_map/all_to_all | solution.py:271
  69.9 1.0 %shard_map.167 = (f32[256,256]{1,0:T(8,128)}, f32[256,256]{1,0:T(8,128)}, f32[256,256]{1,0:T(8,128)}, f32[256,256]{1,0:T(8,128)}) custom-call(bf16[16,64,256]{2,1,0:T(8,128)(2,1)S(1)} %all-to-all-done.2.got_ref), custom_call_target="tpu_custom_call" | custom-call | tf_op jit(solution)/shard_map/pallas_call | solution.py:278
  (12 shorter events, 0.0 us)
Async XLA Ops:
  1.4 0.9 %copy-start = (bf16[256,256]{1,0:T(8,128)(2,1)S(1)}, bf16[256,256]{1,0:T(8,128)(2,1)}, u32[]{:S(2)}) copy-start(bf16[256,256]{1,0:T(8,128)(2,1)} %x_ref.3) | copy-start | bytes 393220
  2.3 9.1 %copy-start.1 = (bf16[256,256]{1,0:T(8,128)(2,1)S(1)}, bf16[256,256]{1,0:T(8,128)(2,1)}, u32[]{:S(2)}) copy-start(bf16[256,256]{1,0:T(8,128)(2,1)} %x_ref.3) | copy-start | bytes 393220
  2.3 9.1 %copy-start.2 = (bf16[256,256]{1,0:T(8,128)(2,1)S(1)}, bf16[256,256]{1,0:T(8,128)(2,1)}, u32[]{:S(2)}) copy-start(bf16[256,256]{1,0:T(8,128)(2,1)} %wq_ref.3) | copy-start | bytes 393220
  3.9 7.5 %copy-start.12 = (s32[48,128]{1,0:T(8,128)S(1)}, s32[48,128]{1,0:T(8,128)}, u32[]{:S(2)}) copy-start(s32[48,128]{1,0:T(8,128)} %dst_ref.1) | copy-start | bytes 73732
  3.9 16.6 %all-to-all-start = ((bf16[16,4,256]{2,1,0:T(4,128)(2,1)}), bf16[16,4,256]{2,1,0:T(4,128)(2,1)S(1)}, u32[]{:S(2)}, u32[]{:S(2)}) async-start(bf16[16,4,256]{2,1,0:T(4,128)(2,1)} %reshape.26), calls=%async_computation | async-start | bytes 65536 | tf_op jit(solution)/shard_map/all_to_all | solution.py:246
  11.4 0.7 copy-start.11
  12.1 0.9 %copy-start.3 = (bf16[256,256]{1,0:T(8,128)(2,1)S(1)}, bf16[256,256]{1,0:T(8,128)(2,1)}, u32[]{:S(2)}) copy-start(bf16[256,256]{1,0:T(8,128)(2,1)} %wk_ref.3) | copy-start | bytes 393220
  13.0 0.9 %copy-start.5 = (bf16[256,256]{1,0:T(8,128)(2,1)S(1)}, bf16[256,256]{1,0:T(8,128)(2,1)}, u32[]{:S(2)}) copy-start(bf16[256,256]{1,0:T(8,128)(2,1)} %wv_ref.3) | copy-start | bytes 393220
  13.9 0.9 %copy-start.7 = (bf16[256,256]{1,0:T(8,128)(2,1)S(1)}, bf16[256,256]{1,0:T(8,128)(2,1)}, u32[]{:S(2)}) copy-start(bf16[256,256]{1,0:T(8,128)(2,1)} %wo_ref.3) | copy-start | bytes 393220
  14.8 0.9 %copy-start.9 = (bf16[256,256]{1,0:T(8,128)(2,1)S(1)}, bf16[256,256]{1,0:T(8,128)(2,1)}, u32[]{:S(2)}) copy-start(bf16[256,256]{1,0:T(8,128)(2,1)} %cot_ref.3) | copy-start | bytes 393220
  15.7 0.7 %copy-start.13 = (s32[48,128]{1,0:T(8,128)S(1)}, s32[48,128]{1,0:T(8,128)}, u32[]{:S(2)}) copy-start(s32[48,128]{1,0:T(8,128)} %src_ref.1) | copy-start | bytes 73732
  16.4 0.7 %copy-start.14 = (s32[48,128]{1,0:T(8,128)S(1)}, s32[48,128]{1,0:T(8,128)}, u32[]{:S(2)}) copy-start(s32[48,128]{1,0:T(8,128)} %mask_ref.1) | copy-start | bytes 73732
  17.2 3.4 %copy-start.4 = (bf16[256,256]{1,0:T(8,128)(2,1)S(1)}, bf16[256,256]{1,0:T(8,128)(2,1)}, u32[]{:S(2)}) copy-start(bf16[256,256]{1,0:T(8,128)(2,1)} %wk_ref.3) | copy-start | bytes 393220
  17.2 3.4 %copy-start.6 = (bf16[256,256]{1,0:T(8,128)(2,1)S(1)}, bf16[256,256]{1,0:T(8,128)(2,1)}, u32[]{:S(2)}) copy-start(bf16[256,256]{1,0:T(8,128)(2,1)} %wv_ref.3) | copy-start | bytes 393220
  17.2 3.4 %copy-start.8 = (bf16[256,256]{1,0:T(8,128)(2,1)S(1)}, bf16[256,256]{1,0:T(8,128)(2,1)}, u32[]{:S(2)}) copy-start(bf16[256,256]{1,0:T(8,128)(2,1)} %wo_ref.3) | copy-start | bytes 393220
  17.2 3.4 %copy-start.10 = (bf16[256,256]{1,0:T(8,128)(2,1)S(1)}, bf16[256,256]{1,0:T(8,128)(2,1)}, u32[]{:S(2)}) copy-start(bf16[256,256]{1,0:T(8,128)(2,1)} %cot_ref.3) | copy-start | bytes 393220
  52.1 17.7 %all-to-all-start.2 = ((bf16[16,64,256]{2,1,0:T(8,128)(2,1)}), bf16[16,64,256]{2,1,0:T(8,128)(2,1)S(1)}, u32[]{:S(2)}, u32[]{:S(2)}) async-start(bf16[16,64,256]{2,1,0:T(8,128)(2,1)} %shard_map.166), calls=%async_computation.2 | async-start | bytes 1048576 | tf_op jit(solution)/shard_map/all_to_all | solution.py:271

commit v2 on v1

--- a/solution.py
+++ b/solution.py
@@ -14,6 +14,7 @@
 BF16 = jnp.bfloat16
 VMEM = pl.BlockSpec(memory_space=pltpu.VMEM)
 SMEM = pl.BlockSpec(memory_space=pltpu.SMEM)
+ANY = pl.BlockSpec(memory_space=pl.ANY)
 LIMIT = 40 * 1024 * 1024
 
 
@@ -35,20 +36,32 @@
     return centered * rstd, rstd
 
 
-def pick_kernel(send_ref, feats_ref, out_ref, wide, picked):
-    peers, slots = send_ref.shape
-    wide[...] = feats_ref[...].astype(F32)
-
-    def one_peer(peer, carry):
-        for slot in range(slots):
-            picked[pl.ds(peer * slots + slot, 1), :] = wide[pl.ds(send_ref[peer, slot], 1), :]
-        return carry
-
-    lax.fori_loop(0, peers, one_peer, 0)
-    out_ref[...] = picked[...].astype(BF16)
-
-
-def local_kernel(
+def pick_kernel(send_ref, feats_hbm, out_ref, feats, wide, sem):
+    slots, peers = send_ref.shape
+    copy = pltpu.make_async_copy(feats_hbm, feats, sem)
+    copy.start()
+    copy.wait()
+    wide[...] = feats[...].astype(F32)
+    for peer in range(peers):
+        rows = [wide[pl.ds(send_ref[slot, peer], 1), :] for slot in range(slots)]
+        out_ref[peer] = jnp.concatenate(rows, axis=0).astype(BF16)
+
+
+def local_kernel(*refs):
+    n = 10
+    fetched = refs[n + 7 : n + 7 + n]
+    sems = refs[-1]
+    copies = [
+        pltpu.make_async_copy(refs[i], fetched[i], sems.at[i]) for i in range(n)
+    ]
+    for copy in copies:
+        copy.start()
+    for copy in copies:
+        copy.wait()
+    local_body(*fetched, *refs[n : n + 7])
+
+
+def local_body(
     x_ref, gain_ref, wq_ref, wk_ref, wv_ref, wo_ref, cot_ref, dst_ref, src_ref, mask_ref,
     q_ref, k_ref, v_ref, qt_ref, normt_ref, datt_ref, count_ref,
 ):
@@ -90,16 +103,16 @@
 def attend_kernel(
     x_ref, far_ref, gain_ref, wq_ref, wk_ref, wv_ref, wo_ref, cot_ref,
     q_ref, k_ref, v_ref, qt_ref, normt_ref, datt_ref, count_ref,
-    out_ref, gf_ref, pay_ref, w_scr, g_scr, dkt_scr, dvt_scr,
+    out_ref, gf_ref, keep_ref, give_ref, w_scr, g_scr, dkt_scr, dvt_scr, grad_scr, away_scr,
 ):
     rows, feats = x_ref.shape
-    far = far_ref.shape[0]
+    peers, slots, _ = far_ref.shape
+    far = peers * slots
     width = count_ref.shape[1]
     head = feats // HEADS
-    peers, block, _ = pay_ref.shape
-    slots = far // peers
+    chips, block, _ = keep_ref.shape
     pad = width - rows - far
-    far_x = far_ref[...].astype(F32)
+    far_x = jnp.concatenate([far_ref[p].astype(F32) for p in range(peers)], axis=0)
     if pad:
         far_x = jnp.concatenate([far_x, jnp.zeros((pad, feats), F32)], axis=0)
     x = x_ref[...].astype(F32)
@@ -164,15 +177,44 @@
     gain_sum = jnp.sum(near * hat, axis=0, keepdims=True) + jnp.sum(
         away * far_hat, axis=0, keepdims=True
     )
-    grads = jnp.concatenate([grad_query, grad_key, grad_value, grad_out], axis=0)
-    share = grads.shape[0] // peers
+    grad_scr[...] = jnp.concatenate([grad_query, grad_key, grad_value, grad_out], axis=0)
+    away_scr[...] = away_dx
+    half = grad_scr.shape[0] // 2
+    share = half // chips
     blank = jnp.zeros((block - share - slots - 1, feats), F32)
-    for p in range(peers):
-        pay_ref[p] = jnp.concatenate(
+    core = lax.rem(lax.axis_index("nodes"), 2)
+    for c in range(chips):
+        for own in (True, False):
+            which = core if own else 1 - core
+            start = pl.multiple_of(which * half + c * share, 8)
+            dx = [away_dx[(2 * c + i) * slots : (2 * c + i + 1) * slots] for i in range(2)]
+            part = jnp.concatenate(
+                [
+                    grad_scr[pl.ds(start, share), :],
+                    jnp.where(which == 0, dx[0], dx[1]),
+                    gain_sum,
+                    blank,
+                ],
+                axis=0,
+            )
+            if own:
+                keep_ref[c] = part
+            else:
+                give_ref[c] = part.astype(BF16)
+
+
+def pair_kernel(share, slots, keep_ref, got_ref, out_ref):
+    chips, block, feats = out_ref.shape
+    blank = jnp.zeros((block - share - 2 * slots - 1, feats), F32)
+    for c in range(chips):
+        keep = keep_ref[c]
+        got = got_ref[c].astype(F32)
+        out_ref[c] = jnp.concatenate(
             [
-                grads[p * share : (p + 1) * share],
-                away_dx[p * slots : (p + 1) * slots],
-                gain_sum,
+                keep[:share] + got[:share],
+                keep[share : share + slots],
+                got[share : share + slots],
+                keep[share + slots : share + slots + 1] + got[share + slots : share + slots + 1],
                 blank,
             ],
             axis=0,
@@ -180,39 +222,47 @@
 
 
 def reduce_kernel(got_ref, share_ref):
-    peers, share, _ = share_ref.shape
+    chips, share, _ = share_ref.shape
     total = jnp.zeros(share_ref.shape[1:], F32)
-    for p in range(peers):
-        total = total + got_ref[p].astype(F32)[:share]
+    for c in range(chips):
+        total = total + got_ref[c].astype(F32)[:share]
     share_ref[...] = jnp.broadcast_to(total.astype(BF16)[None], share_ref.shape)
 
 
 def finish_kernel(share, send_ref, gf_ref, got_ref, feats_ref, gain_ref):
-    peers, slots = send_ref.shape
+    slots, peers = send_ref.shape
     feats_ref[...] = gf_ref[...]
     gain = jnp.zeros(gain_ref.shape, F32)
-    for p in range(peers):
-        got = got_ref[p].astype(F32)
-        gain = gain + got[share + slots : share + slots + 1]
-        for slot in range(slots):
-            at = pl.ds(send_ref[p, slot], 1)
-            feats_ref[at, :] += got[share + slot : share + slot + 1]
+    core = lax.rem(lax.axis_index("nodes"), 2)
+    for c in range(peers // 2):
+        got = got_ref[c].astype(F32)
+        gain = gain + got[share + 2 * slots : share + 2 * slots + 1]
+        for i in range(2 * slots):
+            peer = 2 * c + (core if i < slots else 1 - core)
+            at = pl.ds(send_ref[i % slots, peer], 1)
+            feats_ref[at, :] += got[share + i : share + i + 1]
     gain_ref[...] = gain
 
 
-def spread_kernel(got_ref, *out_refs):
+def spread_kernel(mine_ref, other_ref, *out_refs):
     rows = out_refs[0].shape[0]
-    peers, share, feats = got_ref.shape
-    whole = got_ref[...].astype(F32).reshape(peers * share, feats)
-    for i, out_ref in enumerate(out_refs):
-        out_ref[...] = whole[i * rows : (i + 1) * rows]
-
-
-def call(kernel, out_shape, n_in, scratch=(), smem=(), cost=None):
+    chips, share, feats = mine_ref.shape
+    first = lax.rem(lax.axis_index("nodes"), 2) == 0
+    mine = mine_ref[...].astype(F32).reshape(chips * share, feats)
+    other = other_ref[...].astype(F32).reshape(chips * share, feats)
+    low = jnp.where(first, mine, other)
+    high = jnp.where(first, other, mine)
+    out_refs[0][...] = low[:rows]
+    out_refs[1][...] = low[rows:]
+    out_refs[2][...] = high[:rows]
+    out_refs[3][...] = high[rows:]
+
+
+def call(kernel, out_shape, n_in, scratch=(), smem=(), hbm=(), cost=None):
     return pl.pallas_call(
         kernel,
         out_shape=out_shape,
-        in_specs=[SMEM if i in smem else VMEM for i in range(n_in)],
+        in_specs=[SMEM if i in smem else ANY if i in hbm else VMEM for i in range(n_in)],
         out_specs=jax.tree.map(lambda _: VMEM, out_shape),
         scratch_shapes=list(scratch),
         compiler_params=pltpu.CompilerParams(vmem_limit_bytes=LIMIT),
@@ -228,54 +278,74 @@
     peers, slots = send_rows.shape[1:]
     far = peers * slots
     width = rows + up(far, 128)
-    share = 4 * feats // peers
+    chips = peers // 2
+    share = 2 * feats // chips
     block = up(share + slots + 1, 16)
+    message = up(share + 2 * slots + 1, 16)
     gain = norm_gain.reshape(1, feats)
-    send = send_rows[0]
+    send = send_rows[0].T
+    swap = [(i, i ^ 1) for i in range(peers)]
+    sides = [list(range(k, peers, 2)) for k in range(2)]
 
     def like(shape, dtype):
         return jax.ShapeDtypeStruct(shape, dtype)
 
+    def across(x):
+        return lax.all_to_all(x, "nodes", 0, 0, axis_index_groups=sides, tiled=True)
+
     picked = call(
         pick_kernel,
-        like((far, feats), BF16),
+        like((peers, slots, feats), BF16),
         2,
-        (pltpu.VMEM((rows, feats), F32), pltpu.VMEM((far, feats), F32)),
+        (pltpu.VMEM((rows, feats), BF16), pltpu.VMEM((rows, feats), F32),
+         pltpu.SemaphoreType.DMA),
         smem=(0,),
+        hbm=(1,),
     )(send, node_feats)
-    arrived = lax.all_to_all(
-        picked.reshape(peers, slots, feats), "nodes", split_axis=0, concat_axis=0, tiled=True
-    ).reshape(far, feats)
+    arrived = lax.all_to_all(picked, "nodes", split_axis=0, concat_axis=0, tiled=True)
     square = like((rows, feats), BF16)
     cost = pl.CostEstimate(flops=2_000_000_000, bytes_accessed=2_000_000, transcendentals=0)
+    operands = (
+        node_feats, gain, w_query, w_key, w_value, w_out, cotangent, edge_dst, edge_src, edge_mask
+    )
     near = call(
         local_kernel,
         (square, square, square, like((feats, rows), BF16), like((feats, rows), BF16), square,
          like((rows, width), F32)),
         10,
+        [pltpu.VMEM(a.shape, a.dtype) for a in operands] + [pltpu.SemaphoreType.DMA((10,))],
+        hbm=range(10),
         cost=cost,
-    )(node_feats, gain, w_query, w_key, w_value, w_out, cotangent, edge_dst, edge_src, edge_mask)
-    output, gf, payload = call(
+    )(*operands)
+    output, gf, keep, give = call(
         attend_kernel,
-        (square, like((rows, feats), F32), like((peers, block, feats), BF16)),
+        (square, like((rows, feats), F32), like((chips, block, feats), F32),
+         like((chips, block, feats), BF16)),
         15,
         (
             pltpu.VMEM((HEADS, rows, width), BF16),
             pltpu.VMEM((HEADS, rows, width), F32),
             pltpu.VMEM((feats, width), F32),
             pltpu.VMEM((feats, width), F32),
+            pltpu.VMEM((4 * feats, feats), F32),
+            pltpu.VMEM((width - rows, feats), F32),
         ),
     )(node_feats, arrived, gain, w_query, w_key, w_value, w_out, cotangent, *near)
-    got = lax.all_to_all(payload, "nodes", split_axis=0, concat_axis=0, tiled=True)
-    shares = call(reduce_kernel, like((peers, share, feats), BF16), 1)(got)
-    whole = lax.all_to_all(shares, "nodes", split_axis=0, concat_axis=0, tiled=True)
+    given = lax.ppermute(give, "nodes", swap)
+    paired = call(
+        functools.partial(pair_kernel, share, slots), like((chips, message, feats), BF16), 2
+    )(keep, given)
+    got = across(paired)
+    shares = call(reduce_kernel, like((chips, share, feats), BF16), 1)(got)
+    mine = across(shares)
+    other = lax.ppermute(mine, "nodes", swap)
     grad_feats, grad_gain = call(
         functools.partial(finish_kernel, share),
         (like((rows, feats), F32), like((1, feats), F32)),
         3,
         smem=(0,),
     )(send, gf, got)
-    grads = call(spread_kernel, (like((feats, feats), F32),) * 4, 1)(whole)
+    grads = call(spread_kernel, (like((feats, feats), F32),) * 4, 2)(mine, other)
     return (output, grad_feats, grad_gain.reshape(feats), *grads)
 
 

time: 71.9 us -> 61.3 us (0.85)
  waiting for transfers between devices: 12.5 us -> 1.53 us
  blocking collectives: 23.9 us -> 26 us
  local copies, waits for them, and re-layouts: 8.07 us -> 6.78 us
  Pallas kernels: 14.5 us -> 15.6 us
  starting transfers between devices: 11 us -> 10.1 us
    all_to_all x2 -> x1, waiting for transfers between devices: 12.5 us -> 0.01 us  [on_device(): lax.all_to_all(picked, 'nodes', split_axis=0, concat_axis=0, tiled=True)]
    all_to_all x2 -> x1, starting transfers between devices: 11 us -> 7.36 us  [on_device(): lax.all_to_all(picked, 'nodes', split_axis=0, concat_axis=0, tiled=True)]
    ppermute x0 -> x2, starting transfers between devices: none -> 2.71 us  [the longest x1 2.61 us: on_device(): other = lax.ppermute(mine, 'nodes', swap)]
    all_to_all x1 -> x2, blocking collectives: 23.9 us -> 26 us  [across(): return lax.all_to_all(x, 'nodes', 0, 0, axis_index_groups=sides, tiled=True)]
    ppermute x0 -> x2, waiting for transfers between devices: none -> 1.53 us  [the longest x1 1.53 us: on_device(): given = lax.ppermute(give, 'nodes', swap)]
    pallas_call x1, Pallas kernels: 3.36 us -> 4.62 us  [on_device(): call(local_kernel, (square, square, square, like((feats, rows), BF16), li...]
    squeeze x1 -> x0, local copies, waits for them, and re-layouts: 0.76 us -> none  [on_device(): send = send_rows[0]]
    pallas_call x4 -> x5, Pallas kernels: 9.57 us -> 9.43 us  [the longest x1 6.84 us: on_device(): call(attend_kernel, (square, like((rows, feats), F32), like((chips, block...]
  transfers between devices with their start and end apart: 2 -> 3, of which waited for: 1 -> 1; matrix products, arithmetic and copies ran while one was open for 0% -> 0% of each run, Pallas kernels for 7% -> 10%
where the time goes in v2:
time: 61.3 us; the launch traced here: 60.8 us
  blocking collectives  26 us (42%)
  Pallas kernels  15.6 us (25%)
  starting transfers between devices  10.1 us (16%)
  local copies, waits for them, and re-layouts  6.78 us (11%)
  waiting for transfers between devices  1.53 us (2%)
  between operations  0.8 us (1%)
    all_to_all x2, blocking collectives, across(): return lax.all_to_all(x, 'nodes', 0, 0, axis_index_groups=sides, tiled=True)  26 us
    all_to_all x1, starting transfers between devices, on_device(): lax.all_to_all(picked, 'nodes', split_axis=0, concat_axis=0, tiled=True)  7.36 us
    pallas_call x1, Pallas kernels, on_device(): call(attend_kernel, (square, like((rows, feats), F32), like((chips, block...  6.84 us
    unnamed x36, local copies, waits for them, and re-layouts  6.78 us
    pallas_call x1, Pallas kernels, on_device(): call(local_kernel, (square, square, square, like((feats, rows), BF16), li...  4.62 us
    ppermute x1, starting transfers between devices, on_device(): other = lax.ppermute(mine, 'nodes', swap)  2.61 us
    pallas_call x1, Pallas kernels, on_device(): call(functools.partial(finish_kernel, share), (like((rows, feats), F32),...  1.55 us
    ppermute x1, waiting for transfers between devices, on_device(): given = lax.ppermute(give, 'nodes', swap)  1.53 us
  transfers between devices with their start and end apart: 3, of which 1 were waited for; matrix products, arithmetic and copies ran while one was open for 0% of the time, Pallas kernels for 10%

profile of v2, /device:TPU:1, one launch (start us, length us, event | category | flops | bytes accessed | tf_op | source)
XLA Modules:
  0.0 60.8 jit_solution(12778342371231453800)
XLA Ops:
  0.6 0.0 copy-start
  0.6 0.9 %copy-done = bf16[256,256]{1,0:T(8,128)(2,1)S(1)} copy-done((bf16[256,256]{1,0:T(8,128)(2,1)S(1)}, bf16[256,256]{1,0:T(8,128)(2,1)}, u32[]{:S(2)}) %copy-start) | copy-done | bytes 131096
  1.5 0.7 %copy-done.12 = s32[1,16,4]{1,2,0:T(4,128)S(1)} copy-done((s32[1,16,4]{1,2,0:T(4,128)S(1)}, s32[1,16,4]{1,2,0:T(4,128)}, u32[]{:S(2)}) %copy-start.12) | copy-done | bytes 280
  2.2 1.5 %shard_map.162 = bf16[16,4,256]{2,1,0:T(4,128)(2,1)} custom-call(s32[4,16]{1,0:T(4,128)S(1)} %bitcast.5, bf16[256,256]{1,0:T(8,128)(2,1)S(1)} %copy-done), custom_call_target="tpu_custom_call" | custom-call | tf_op jit(solution)/shard_map/pallas_call | solution.py:296
  3.7 0.0 copy-start.15
  3.7 0.0 copy-start.16
  3.7 7.4 %all-to-all-start = ((bf16[16,4,256]{2,1,0:T(4,128)(2,1)}), bf16[16,4,256]{2,1,0:T(4,128)(2,1)S(1)}, u32[]{:S(2)}, u32[]{:S(2)}) async-start(bf16[16,4,256]{2,1,0:T(4,128)(2,1)} %shard_map.162), calls=%async_computation | async-start | bytes 65536 | tf_op jit(solution)/shard_map/all_to_all | solution.py:305
  11.1 0.0 copy-done.1
  11.1 0.0 copy-done.17
  11.1 0.0 copy-done.15
  11.1 0.0 copy-done.16
  11.1 0.6 %copy-done.14 = f32[256]{0:T(256)S(1)} copy-done((f32[256]{0:T(256)S(1)}, f32[256]{0:T(256)}, u32[]{:S(2)}) %copy-start.14) | copy-done | bytes 1048
  11.8 0.9 %copy-done.2 = bf16[256,256]{1,0:T(8,128)(2,1)S(1)} copy-done((bf16[256,256]{1,0:T(8,128)(2,1)S(1)}, bf16[256,256]{1,0:T(8,128)(2,1)}, u32[]{:S(2)}) %copy-start.2) | copy-done | bytes 131096
  12.7 0.9 %copy-done.4 = bf16[256,256]{1,0:T(8,128)(2,1)S(1)} copy-done((bf16[256,256]{1,0:T(8,128)(2,1)S(1)}, bf16[256,256]{1,0:T(8,128)(2,1)}, u32[]{:S(2)}) %copy-start.4) | copy-done | bytes 131096
  13.6 0.9 %copy-done.6 = bf16[256,256]{1,0:T(8,128)(2,1)S(1)} copy-done((bf16[256,256]{1,0:T(8,128)(2,1)S(1)}, bf16[256,256]{1,0:T(8,128)(2,1)}, u32[]{:S(2)}) %copy-start.6) | copy-done | bytes 131096
  14.5 0.9 %copy-done.8 = bf16[256,256]{1,0:T(8,128)(2,1)S(1)} copy-done((bf16[256,256]{1,0:T(8,128)(2,1)S(1)}, bf16[256,256]{1,0:T(8,128)(2,1)}, u32[]{:S(2)}) %copy-start.8) | copy-done | bytes 131096
  15.4 0.9 %copy-done.10 = bf16[256,256]{1,0:T(8,128)(2,1)S(1)} copy-done((bf16[256,256]{1,0:T(8,128)(2,1)S(1)}, bf16[256,256]{1,0:T(8,128)(2,1)}, u32[]{:S(2)}) %copy-start.10) | copy-done | bytes 131096
  16.3 0.0 copy-start.11
  16.3 4.6 %shard_map.163 = (bf16[256,256]{1,0:T(8,128)(2,1)S(1)}, bf16[256,256]{1,0:T(8,128)(2,1)S(1)}, bf16[256,256]{1,0:T(8,128)(2,1)S(1)}, bf16[256,256]{1,0:T(8,128)(2...) custom-call(bf16[256,256]{1,0:T(8,128)(2,1)S(1)} %copy-done.1, ...), custom_call_target="tpu_custom_call" | custom-call | flops 2000000000 | bytes 2000000 | tf_op jit(solution)/shard_map/pallas_call | solution.py:311
  20.9 0.0 all-to-all-done.far_ref
  21.0 6.8 %shard_map.164 = (bf16[256,256]{1,0:T(8,128)(2,1)}, f32[256,256]{1,0:T(8,128)S(1)}, f32[8,80,256]{2,1,0:T(8,128)S(1)}, bf16[8,80,256]{2,1,0:T(8,128)(2,1)S(1)}) custom-call(bf16[256,256]{1,0:T(8,128)(2,1)S(1)} %copy-done.1, bf16[16,4,256]{2,1,0:T(4,128)(2,1)S(1)} %all-to-all-done.far_ref, f32[1,256]{1,0:T(1,128)S(1)} %bitcast.8, ...), custom_call_target="tpu_custom_call" | custom-call | tf_op jit(solution)/shard_map/pallas_call | solution.py:320
  27.8 0.1 collective-permute-start
  27.9 1.5 %collective-permute-done.got_ref = bf16[8,80,256]{2,1,0:T(8,128)(2,1)S(1)} collective-permute-done((bf16[8,80,256]{2,1,0:T(8,128)(2,1)S(1)}, bf16[8,80,256]{2,1,0:T(8,128)(2,1)S(1)}, u32[]{:S(2)}, u32[]{:S(2)}) %collective-permute-start) | collective-permute-done | bytes 327712 | tf_op jit(solution)/shard_map/ppermute | solution.py:334
  29.5 0.1 shard_map.165
  29.6 14.7 %all_to_all.15.got_ref = bf16[8,80,256]{2,1,0:T(8,128)(2,1)S(1)} all-to-all(bf16[8,80,256]{2,1,0:T(8,128)(2,1)S(1)} %shard_map.165), channel_id=1, replica_groups={{0,2,4,6,8,10,12,14},{1,3,5,7,9,11,13,15},{16,18,20,22,24,26,28,30},{17..., dimensions={0} | all-to-all | bytes 655360 | tf_op jit(solution)/shard_map/all_to_all | solution.py:294
  44.3 0.0 copy-start.13
  44.4 11.3 %all_to_all.16.mine_ref = bf16[8,64,256]{2,1,0:T(8,128)(2,1)S(1)} all-to-all(bf16[8,64,256]{2,1,0:T(8,128)(2,1)S(1)} %shard_map.167), channel_id=1, replica_groups={{0,2,4,6,8,10,12,14},{1,3,5,7,9,11,13,15},{16,18,20,22,24,26,28,30},{17..., dimensions={0} | all-to-all | bytes 524288 | tf_op jit(solution)/shard_map/all_to_all | solution.py:294
  55.7 2.6 %collective-permute-start.1 = (bf16[8,64,256]{2,1,0:T(8,128)(2,1)S(1)}, bf16[8,64,256]{2,1,0:T(8,128)(2,1)S(1)}, u32[]{:S(2)}, u32[]{:S(2)}) collective-permute-start(bf16[8,64,256]{2,1,0:T(8,128)(2,1)S(1)} %all_to_all.16.mine_ref), channel_id=1, source_target_pairs={{0,1},{1,0},{2,3},{3,2},{4,5},{5,4},{6,7},{7,6},{8,9},{9,8},{10,11... | collective-permute-start | bytes 786440 | tf_op jit(solution)/shard_map/ppermute | solution.py:341
  58.3 0.0 copy-done.13
  58.3 1.6 %shard_map.166 = (f32[256,256]{1,0:T(8,128)}, f32[1,256]{1,0:T(1,128)}) custom-call(s32[4,16]{1,0:T(4,128)S(1)} %bitcast.6, f32[256,256]{1,0:T(8,128)S(1)} %get-tuple-element.32.gf_ref, bf16[8,80,256]{2,1,0:T(8,128)(2,1)S(1)} %all_to_all.15.got_ref), custom_call_target="tpu_custom_call" | custom-call | tf_op jit(solution)/shard_map/pallas_call | solution.py:342
  59.8 0.0 collective-permute-done.1.other_ref
  59.8 1.0 %shard_map.168 = (f32[256,256]{1,0:T(8,128)}, f32[256,256]{1,0:T(8,128)}, f32[256,256]{1,0:T(8,128)}, f32[256,256]{1,0:T(8,128)}) custom-call(bf16[8,64,256]{2,1,0:T(8,128)(2,1)S(1)} %all_to_all.16.mine_ref, bf16[8,64,256]{2,1,0:T(8,128)(2,1)S(1)} %collective-permute-done.1.other_ref), custom_call_target="tpu_custom_call" | custom-call | tf_op jit(solution)/shard_map/pallas_call | solution.py:348
  (19 shorter events, 0.1 us)
Async XLA Ops:
  0.6 0.9 %copy-start = (bf16[256,256]{1,0:T(8,128)(2,1)S(1)}, bf16[256,256]{1,0:T(8,128)(2,1)}, u32[]{:S(2)}) copy-start(bf16[256,256]{1,0:T(8,128)(2,1)} %x_ref.1) | copy-start | bytes 393220
  1.5 0.7 %copy-start.12 = (s32[1,16,4]{1,2,0:T(4,128)S(1)}, s32[1,16,4]{1,2,0:T(4,128)}, u32[]{:S(2)}) copy-start(s32[1,16,4]{1,2,0:T(4,128)} %param.21) | copy-start | bytes 772
  2.2 8.9 %copy-start.1 = (bf16[256,256]{1,0:T(8,128)(2,1)S(1)}, bf16[256,256]{1,0:T(8,128)(2,1)}, u32[]{:S(2)}) copy-start(bf16[256,256]{1,0:T(8,128)(2,1)} %x_ref.1) | copy-start | bytes 393220
  2.2 8.9 %copy-start.17 = (s32[48,128]{1,0:T(8,128)S(1)}, s32[48,128]{1,0:T(8,128)}, u32[]{:S(2)}) copy-start(s32[48,128]{1,0:T(8,128)} %refs_9_.1) | copy-start | bytes 73732
  3.7 7.4 %copy-start.15 = (s32[48,128]{1,0:T(8,128)S(1)}, s32[48,128]{1,0:T(8,128)}, u32[]{:S(2)}) copy-start(s32[48,128]{1,0:T(8,128)} %refs_7_.1) | copy-start | bytes 73732
  3.7 7.4 %copy-start.16 = (s32[48,128]{1,0:T(8,128)S(1)}, s32[48,128]{1,0:T(8,128)}, u32[]{:S(2)}) copy-start(s32[48,128]{1,0:T(8,128)} %refs_8_.1) | copy-start | bytes 73732
  3.7 17.2 %all-to-all-start = ((bf16[16,4,256]{2,1,0:T(4,128)(2,1)}), bf16[16,4,256]{2,1,0:T(4,128)(2,1)S(1)}, u32[]{:S(2)}, u32[]{:S(2)}) async-start(bf16[16,4,256]{2,1,0:T(4,128)(2,1)} %shard_map.162), calls=%async_computation | async-start | bytes 65536 | tf_op jit(solution)/shard_map/all_to_all | solution.py:305
  11.1 0.7 %copy-start.14 = (f32[256]{0:T(256)S(1)}, f32[256]{0:T(256)}, u32[]{:S(2)}) copy-start(f32[256]{0:T(256)} %param.12) | copy-start | bytes 3076
  11.8 0.9 %copy-start.2 = (bf16[256,256]{1,0:T(8,128)(2,1)S(1)}, bf16[256,256]{1,0:T(8,128)(2,1)}, u32[]{:S(2)}) copy-start(bf16[256,256]{1,0:T(8,128)(2,1)} %wq_ref.1) | copy-start | bytes 393220
  12.7 0.9 %copy-start.4 = (bf16[256,256]{1,0:T(8,128)(2,1)S(1)}, bf16[256,256]{1,0:T(8,128)(2,1)}, u32[]{:S(2)}) copy-start(bf16[256,256]{1,0:T(8,128)(2,1)} %wk_ref.1) | copy-start | bytes 393220
  13.6 0.9 %copy-start.6 = (bf16[256,256]{1,0:T(8,128)(2,1)S(1)}, bf16[256,256]{1,0:T(8,128)(2,1)}, u32[]{:S(2)}) copy-start(bf16[256,256]{1,0:T(8,128)(2,1)} %wv_ref.1) | copy-start | bytes 393220
  14.5 0.9 %copy-start.8 = (bf16[256,256]{1,0:T(8,128)(2,1)S(1)}, bf16[256,256]{1,0:T(8,128)(2,1)}, u32[]{:S(2)}) copy-start(bf16[256,256]{1,0:T(8,128)(2,1)} %wo_ref.1) | copy-start | bytes 393220
  15.4 0.9 %copy-start.10 = (bf16[256,256]{1,0:T(8,128)(2,1)S(1)}, bf16[256,256]{1,0:T(8,128)(2,1)}, u32[]{:S(2)}) copy-start(bf16[256,256]{1,0:T(8,128)(2,1)} %cot_ref.1) | copy-start | bytes 393220
  16.3 4.7 %copy-start.3 = (bf16[256,256]{1,0:T(8,128)(2,1)S(1)}, bf16[256,256]{1,0:T(8,128)(2,1)}, u32[]{:S(2)}) copy-start(bf16[256,256]{1,0:T(8,128)(2,1)} %wq_ref.1) | copy-start | bytes 393220
  16.3 4.7 %copy-start.5 = (bf16[256,256]{1,0:T(8,128)(2,1)S(1)}, bf16[256,256]{1,0:T(8,128)(2,1)}, u32[]{:S(2)}) copy-start(bf16[256,256]{1,0:T(8,128)(2,1)} %wk_ref.1) | copy-start | bytes 393220
  16.3 4.7 %copy-start.7 = (bf16[256,256]{1,0:T(8,128)(2,1)S(1)}, bf16[256,256]{1,0:T(8,128)(2,1)}, u32[]{:S(2)}) copy-start(bf16[256,256]{1,0:T(8,128)(2,1)} %wv_ref.1) | copy-start | bytes 393220
  16.3 4.7 %copy-start.9 = (bf16[256,256]{1,0:T(8,128)(2,1)S(1)}, bf16[256,256]{1,0:T(8,128)(2,1)}, u32[]{:S(2)}) copy-start(bf16[256,256]{1,0:T(8,128)(2,1)} %wo_ref.1) | copy-start | bytes 393220
  16.3 4.7 %copy-start.11 = (bf16[256,256]{1,0:T(8,128)(2,1)S(1)}, bf16[256,256]{1,0:T(8,128)(2,1)}, u32[]{:S(2)}) copy-start(bf16[256,256]{1,0:T(8,128)(2,1)} %cot_ref.1) | copy-start | bytes 393220
  27.8 1.6 %collective-permute-start = (bf16[8,80,256]{2,1,0:T(8,128)(2,1)S(1)}, bf16[8,80,256]{2,1,0:T(8,128)(2,1)S(1)}, u32[]{:S(2)}, u32[]{:S(2)}) collective-permute-start(bf16[8,80,256]{2,1,0:T(8,128)(2,1)S(1)} %get-tuple-element.34), channel_id=1, source_target_pairs={{0,1},{1,0},{2,3},{3,2},{4,5},{5,4},{6,7},{7,6},{8,9},{9,8},{10,11... | collective-permute-start | bytes 983048 | tf_op jit(solution)/shard_map/ppermute | solution.py:334
  44.3 13.9 %copy-start.13 = (s32[1,16,4]{1,2,0:T(4,128)S(1)}, s32[1,16,4]{1,2,0:T(4,128)}, u32[]{:S(2)}) copy-start(s32[1,16,4]{1,2,0:T(4,128)} %param.21) | copy-start | bytes 772
  55.7 4.2 %collective-permute-start.1 = (bf16[8,64,256]{2,1,0:T(8,128)(2,1)S(1)}, bf16[8,64,256]{2,1,0:T(8,128)(2,1)S(1)}, u32[]{:S(2)}, u32[]{:S(2)}) collective-permute-start(bf16[8,64,256]{2,1,0:T(8,128)(2,1)S(1)} %all_to_all.16.mine_ref), channel_id=1, source_target_pairs={{0,1},{1,0},{2,3},{3,2},{4,5},{5,4},{6,7},{7,6},{8,9},{9,8},{10,11... | collective-permute-start | bytes 786440 | tf_op jit(solution)/shard_map/ppermute | solution.py:341

commit v3 on v2

v3 whole, which is shorter than its diff:
```python
import functools
import math

import jax
import jax.numpy as jnp
from jax import lax
from jax.experimental import pallas as pl
from jax.experimental.pallas import tpu as pltpu
from jax.sharding import PartitionSpec as P

HEADS = 8
EARLY = 4
EPS = 1e-05
F32 = jnp.float32
BF16 = jnp.bfloat16
VMEM = pl.BlockSpec(memory_space=pltpu.VMEM)
SMEM = pl.BlockSpec(memory_space=pltpu.SMEM)
HBM = pl.BlockSpec(memory_space=pltpu.HBM)
MIB = 1024 * 1024
FULL = 60


def up(n, m):
    return -(-n // m) * m


def dot(a, b):
    return jnp.dot(a, b, preferred_element_type=F32)


def dot_t(a, b):
    return lax.dot_general(a, b, (((1,), (1,)), ((), ())), preferred_element_type=F32)


def standardize(x):
    centered = x - jnp.mean(x, axis=1, keepdims=True)
    rstd = lax.rsqrt(jnp.mean(centered * centered, axis=1, keepdims=True) + EPS)
    return centered * rstd, rstd


def pull(g, xhat, rstd):
    mean_g = jnp.mean(g, axis=1, keepdims=True)
    mean_gx = jnp.mean(g * xhat, axis=1, keepdims=True)
    return rstd * (g - mean_g - xhat * mean_gx)


def begin(sources, targets, sems):
    copies = [
        pltpu.make_async_copy(source, target, sems.at[i])
        for i, (source, target) in enumerate(zip(sources, targets))
    ]
    for copy in copies:
        copy.start()
    return copies


def finish_all(copies):
    for copy in copies:
        copy.wait()


def pick_kernel(send_hbm, *refs):
    squares = refs[:6]
    edges = refs[6:9]
    out_ref, square_ref, edge_ref, send, wide, sems = refs[9:]
    copies = begin(
        (send_hbm,) + squares + edges,
        [send] + [square_ref.at[i] for i in range(6)] + [edge_ref.at[i] for i in range(3)],
        sems,
    )
    finish_all(copies[:2])
    slots, peers = send.shape
    wide[...] = square_ref[0].astype(F32)
    for peer in range(peers):
        rows = [wide[pl.ds(send[slot, peer], 1), :] for slot in range(slots)]
        out_ref[peer] = jnp.concatenate(rows, axis=0).astype(BF16)
    finish_all(copies[2:])


def head_hots(feats):
    lane = lax.broadcasted_iota(jnp.int32, (1, feats), 1)
    size = feats // HEADS
    masks = [(lane >= h * size) & (lane < (h + 1) * size) for h in range(HEADS)]
    return masks, [m.astype(F32).astype(BF16) for m in masks]


def weigh(queries, keys, count, head):
    t = jnp.tanh(dot_t(queries, keys) * (0.2 / math.sqrt(head)))
    w = count * jnp.exp(5.0 * t)
    return w.astype(BF16), (w * (1.0 - t * t) * (1.0 / math.sqrt(head))).astype(BF16)


def local_kernel(gain_ref, square_ref, edge_ref, low_ref, far_count, near_count, w_ref, g_ref):
    x_ref, wq_ref, wk_ref, wv_ref, wo_ref, cot_ref = [square_ref.at[i] for i in range(6)]
    queries, keys = local_project(
        x_ref, gain_ref, wq_ref, wk_ref, wv_ref, wo_ref, cot_ref, low_ref
    )
    rows, feats = queries.shape
    local_count(edge_ref.at[0], edge_ref.at[1], edge_ref.at[2], far_count, near_count)
    _, hots = head_hots(feats)
    for h in range(EARLY):
        w_ref[h], g_ref[h] = weigh(queries * hots[h], keys, near_count[...], feats // HEADS)


def local_project(x_ref, gain_ref, wq_ref, wk_ref, wv_ref, wo_ref, cot_ref, low_ref):
    xhat, _ = standardize(x_ref[...].astype(F32))
    normed = (xhat * gain_ref[...]).astype(BF16)
    queries = dot(normed, wq_ref[...]).astype(BF16)
    keys = dot(normed, wk_ref[...]).astype(BF16)
    low_ref[0] = queries
    low_ref[1] = keys
    low_ref[2] = dot(normed, wv_ref[...]).astype(BF16)
    low_ref[3] = queries.T
    low_ref[4] = normed.T
    low_ref[5] = dot_t(cot_ref[...], wo_ref[...]).astype(BF16)
    return queries, keys


def local_count(dst_ref, src_ref, mask_ref, far_count, near_count):
    rows, far = far_count.shape
    row_id = lax.broadcasted_iota(jnp.int32, (rows, rows), 0)
    col_id = lax.broadcasted_iota(jnp.int32, (rows, rows), 1)
    near_count[...] = (row_id == col_id).astype(F32)
    far_count[...] = jnp.zeros((rows, far), F32)
    group = 8
    edge = 128
    dst_id = lax.broadcasted_iota(jnp.int32, (rows, edge), 0)
    src_id = lax.broadcasted_iota(jnp.int32, (rows + far, edge), 0)

    def step(i, carry):
        base = pl.multiple_of(i * group, group)
        dst = dst_ref[pl.ds(base, group), :]
        src = jnp.where(mask_ref[pl.ds(base, group), :] > 0, src_ref[pl.ds(base, group), :], -1)
        hot_dst = jnp.concatenate(
            [(dst_id == dst[j : j + 1]).astype(F32).astype(BF16) for j in range(group)], axis=1
        )
        hot_src = jnp.concatenate(
            [(src_id == src[j : j + 1]).astype(F32).astype(BF16) for j in range(group)], axis=1
        )
        part = dot_t(hot_dst, hot_src)
        near_count[...] += part[:, :rows]
        far_count[...] += part[:, rows:]
        return carry

    lax.fori_loop(0, dst_ref.shape[0] // group, step, 0)


def attend_kernel(
    far_ref, gain_ref, square_ref, low_ref, far_count, near_count, near_w, near_g,
    att_ref, near_ref, keep_ref, give_ref,
    w_scr, g_scr, dkt_scr, dvt_scr, grad_scr,
):
    _, wq_ref, wk_ref, wv_ref, _, cot_ref = [square_ref.at[i] for i in range(6)]
    _, rows, feats = low_ref.shape
    q_ref, k_ref, v_ref, qt_ref, normt_ref, datt_ref = [low_ref.at[i] for i in range(6)]
    peers, slots, _ = far_ref.shape
    far = peers * slots
    width = far_count.shape[1]
    head = feats // HEADS
    chips, block, _ = keep_ref.shape
    pad = width - far
    far_x = jnp.concatenate([far_ref[p].astype(F32) for p in range(peers)], axis=0)
    if pad:
        far_x = jnp.concatenate([far_x, jnp.zeros((pad, feats), F32)], axis=0)
    gain = gain_ref[...]
    far_hat, far_rstd = standardize(far_x)
    far_normed = (far_hat * gain).astype(BF16)
    far_keys = dot(far_normed, wk_ref[...]).astype(BF16)
    far_values = dot(far_normed, wv_ref[...]).astype(BF16)
    keys = jnp.concatenate([k_ref[...], far_keys], axis=0)
    values = jnp.concatenate([v_ref[...], far_values], axis=0)
    masks, hots = head_hots(feats)
    queries = q_ref[...]
    count = far_count[...]
    both_count = jnp.concatenate([near_count[...], count], axis=1)
    num = jnp.zeros((rows, feats), F32)
    den = jnp.zeros((rows, feats), F32)
    for h in range(HEADS):
        q_head = queries * hots[h]
        if h < EARLY:
            w, g = weigh(q_head, far_keys, count, head)
            w = jnp.concatenate([near_w[h], w], axis=1)
            g = jnp.concatenate([near_g[h], g], axis=1)
        else:
            w, g = weigh(q_head, keys, both_count, head)
        w_scr[h] = w
        g_scr[h] = g
        num = num + dot(w, values * hots[h])
        den = den + dot(w, jnp.broadcast_to(hots[h], (rows + width, feats)))
    rden = 1.0 / den
    att32 = num * rden
    att = att32.astype(BF16)
    att_ref[...] = att
    grad_out = dot(att.T, cot_ref[...])
    dnum = (datt_ref[...].astype(F32) * rden).astype(BF16)
    dnum_t = dnum.T
    prod = dnum.astype(F32) * att32
    qt = qt_ref[...]
    dq = jnp.zeros((rows, feats), F32)
    for h in range(HEADS):
        z = jnp.sum(jnp.where(masks[h], prod, 0.0), axis=1, keepdims=True)
        dw = dot_t(dnum * hots[h], values) - z
        ds = (g_scr[h].astype(F32) * dw).astype(BF16)
        dq = dq + dot(ds, keys * hots[h])
        at = slice(h * head, (h + 1) * head)
        dkt_scr[at, :] = dot(qt[at, :], ds)
        dvt_scr[at, :] = dot(dnum_t[at, :], w_scr[h])
    dq = dq.astype(BF16)
    dkt = dkt_scr[...].astype(BF16)
    dvt = dvt_scr[...].astype(BF16)
    norm_t = jnp.concatenate([normt_ref[...], far_normed.T], axis=1)
    grad_query = dot(normt_ref[...], dq)
    grad_key = dot_t(norm_t, dkt)
    grad_value = dot_t(norm_t, dvt)
    d_normed = (dot(wk_ref[...], dkt) + dot(wv_ref[...], dvt)).T
    near = d_normed[:rows] + dot_t(dq, wq_ref[...])
    near_ref[...] = near
    away = d_normed[rows:]
    away_dx = pull(away * gain, far_hat, far_rstd)
    grad_scr[...] = jnp.concatenate([grad_query, grad_key, grad_value, grad_out], axis=0)
    half = grad_scr.shape[0] // 2
    share = half // chips
    blank = jnp.zeros((block - share - slots, feats), F32)
    core = lax.rem(lax.axis_index("nodes"), 2)
    for c in range(chips):
        for own in (True, False):
            which = core if own else 1 - core
            start = pl.multiple_of(which * half + c * share, 8)
            dx = [away_dx[(2 * c + i) * slots : (2 * c + i + 1) * slots] for i in range(2)]
            part = jnp.concatenate(
                [grad_scr[pl.ds(start, share), :], jnp.where(which == 0, dx[0], dx[1]), blank],
                axis=0,
            )
            if own:
                keep_ref[c] = part
            else:
                give_ref[c] = part.astype(BF16)


def pair_kernel(share, slots, keep_ref, got_ref, out_ref):
    chips, block, feats = out_ref.shape
    blank = [jnp.zeros((block - share - 2 * slots, feats), F32)] * (block > share + 2 * slots)
    for c in range(chips):
        keep = keep_ref[c]
        got = got_ref[c].astype(F32)
        end = share + slots
        out_ref[c] = jnp.concatenate(
            [keep[:share] + got[:share], keep[share:end], got[share:end]] + blank, axis=0
        ).astype(BF16)


def reduce_kernel(got_ref, share_ref):
    chips, share, _ = share_ref.shape
    total = jnp.zeros(share_ref.shape[1:], F32)
    for c in range(chips):
        total = total + got_ref[c].astype(F32)[:share]
    share_ref[...] = jnp.broadcast_to(total.astype(BF16)[None], share_ref.shape)


def own_kernel(square_ref, gain_ref, near_ref, att_ref, out_ref, feats_ref):
    x = square_ref[0].astype(F32)
    out_ref[...] = (x + dot(att_ref[...], square_ref[4])).astype(BF16)
    dx = pull(near_ref[...] * gain_ref[...], *standardize(x))
    feats_ref[...] = square_ref[5].astype(F32) + dx


def finish_kernel(share, send_ref, got_ref, own_ref, feats_ref):
    slots, peers = send_ref.shape
    feats_ref[...] = own_ref[...]
    core = lax.rem(lax.axis_index("nodes"), 2)
    for c in range(peers // 2):
        got = got_ref[c].astype(F32)
        for i in range(2 * slots):
            peer = 2 * c + (core if i < slots else 1 - core)
            at = pl.ds(send_ref[i % slots, peer], 1)
            feats_ref[at, :] += got[share + i : share + i + 1]


def spread_kernel(mine_ref, other_ref, gain_ref, wq_ref, wk_ref, wv_ref, *out_refs):
    rows = wq_ref.shape[0]
    chips, share, feats = mine_ref.shape
    first = lax.rem(lax.axis_index("nodes"), 2) == 0
    mine = mine_ref[...].astype(F32).reshape(chips * share, feats)
    other = other_ref[...].astype(F32).reshape(chips * share, feats)
    low = jnp.where(first, mine, other)
    high = jnp.where(first, other, mine)
    grads = (low[:rows], low[rows:], high[:rows], high[rows:])
    for grad, out_ref in zip(grads, out_refs):
        out_ref[...] = grad
    prod = jnp.zeros((rows, feats), F32)
    for grad, w_ref in zip(grads, (wq_ref, wk_ref, wv_ref)):
        prod = prod + grad * w_ref[...].astype(F32)
    out_refs[4][...] = jnp.sum(prod.T, axis=0, keepdims=True) / gain_ref[...]


def call(kernel, out_shape, in_specs, scratch=(), cost=None, out_specs=None, mib=16):
    return pl.pallas_call(
        kernel,
        out_shape=out_shape,
        in_specs=in_specs,
        out_specs=jax.tree.map(lambda _: VMEM, out_shape) if out_specs is None else out_specs,
        scratch_shapes=list(scratch),
        compiler_params=pltpu.CompilerParams(vmem_limit_bytes=mib * MIB),
        cost_estimate=cost,
    )


def on_device(
    node_feats, norm_gain, w_query, w_key, w_value, w_out, cotangent,
    edge_dst, edge_src, edge_mask, send_rows,
):
    rows, feats = node_feats.shape
    peers, slots = send_rows.shape[1:]
    far = peers * slots
    width = up(far, 128)
    chips = peers // 2
    share = 2 * feats // chips
    block = up(share + slots, 8)
    message = up(share + 2 * slots, 8)
    gain = norm_gain.reshape(1, feats)
    send = send_rows[0].T
    swap = [(i, i ^ 1) for i in range(peers)]
    sides = [list(range(k, peers, 2)) for k in range(2)]

    def like(shape, dtype):
        return jax.ShapeDtypeStruct(shape, dtype)

    def across(x):
        return lax.all_to_all(x, "nodes", 0, 0, axis_index_groups=sides, tiled=True)

    cost = pl.CostEstimate(flops=8_000_000_000, bytes_accessed=2_000_000, transcendentals=0)
    square = like((rows, feats), BF16)
    wide = like((rows, feats), F32)
    picked, squares, edges = call(
        pick_kernel,
        (like((peers, slots, feats), BF16), like((6, rows, feats), BF16),
         like((3,) + edge_dst.shape, jnp.int32)),
        [HBM] * 10,
        (pltpu.SMEM((slots, peers), jnp.int32), pltpu.VMEM((rows, feats), F32),
         pltpu.SemaphoreType.DMA((10,))),
        mib=FULL,
    )(send, node_feats, w_query, w_key, w_value, w_out, cotangent, edge_dst, edge_src, edge_mask)
    arrived = lax.all_to_all(picked, "nodes", split_axis=0, concat_axis=0, tiled=True)
    heads = like((EARLY, rows, rows), BF16)
    low, far_count, near_count, w, g = call(
        local_kernel,
        (like((6, rows, feats), BF16), like((rows, width), F32), like((rows, rows), F32),
         heads, heads),
        [VMEM] * 3,
        cost=cost,
    )(gain, squares, edges)
    att, near, keep, give = call(
        attend_kernel,
        (square, wide, like((chips, block, feats), F32), like((chips, block, feats), BF16)),
        [VMEM] * 8,
        [
            pltpu.VMEM((HEADS, rows, rows + width), BF16),
            pltpu.VMEM((HEADS, rows, rows + width), BF16),
            pltpu.VMEM((feats, rows + width), F32),
            pltpu.VMEM((feats, rows + width), F32),
            pltpu.VMEM((4 * feats, feats), F32),
        ],
    )(arrived, gain, squares, low, far_count, near_count, w, g)
    given = lax.ppermute(give, "nodes", swap)
    output, own = call(own_kernel, (square, wide), [VMEM] * 4, cost=cost)(
        squares, gain, near, att
    )
    given, own = lax.optimization_barrier((given, own))
    paired = call(
        functools.partial(pair_kernel, share, slots),
        like((chips, message, feats), BF16),
        [VMEM] * 2,
    )(keep, given)
    got = across(paired)
    shares = call(reduce_kernel, like((chips, share, feats), BF16), [VMEM])(got)
    mine = across(shares)
    other = lax.ppermute(mine, "nodes", swap)
    grad_feats = call(
        functools.partial(finish_kernel, share), wide, [SMEM] + [VMEM] * 2, cost=cost
    )(send, got, own)
    *grads, grad_gain = call(
        spread_kernel, (like((feats, feats), F32),) * 4 + (like((1, feats), F32),), [VMEM] * 6
    )(mine, other, gain, w_query, w_key, w_value)
    return (output, grad_feats, grad_gain.reshape(feats), *grads)


def solution(mesh):
    nodes = P(("groups", "nodes"), None)
    in_specs = (
        nodes, P(), P(), P(), P(), P(), nodes, nodes, nodes, nodes,
        P(("groups", "nodes"), None, None),
    )
    out_specs = (nodes, nodes, P("groups")) + (P("groups", None),) * 4
    return jax.shard_map(
        on_device, mesh=mesh, in_specs=in_specs, out_specs=out_specs, check_vma=False
    )
```

time: 61.3 us -> 55.8 us (0.910)
  local copies, waits for them, and re-layouts: 6.78 us -> 2.71 us
  waiting for transfers between devices: 1.53 us -> 0.56 us
    unnamed x36 -> x16, local copies, waits for them, and re-layouts: 6.78 us -> 2.71 us
    ppermute x1, waiting for transfers between devices: 1.53 us -> 0.56 us  [on_device(): given = lax.ppermute(give, 'nodes', swap)]
    all_to_all x2, blocking collectives: 26 us -> 25.4 us  [across(): return lax.all_to_all(x, 'nodes', 0, 0, axis_index_groups=sides, tiled=True)]
    pallas_call x6 -> x7, Pallas kernels: 15.5 us -> 15.8 us  [the longest x1 6.12 us: on_device(): call(attend_kernel, (square, wide, like((chips, block, feats), F32), like...]
  transfers between devices with their start and end apart: 3 -> 3, of which waited for: 1 -> 1; matrix products, arithmetic and copies ran while one was open for 0% -> 0% of each run, Pallas kernels for 10% -> 11%
where the time goes in v3:
time: 55.8 us; the launch traced here: 55.4 us
  blocking collectives  25.4 us (46%)
  Pallas kernels  15.9 us (28%)
  starting transfers between devices  10.2 us (18%)
  local copies, waits for them, and re-layouts  2.71 us (5%)
  between operations  0.71 us (1%)
  waiting for transfers between devices  0.56 us (1%)
    all_to_all x2, blocking collectives, across(): return lax.all_to_all(x, 'nodes', 0, 0, axis_index_groups=sides, tiled=True)  25.4 us
    all_to_all x1, starting transfers between devices, on_device(): lax.all_to_all(picked, 'nodes', split_axis=0, concat_axis=0, tiled=True)  7.36 us
    pallas_call x1, Pallas kernels, on_device(): call(attend_kernel, (square, wide, like((chips, block, feats), F32), like...  6.12 us
    pallas_call x1, Pallas kernels, on_device(): call(local_kernel, (like((6, rows, feats), BF16), like((rows, width), F32...  3.93 us
    unnamed x16, local copies, waits for them, and re-layouts  2.71 us
    ppermute x1, starting transfers between devices, on_device(): other = lax.ppermute(mine, 'nodes', swap)  2.6 us
    pallas_call x1, Pallas kernels, on_device(): call(pick_kernel, (like((peers, slots, feats), BF16), like((6, rows, feat...  2.2 us
    pallas_call x1, Pallas kernels, on_device(): call(functools.partial(finish_kernel, share), wide, [SMEM] + [VMEM] * 2,...  1.54 us
  transfers between devices with their start and end apart: 3, of which 1 were waited for; matrix products, arithmetic and copies ran while one was open for 0% of the time, Pallas kernels for 11%

profile of v3, /device:TPU:1, one launch (start us, length us, event | category | flops | bytes accessed | tf_op | source)
XLA Modules:
  0.0 55.4 jit_solution(15036574024988191473)
XLA Ops:
  0.6 2.2 %shard_map.162 = (bf16[16,4,256]{2,1,0:T(4,128)(2,1)}, bf16[6,256,256]{2,1,0:T(8,128)(2,1)}, s32[3,48,128]{2,1,0:T(8,128)}) custom-call(s32[4,16]{1,0:T(4,128)} %bitcast.9, bf16[256,256]{1,0:T(8,128)(2,1)} %refs_0_.1, bf16[256,256]{1,0:T(8,128)(2,1)} %wq_ref.1, bf16[256,256]{1,0:T(8,128)(2,1)} %wk_ref.1, bf16[256,256]{1,0:T(8,128)(2,1)} %wv_ref.1, ...), custom_call_target="tpu_custom_call" | custom-call | tf_op jit(solution)/shard_map/pallas_call | solution.py:334
  2.8 7.4 %all-to-all-start = ((bf16[16,4,256]{2,1,0:T(4,128)(2,1)}), bf16[16,4,256]{2,1,0:T(4,128)(2,1)S(1)}, u32[]{:S(2)}, u32[]{:S(2)}) async-start(bf16[16,4,256]{2,1,0:T(4,128)(2,1)} %get-tuple-element.29), calls=%async_computation | async-start | bytes 65536 | tf_op jit(solution)/shard_map/all_to_all | solution.py:343
  10.2 0.0 copy-start.5
  10.2 0.7 %copy-done.5 = f32[256]{0:T(256)S(1)} copy-done((f32[256]{0:T(256)S(1)}, f32[256]{0:T(256)}, u32[]{:S(2)}) %copy-start.5) | copy-done | bytes 1048
  10.9 0.0 copy-start
  10.9 1.1 %copy-done = bf16[6,256,256]{2,1,0:T(8,128)(2,1)S(1)} copy-done((bf16[6,256,256]{2,1,0:T(8,128)(2,1)S(1)}, bf16[6,256,256]{2,1,0:T(8,128)(2,1)}, u32[]{:S(2)}) %copy-start) | copy-done | bytes 786456
  12.0 0.0 copy-start.7
  12.0 0.9 %copy-done.7 = s32[3,48,128]{2,1,0:T(8,128)S(1)} copy-done((s32[3,48,128]{2,1,0:T(8,128)S(1)}, s32[3,48,128]{2,1,0:T(8,128)}, u32[]{:S(2)}) %copy-start.7) | copy-done | bytes 73752
  12.9 0.0 copy-start.1
  12.9 3.9 %shard_map.163 = (bf16[6,256,256]{2,1,0:T(8,128)(2,1)S(1)}, f32[256,128]{1,0:T(8,128)S(1)}, f32[256,256]{1,0:T(8,128)S(1)}, bf16[4,256,256]{2,1,0:T(8,128)(2,1)S(1)}, bf16[4,256,256]{2,1,0:T(8,128)(2,1)S(1)}) custom-call(f32[1,256]{1,0:T(1,128)S(1)} %bitcast.5, bf16[6,256,256]{2,1,0:T(8,128)(2,1)S(1)} %copy-done, s32[3,48,128]{2,1,0:T(8,128)S(1)} %copy-done.7), custom_call_target="tpu_custom_call" | custom-call | flops 8000000000 | bytes 2000000 | tf_op jit(solution)/shard_map/pallas_call | solution.py:345
  16.8 0.0 all-to-all-done.far_ref
  16.8 0.0 copy-done.1
  16.9 6.1 %shard_map.164 = (bf16[256,256]{1,0:T(8,128)(2,1)S(1)}, f32[256,256]{1,0:T(8,128)S(1)}, f32[8,72,256]{2,1,0:T(8,128)S(1)}, bf16[8,72,256]{2,1,0:T(8,128)(2,1)S(1)}) custom-call(bf16[16,4,256]{2,1,0:T(4,128)(2,1)S(1)} %all-to-all-done.far_ref, f32[1,256]{1,0:T(1,128)S(1)} %bitcast.6, bf16[6,256,256]{2,1,0:T(8,128)(2,1)S(1)} %copy-done.1, ...), custom_call_target="tpu_custom_call" | custom-call | tf_op jit(solution)/shard_map/pallas_call | solution.py:352
  23.0 0.2 collective-permute-start
  23.2 0.9 %shard_map.165 = (bf16[256,256]{1,0:T(8,128)(2,1)}, f32[256,256]{1,0:T(8,128)S(1)}) custom-call(bf16[6,256,256]{2,1,0:T(8,128)(2,1)S(1)} %copy-done.1, f32[1,256]{1,0:T(1,128)S(1)} %bitcast.7, f32[256,256]{1,0:T(8,128)S(1)} %get-tuple-element.36.near_ref, bf16[256,256]{1,0:T(8,128)(2,1)S(1)} %get-tuple-element.37.att_ref), custom_call_target="tpu_custom_call" | custom-call | flops 8000000000 | bytes 2000000 | tf_op jit(solution)/shard_map/pallas_call | solution.py:365
  24.1 0.6 %collective-permute-done.got_ref = bf16[8,72,256]{2,1,0:T(8,128)(2,1)S(1)} collective-permute-done((bf16[8,72,256]{2,1,0:T(8,128)(2,1)S(1)}, bf16[8,72,256]{2,1,0:T(8,128)(2,1)S(1)}, u32[]{:S(2)}, u32[]{:S(2)}) %collective-permute-start) | collective-permute-done | bytes 294944 | tf_op jit(solution)/shard_map/ppermute | solution.py:364
  24.6 0.1 shard_map.166
  24.7 14.1 %all_to_all.15.got_ref = bf16[8,72,256]{2,1,0:T(8,128)(2,1)S(1)} all-to-all(bf16[8,72,256]{2,1,0:T(8,128)(2,1)S(1)} %shard_map.166), channel_id=1, replica_groups={{0,2,4,6,8,10,12,14},{1,3,5,7,9,11,13,15},{16,18,20,22,24,26,28,30},{17..., dimensions={0} | all-to-all | bytes 589824 | tf_op jit(solution)/shard_map/all_to_all | solution.py:329
  38.8 0.0 copy-start.6
  38.8 11.3 %all_to_all.16.mine_ref = bf16[8,64,256]{2,1,0:T(8,128)(2,1)S(1)} all-to-all(bf16[8,64,256]{2,1,0:T(8,128)(2,1)S(1)} %shard_map.168), channel_id=1, replica_groups={{0,2,4,6,8,10,12,14},{1,3,5,7,9,11,13,15},{16,18,20,22,24,26,28,30},{17..., dimensions={0} | all-to-all | bytes 524288 | tf_op jit(solution)/shard_map/all_to_all | solution.py:329
  50.1 0.0 copy-start.2
  50.2 0.0 copy-start.3
  50.2 0.0 copy-start.4
  50.2 2.6 %collective-permute-start.1 = (bf16[8,64,256]{2,1,0:T(8,128)(2,1)S(1)}, bf16[8,64,256]{2,1,0:T(8,128)(2,1)S(1)}, u32[]{:S(2)}, u32[]{:S(2)}) collective-permute-start(bf16[8,64,256]{2,1,0:T(8,128)(2,1)S(1)} %all_to_all.16.mine_ref), channel_id=1, source_target_pairs={{0,1},{1,0},{2,3},{3,2},{4,5},{5,4},{6,7},{7,6},{8,9},{9,8},{10,11... | collective-permute-start | bytes 786440 | tf_op jit(solution)/shard_map/ppermute | solution.py:377
  52.8 0.0 copy-done.6
  52.8 1.5 %shard_map.167 = f32[256,256]{1,0:T(8,128)} custom-call(s32[4,16]{1,0:T(4,128)S(1)} %bitcast.10, bf16[8,72,256]{2,1,0:T(8,128)(2,1)S(1)} %all_to_all.15.got_ref, f32[256,256]{1,0:T(8,128)S(1)} %get-tuple-element.43.own_ref), custom_call_target="tpu_custom_call" | custom-call | flops 8000000000 | bytes 2000000 | tf_op jit(solution)/shard_map/pallas_call | solution.py:378
  54.3 0.0 collective-permute-done.1.other_ref
  54.3 0.0 copy-done.2
  54.3 0.0 copy-done.3
  54.3 0.0 copy-done.4
  54.3 1.1 %shard_map.169 = (f32[256,256]{1,0:T(8,128)}, f32[256,256]{1,0:T(8,128)}, f32[256,256]{1,0:T(8,128)}, f32[256,256]{1,0:T(8,128)}, f32[1,256]{1,0:T(1,128)}) custom-call(bf16[8,64,256]{2,1,0:T(8,128)(2,1)S(1)} %all_to_all.16.mine_ref, bf16[8,64,256]{2,1,0:T(8,128)(2,1)S(1)} %collective-permute-done.1.other_ref, f32[1,256]{1,0:T(1,128)S(1)} %bitcast.8, ...), custom_call_target="tpu_custom_call" | custom-call | tf_op jit(solution)/shard_map/pallas_call | solution.py:381
  (1 shorter events, 0.0 us)
Async XLA Ops:
  2.8 14.0 %all-to-all-start = ((bf16[16,4,256]{2,1,0:T(4,128)(2,1)}), bf16[16,4,256]{2,1,0:T(4,128)(2,1)S(1)}, u32[]{:S(2)}, u32[]{:S(2)}) async-start(bf16[16,4,256]{2,1,0:T(4,128)(2,1)} %get-tuple-element.29), calls=%async_computation | async-start | bytes 65536 | tf_op jit(solution)/shard_map/all_to_all | solution.py:343
  10.2 0.7 %copy-start.5 = (f32[256]{0:T(256)S(1)}, f32[256]{0:T(256)}, u32[]{:S(2)}) copy-start(f32[256]{0:T(256)} %param.12) | copy-start | bytes 3076
  10.9 1.1 %copy-start = (bf16[6,256,256]{2,1,0:T(8,128)(2,1)S(1)}, bf16[6,256,256]{2,1,0:T(8,128)(2,1)}, u32[]{:S(2)}) copy-start(bf16[6,256,256]{2,1,0:T(8,128)(2,1)} %get-tuple-element.28.square_ref) | copy-start | bytes 2359300
  12.0 0.9 %copy-start.7 = (s32[3,48,128]{2,1,0:T(8,128)S(1)}, s32[3,48,128]{2,1,0:T(8,128)}, u32[]{:S(2)}) copy-start(s32[3,48,128]{2,1,0:T(8,128)} %get-tuple-element.30.edge_ref) | copy-start | bytes 221188
  12.9 3.9 %copy-start.1 = (bf16[6,256,256]{2,1,0:T(8,128)(2,1)S(1)}, bf16[6,256,256]{2,1,0:T(8,128)(2,1)}, u32[]{:S(2)}) copy-start(bf16[6,256,256]{2,1,0:T(8,128)(2,1)} %get-tuple-element.28.square_ref) | copy-start | bytes 2359300
  23.0 1.6 %collective-permute-start = (bf16[8,72,256]{2,1,0:T(8,128)(2,1)S(1)}, bf16[8,72,256]{2,1,0:T(8,128)(2,1)S(1)}, u32[]{:S(2)}, u32[]{:S(2)}) collective-permute-start(bf16[8,72,256]{2,1,0:T(8,128)(2,1)S(1)} %get-tuple-element.40), channel_id=1, source_target_pairs={{0,1},{1,0},{2,3},{3,2},{4,5},{5,4},{6,7},{7,6},{8,9},{9,8},{10,11... | collective-permute-start | bytes 884744 | tf_op jit(solution)/shard_map/ppermute | solution.py:364
  38.8 13.9 %copy-start.6 = (s32[1,16,4]{1,2,0:T(4,128)S(1)}, s32[1,16,4]{1,2,0:T(4,128)}, u32[]{:S(2)}) copy-start(s32[1,16,4]{1,2,0:T(4,128)} %param.21) | copy-start | bytes 772
  50.1 4.2 %copy-start.2 = (bf16[256,256]{1,0:T(8,128)(2,1)S(1)}, bf16[256,256]{1,0:T(8,128)(2,1)}, u32[]{:S(2)}) copy-start(bf16[256,256]{1,0:T(8,128)(2,1)} %wq_ref.1) | copy-start | bytes 393220
  50.2 4.2 %copy-start.3 = (bf16[256,256]{1,0:T(8,128)(2,1)S(1)}, bf16[256,256]{1,0:T(8,128)(2,1)}, u32[]{:S(2)}) copy-start(bf16[256,256]{1,0:T(8,128)(2,1)} %wk_ref.1) | copy-start | bytes 393220
  50.2 4.2 %copy-start.4 = (bf16[256,256]{1,0:T(8,128)(2,1)S(1)}, bf16[256,256]{1,0:T(8,128)(2,1)}, u32[]{:S(2)}) copy-start(bf16[256,256]{1,0:T(8,128)(2,1)} %wv_ref.1) | copy-start | bytes 393220
  50.2 4.1 %collective-permute-start.1 = (bf16[8,64,256]{2,1,0:T(8,128)(2,1)S(1)}, bf16[8,64,256]{2,1,0:T(8,128)(2,1)S(1)}, u32[]{:S(2)}, u32[]{:S(2)}) collective-permute-start(bf16[8,64,256]{2,1,0:T(8,128)(2,1)S(1)} %all_to_all.16.mine_ref), channel_id=1, source_target_pairs={{0,1},{1,0},{2,3},{3,2},{4,5},{5,4},{6,7},{7,6},{8,9},{9,8},{10,11... | collective-permute-start | bytes 786440 | tf_op jit(solution)/shard_map/ppermute | solution.py:377

commit v4 on v3

--- a/solution.py
+++ b/solution.py
@@ -61,20 +61,47 @@
 
 def pick_kernel(send_hbm, *refs):
     squares = refs[:6]
-    edges = refs[6:9]
-    out_ref, square_ref, edge_ref, send, wide, sems = refs[9:]
+    small = refs[6:10]
+    out_ref, pack_ref, send, wide, dst_ref, src_ref, mask_ref, gain_ref, sems = refs[10:]
     copies = begin(
-        (send_hbm,) + squares + edges,
-        [send] + [square_ref.at[i] for i in range(6)] + [edge_ref.at[i] for i in range(3)],
+        (send_hbm,) + squares + small,
+        [send] + [pack_ref.at[i] for i in range(6)] + [dst_ref, src_ref, mask_ref, gain_ref],
         sems,
     )
     finish_all(copies[:2])
     slots, peers = send.shape
-    wide[...] = square_ref[0].astype(F32)
+    rows, feats = wide.shape
+    wide[...] = pack_ref[0].astype(F32)
     for peer in range(peers):
-        rows = [wide[pl.ds(send[slot, peer], 1), :] for slot in range(slots)]
-        out_ref[peer] = jnp.concatenate(rows, axis=0).astype(BF16)
-    finish_all(copies[2:])
+        picked = [wide[pl.ds(send[slot, peer], 1), :] for slot in range(slots)]
+        out_ref[peer] = jnp.concatenate(picked, axis=0).astype(BF16)
+    finish_all(copies[7:])
+    src = jnp.where(mask_ref[...] > 0, src_ref[...], -1)
+    parts = [dst_ref[...].astype(F32)]
+    for base in range(0, rows + up(slots * peers, 128), rows):
+        inside = (src >= base) & (src < base + rows)
+        parts.append(jnp.where(inside, src - base, -1).astype(F32))
+    if len(parts) % 2:
+        parts.append(parts[0])
+    tall = [jnp.concatenate(parts[i : i + 2], axis=1) for i in range(0, len(parts), 2)]
+    gain = gain_ref[...]
+    first = gain.astype(BF16).astype(F32)
+    second = (gain - first).astype(BF16).astype(F32)
+    gains = [first, second, gain - first - second]
+    used = sum(t.shape[0] for t in tall)
+    blank = jnp.zeros((rows - used - 3, feats), F32)
+    pack_ref[6] = jnp.concatenate(tall + gains + [blank], axis=0).astype(BF16)
+    finish_all(copies[2:7])
+
+
+def gain_row(edge_rows, rows, width):
+    tables = 1 + -(-(rows + width) // rows)
+    return up(tables, 2) // 2 * edge_rows
+
+
+def packed_gain(pack_ref, at):
+    parts = pack_ref[6].astype(F32)[at : at + 3]
+    return parts[0:1] + parts[1:2] + parts[2:3]
 
 
 def head_hots(feats):
@@ -90,21 +117,23 @@
     return w.astype(BF16), (w * (1.0 - t * t) * (1.0 / math.sqrt(head))).astype(BF16)
 
 
-def local_kernel(gain_ref, square_ref, edge_ref, low_ref, far_count, near_count, w_ref, g_ref):
-    x_ref, wq_ref, wk_ref, wv_ref, wo_ref, cot_ref = [square_ref.at[i] for i in range(6)]
+def local_kernel(edge_rows, pack_ref, low_ref, far_count, near_count, w_ref, g_ref):
+    x_ref, wq_ref, wk_ref, wv_ref, wo_ref, cot_ref = [pack_ref.at[i] for i in range(6)]
+    rows, width = far_count.shape
+    gain = packed_gain(pack_ref, gain_row(edge_rows, rows, width))
     queries, keys = local_project(
-        x_ref, gain_ref, wq_ref, wk_ref, wv_ref, wo_ref, cot_ref, low_ref
+        x_ref, gain, wq_ref, wk_ref, wv_ref, wo_ref, cot_ref, low_ref
     )
-    rows, feats = queries.shape
-    local_count(edge_ref.at[0], edge_ref.at[1], edge_ref.at[2], far_count, near_count)
+    feats = queries.shape[1]
+    local_count(edge_rows, pack_ref, far_count, near_count)
     _, hots = head_hots(feats)
     for h in range(EARLY):
         w_ref[h], g_ref[h] = weigh(queries * hots[h], keys, near_count[...], feats // HEADS)
 
 
-def local_project(x_ref, gain_ref, wq_ref, wk_ref, wv_ref, wo_ref, cot_ref, low_ref):
+def local_project(x_ref, gain, wq_ref, wk_ref, wv_ref, wo_ref, cot_ref, low_ref):
     xhat, _ = standardize(x_ref[...].astype(F32))
-    normed = (xhat * gain_ref[...]).astype(BF16)
+    normed = (xhat * gain).astype(BF16)
     queries = dot(normed, wq_ref[...]).astype(BF16)
     keys = dot(normed, wk_ref[...]).astype(BF16)
     low_ref[0] = queries
@@ -116,41 +145,46 @@
     return queries, keys
 
 
-def local_count(dst_ref, src_ref, mask_ref, far_count, near_count):
+def local_count(edge_rows, pack_ref, far_count, near_count):
     rows, far = far_count.shape
+    edge = 128
+    group = 8
+    table = pack_ref[6].astype(F32)
+
+    def part(i):
+        at = i // 2 * edge_rows
+        return table[at : at + edge_rows, i % 2 * edge : (i % 2 + 1) * edge]
+
+    ids = lax.broadcasted_iota(jnp.int32, (rows, edge), 0).astype(F32)
+
+    def hot(values, height, base):
+        at = ids[:height]
+        return jnp.concatenate(
+            [(at == values[j : j + 1]).astype(F32).astype(BF16) for j in range(base, base + group)],
+            axis=1,
+        )
+
     row_id = lax.broadcasted_iota(jnp.int32, (rows, rows), 0)
     col_id = lax.broadcasted_iota(jnp.int32, (rows, rows), 1)
-    near_count[...] = (row_id == col_id).astype(F32)
-    far_count[...] = jnp.zeros((rows, far), F32)
-    group = 8
-    edge = 128
-    dst_id = lax.broadcasted_iota(jnp.int32, (rows, edge), 0)
-    src_id = lax.broadcasted_iota(jnp.int32, (rows + far, edge), 0)
-
-    def step(i, carry):
-        base = pl.multiple_of(i * group, group)
-        dst = dst_ref[pl.ds(base, group), :]
-        src = jnp.where(mask_ref[pl.ds(base, group), :] > 0, src_ref[pl.ds(base, group), :], -1)
-        hot_dst = jnp.concatenate(
-            [(dst_id == dst[j : j + 1]).astype(F32).astype(BF16) for j in range(group)], axis=1
-        )
-        hot_src = jnp.concatenate(
-            [(src_id == src[j : j + 1]).astype(F32).astype(BF16) for j in range(group)], axis=1
-        )
-        part = dot_t(hot_dst, hot_src)
-        near_count[...] += part[:, :rows]
-        far_count[...] += part[:, rows:]
-        return carry
-
-    lax.fori_loop(0, dst_ref.shape[0] // group, step, 0)
+    spans = [(b, min(rows, rows + far - b)) for b in range(0, rows + far, rows)]
+    totals = [jnp.zeros((rows, height), F32) for _, height in spans]
+    totals[0] = (row_id == col_id).astype(F32)
+    values = [part(i) for i in range(len(spans) + 1)]
+    for base in range(0, edge_rows, group):
+        hot_dst = hot(values[0], rows, base)
+        for i, (_, height) in enumerate(spans):
+            totals[i] = totals[i] + dot_t(hot_dst, hot(values[i + 1], height, base))
+    near_count[...] = totals[0]
+    for (b, height), total in zip(spans[1:], totals[1:]):
+        far_count[:, b - rows : b - rows + height] = total
 
 
 def attend_kernel(
-    far_ref, gain_ref, square_ref, low_ref, far_count, near_count, near_w, near_g,
+    edge_rows, far_ref, pack_ref, low_ref, far_count, near_count, near_w, near_g,
     att_ref, near_ref, keep_ref, give_ref,
     w_scr, g_scr, dkt_scr, dvt_scr, grad_scr,
 ):
-    _, wq_ref, wk_ref, wv_ref, _, cot_ref = [square_ref.at[i] for i in range(6)]
+    _, wq_ref, wk_ref, wv_ref, _, cot_ref = [pack_ref.at[i] for i in range(6)]
     _, rows, feats = low_ref.shape
     q_ref, k_ref, v_ref, qt_ref, normt_ref, datt_ref = [low_ref.at[i] for i in range(6)]
     peers, slots, _ = far_ref.shape
@@ -162,7 +196,7 @@
     far_x = jnp.concatenate([far_ref[p].astype(F32) for p in range(peers)], axis=0)
     if pad:
         far_x = jnp.concatenate([far_x, jnp.zeros((pad, feats), F32)], axis=0)
-    gain = gain_ref[...]
+    gain = packed_gain(pack_ref, gain_row(edge_rows, rows, width))
     far_hat, far_rstd = standardize(far_x)
     far_normed = (far_hat * gain).astype(BF16)
     far_keys = dot(far_normed, wk_ref[...]).astype(BF16)
@@ -257,10 +291,11 @@
     share_ref[...] = jnp.broadcast_to(total.astype(BF16)[None], share_ref.shape)
 
 
-def own_kernel(square_ref, gain_ref, near_ref, att_ref, out_ref, feats_ref):
+def own_kernel(gain_at, square_ref, near_ref, att_ref, out_ref, feats_ref):
     x = square_ref[0].astype(F32)
     out_ref[...] = (x + dot(att_ref[...], square_ref[4])).astype(BF16)
-    dx = pull(near_ref[...] * gain_ref[...], *standardize(x))
+    gain = packed_gain(square_ref, gain_at)
+    dx = pull(near_ref[...] * gain, *standardize(x))
     feats_ref[...] = square_ref[5].astype(F32) + dx
 
 
@@ -331,28 +366,30 @@
     cost = pl.CostEstimate(flops=8_000_000_000, bytes_accessed=2_000_000, transcendentals=0)
     square = like((rows, feats), BF16)
     wide = like((rows, feats), F32)
-    picked, squares, edges = call(
+    edges = edge_dst.shape
+    ints = pltpu.VMEM(edges, jnp.int32)
+    picked, pack = call(
         pick_kernel,
-        (like((peers, slots, feats), BF16), like((6, rows, feats), BF16),
-         like((3,) + edge_dst.shape, jnp.int32)),
-        [HBM] * 10,
-        (pltpu.SMEM((slots, peers), jnp.int32), pltpu.VMEM((rows, feats), F32),
-         pltpu.SemaphoreType.DMA((10,))),
+        (like((peers, slots, feats), BF16), like((7, rows, feats), BF16)),
+        [HBM] * 11,
+        (pltpu.SMEM((slots, peers), jnp.int32), pltpu.VMEM((rows, feats), F32), ints, ints, ints,
+         pltpu.VMEM((1, feats), F32), pltpu.SemaphoreType.DMA((11,))),
         mib=FULL,
-    )(send, node_feats, w_query, w_key, w_value, w_out, cotangent, edge_dst, edge_src, edge_mask)
+    )(send, node_feats, w_query, w_key, w_value, w_out, cotangent, edge_dst, edge_src, edge_mask,
+      gain)
     arrived = lax.all_to_all(picked, "nodes", split_axis=0, concat_axis=0, tiled=True)
     heads = like((EARLY, rows, rows), BF16)
     low, far_count, near_count, w, g = call(
-        local_kernel,
+        functools.partial(local_kernel, edges[0]),
         (like((6, rows, feats), BF16), like((rows, width), F32), like((rows, rows), F32),
          heads, heads),
-        [VMEM] * 3,
+        [VMEM],
         cost=cost,
-    )(gain, squares, edges)
+    )(pack)
     att, near, keep, give = call(
-        attend_kernel,
+        functools.partial(attend_kernel, edges[0]),
         (square, wide, like((chips, block, feats), F32), like((chips, block, feats), BF16)),
-        [VMEM] * 8,
+        [VMEM] * 7,
         [
             pltpu.VMEM((HEADS, rows, rows + width), BF16),
             pltpu.VMEM((HEADS, rows, rows + width), BF16),
@@ -360,11 +397,14 @@
             pltpu.VMEM((feats, rows + width), F32),
             pltpu.VMEM((4 * feats, feats), F32),
         ],
-    )(arrived, gain, squares, low, far_count, near_count, w, g)
+    )(arrived, pack, low, far_count, near_count, w, g)
     given = lax.ppermute(give, "nodes", swap)
-    output, own = call(own_kernel, (square, wide), [VMEM] * 4, cost=cost)(
-        squares, gain, near, att
-    )
+    output, own = call(
+        functools.partial(own_kernel, gain_row(edges[0], rows, width)),
+        (square, wide),
+        [VMEM] * 3,
+        cost=cost,
+    )(pack, near, att)
     given, own = lax.optimization_barrier((given, own))
     paired = call(
         functools.partial(pair_kernel, share, slots),

time: 55.8 us -> 52.8 us (0.946)
  blocking collectives: 25.4 us -> 22.6 us
  waiting for transfers between devices: 0.56 us -> 2.62 us
  local copies, waits for them, and re-layouts: 2.71 us -> 1.2 us
  Pallas kernels: 15.9 us -> 14.4 us
  starting transfers between devices: 10.2 us -> 10.9 us
    all_to_all x2, blocking collectives: 25.4 us -> 22.6 us  [across(): return lax.all_to_all(x, 'nodes', 0, 0, axis_index_groups=sides, tiled=True)]
    all_to_all x1, waiting for transfers between devices: 0.01 us -> 2.3 us  [on_device(): lax.all_to_all(picked, 'nodes', split_axis=0, concat_axis=0, tiled=True)]
    unnamed x16 -> x14, local copies, waits for them, and re-layouts: 2.71 us -> 1.2 us
    pallas_call x4, Pallas kernels: 13.1 us -> 11.7 us  [the longest x1 6.14 us: on_device(): call(functools.partial(attend_kernel, edges[0]), (square, wide, like((chi...]
    ppermute x1, starting transfers between devices: 0.2 us -> 0.88 us  [on_device(): given = lax.ppermute(give, 'nodes', swap)]
  transfers between devices with their start and end apart: 3 -> 3, of which waited for: 1 -> 2; matrix products, arithmetic and copies ran while one was open for 0% -> 0% of each run, Pallas kernels for 11% -> 9%
where the time goes in v4:
time: 52.8 us; the launch traced here: 52.5 us
  blocking collectives  22.6 us (43%)
  Pallas kernels  14.4 us (27%)
  starting transfers between devices  10.9 us (21%)
  waiting for transfers between devices  2.62 us (5%)
  local copies, waits for them, and re-layouts  1.2 us (2%)
  between operations  0.7 us (1%)
    all_to_all x2, blocking collectives, across(): return lax.all_to_all(x, 'nodes', 0, 0, axis_index_groups=sides, tiled=True)  22.6 us
    all_to_all x1, starting transfers between devices, on_device(): lax.all_to_all(picked, 'nodes', split_axis=0, concat_axis=0, tiled=True)  7.36 us
    pallas_call x1, Pallas kernels, on_device(): call(functools.partial(attend_kernel, edges[0]), (square, wide, like((chi...  6.14 us
    ppermute x1, starting transfers between devices, on_device(): other = lax.ppermute(mine, 'nodes', swap)  2.66 us
    pallas_call x1, Pallas kernels, on_device(): call(functools.partial(local_kernel, edges[0]), (like((6, rows, feats), B...  2.42 us
    all_to_all x1, waiting for transfers between devices, on_device(): lax.all_to_all(picked, 'nodes', split_axis=0, concat_axis=0, tiled=True)  2.3 us
    pallas_call x1, Pallas kernels, on_device(): call(pick_kernel, (like((peers, slots, feats), BF16), like((7, rows, feat...  2.24 us
    pallas_call x1, Pallas kernels, on_device(): call(functools.partial(finish_kernel, share), wide, [SMEM] + [VMEM] * 2,...  1.54 us
  transfers between devices with their start and end apart: 3, of which 2 were waited for; matrix products, arithmetic and copies ran while one was open for 0% of the time, Pallas kernels for 9%

profile of v4, /device:TPU:1, one launch (start us, length us, event | category | flops | bytes accessed | tf_op | source)
XLA Modules:
  0.0 52.5 jit_solution(268657206535309533)
XLA Ops:
  0.6 2.2 %shard_map.162 = (bf16[16,4,256]{2,1,0:T(4,128)(2,1)}, bf16[7,256,256]{2,1,0:T(8,128)(2,1)}) custom-call(s32[4,16]{1,0:T(4,128)} %bitcast.7, bf16[256,256]{1,0:T(8,128)(2,1)} %refs_0_.1, bf16[256,256]{1,0:T(8,128)(2,1)} %wq_ref.1, bf16[256,256]{1,0:T(8,128)(2,1)} %wk_ref.1, bf16[256,256]{1,0:T(8,128)(2,1)} %wv_ref.1, bf16[256,256]{1,0:T(8,128)(2,1)} %refs_4_.1, ...), custom_call_target="tpu_custom_call" | custom-call | tf_op jit(solution)/shard_map/pallas_call | solution.py:371
  2.9 7.4 %all-to-all-start = ((bf16[16,4,256]{2,1,0:T(4,128)(2,1)}), bf16[16,4,256]{2,1,0:T(4,128)(2,1)S(1)}, u32[]{:S(2)}, u32[]{:S(2)}) async-start(bf16[16,4,256]{2,1,0:T(4,128)(2,1)} %get-tuple-element.28), calls=%async_computation | async-start | bytes 65536 | tf_op jit(solution)/shard_map/all_to_all | solution.py:380
  10.2 0.0 copy-start
  10.2 1.2 %copy-done = bf16[7,256,256]{2,1,0:T(8,128)(2,1)S(1)} copy-done((bf16[7,256,256]{2,1,0:T(8,128)(2,1)S(1)}, bf16[7,256,256]{2,1,0:T(8,128)(2,1)}, u32[]{:S(2)}) %copy-start) | copy-done | bytes 917528
  11.4 0.0 copy-start.1
  11.4 2.4 %shard_map.163 = (bf16[6,256,256]{2,1,0:T(8,128)(2,1)S(1)}, f32[256,128]{1,0:T(8,128)S(1)}, f32[256,256]{1,0:T(8,128)S(1)}, bf16[4,256,256]{2,1,0:T(8,128)(2,1)S(1)}, bf16[4,256,256]{2,1,0:T(8,128)(2,1)S(1)}) custom-call(bf16[7,256,256]{2,1,0:T(8,128)(2,1)S(1)} %copy-done), custom_call_target="tpu_custom_call" | custom-call | flops 8000000000 | bytes 2000000 | tf_op jit(solution)/shard_map/pallas_call | solution.py:382
  13.9 2.3 %all-to-all-done.far_ref = bf16[16,4,256]{2,1,0:T(4,128)(2,1)S(1)} async-done(((bf16[16,4,256]{2,1,0:T(4,128)(2,1)}), bf16[16,4,256]{2,1,0:T(4,128)(2,1)S(1)}, u32[]{:S(2)}, u32[]{:S(2)}) %all-to-all-start) | async-done | bytes 32800 | tf_op jit(solution)/shard_map/all_to_all | solution.py:380
  16.2 0.0 copy-done.1
  16.2 6.1 %shard_map.164 = (bf16[256,256]{1,0:T(8,128)(2,1)S(1)}, f32[256,256]{1,0:T(8,128)S(1)}, f32[8,72,256]{2,1,0:T(8,128)S(1)}, bf16[8,72,256]{2,1,0:T(8,128)(2,1)S(1)}) custom-call(bf16[16,4,256]{2,1,0:T(4,128)(2,1)S(1)} %all-to-all-done.far_ref, bf16[7,256,256]{2,1,0:T(8,128)(2,1)S(1)} %copy-done.1, bf16[6,256,256]{2,1,0:T(8,128)(2,1)S(1)} %get-tuple-element.29.low_ref, ...), custom_call_target="tpu_custom_call" | custom-call | tf_op jit(solution)/shard_map/pallas_call | solution.py:389
  22.3 0.9 %collective-permute-start = (bf16[8,72,256]{2,1,0:T(8,128)(2,1)S(1)}, bf16[8,72,256]{2,1,0:T(8,128)(2,1)S(1)}, u32[]{:S(2)}, u32[]{:S(2)}) collective-permute-start(bf16[8,72,256]{2,1,0:T(8,128)(2,1)S(1)} %get-tuple-element.38), channel_id=1, source_target_pairs={{0,1},{1,0},{2,3},{3,2},{4,5},{5,4},{6,7},{7,6},{8,9},{9,8},{10,11... | collective-permute-start | bytes 884744 | tf_op jit(solution)/shard_map/ppermute | solution.py:401
  23.2 0.9 %shard_map.165 = (bf16[256,256]{1,0:T(8,128)(2,1)}, f32[256,256]{1,0:T(8,128)S(1)}) custom-call(bf16[7,256,256]{2,1,0:T(8,128)(2,1)S(1)} %copy-done.1, f32[256,256]{1,0:T(8,128)S(1)} %get-tuple-element.34.near_ref, bf16[256,256]{1,0:T(8,128)(2,1)S(1)} %get-tuple-element.35.att_ref), custom_call_target="tpu_custom_call" | custom-call | flops 8000000000 | bytes 2000000 | tf_op jit(solution)/shard_map/pallas_call | solution.py:402
  24.1 0.3 collective-permute-done.got_ref
  24.4 0.1 shard_map.166
  24.4 11.3 %all_to_all.15.got_ref = bf16[8,72,256]{2,1,0:T(8,128)(2,1)S(1)} all-to-all(bf16[8,72,256]{2,1,0:T(8,128)(2,1)S(1)} %shard_map.166), channel_id=1, replica_groups={{0,2,4,6,8,10,12,14},{1,3,5,7,9,11,13,15},{16,18,20,22,24,26,28,30},{17..., dimensions={0} | all-to-all | bytes 589824 | tf_op jit(solution)/shard_map/all_to_all | solution.py:364
  35.8 0.0 copy-start.6
  35.8 11.3 %all_to_all.16.mine_ref = bf16[8,64,256]{2,1,0:T(8,128)(2,1)S(1)} all-to-all(bf16[8,64,256]{2,1,0:T(8,128)(2,1)S(1)} %shard_map.168), channel_id=1, replica_groups={{0,2,4,6,8,10,12,14},{1,3,5,7,9,11,13,15},{16,18,20,22,24,26,28,30},{17..., dimensions={0} | all-to-all | bytes 524288 | tf_op jit(solution)/shard_map/all_to_all | solution.py:364
  47.1 0.0 copy-start.2
  47.1 0.0 copy-start.3
  47.1 0.0 copy-start.4
  47.1 0.0 copy-start.5
  47.2 2.7 %collective-permute-start.1 = (bf16[8,64,256]{2,1,0:T(8,128)(2,1)S(1)}, bf16[8,64,256]{2,1,0:T(8,128)(2,1)S(1)}, u32[]{:S(2)}, u32[]{:S(2)}) collective-permute-start(bf16[8,64,256]{2,1,0:T(8,128)(2,1)S(1)} %all_to_all.16.mine_ref), channel_id=1, source_target_pairs={{0,1},{1,0},{2,3},{3,2},{4,5},{5,4},{6,7},{7,6},{8,9},{9,8},{10,11... | collective-permute-start | bytes 786440 | tf_op jit(solution)/shard_map/ppermute | solution.py:417
  49.8 0.0 copy-done.6
  49.8 1.5 %shard_map.167 = f32[256,256]{1,0:T(8,128)} custom-call(s32[4,16]{1,0:T(4,128)S(1)} %bitcast.8, bf16[8,72,256]{2,1,0:T(8,128)(2,1)S(1)} %all_to_all.15.got_ref, f32[256,256]{1,0:T(8,128)S(1)} %get-tuple-element.41.own_ref), custom_call_target="tpu_custom_call" | custom-call | flops 8000000000 | bytes 2000000 | tf_op jit(solution)/shard_map/pallas_call | solution.py:418
  51.4 0.0 collective-permute-done.1.other_ref
  51.4 0.0 copy-done.2
  51.4 0.0 copy-done.3
  51.4 0.0 copy-done.4
  51.4 0.0 copy-done.5
  51.4 1.1 %shard_map.169 = (f32[256,256]{1,0:T(8,128)}, f32[256,256]{1,0:T(8,128)}, f32[256,256]{1,0:T(8,128)}, f32[256,256]{1,0:T(8,128)}, f32[1,256]{1,0:T(1,128)}) custom-call(bf16[8,64,256]{2,1,0:T(8,128)(2,1)S(1)} %all_to_all.16.mine_ref, bf16[8,64,256]{2,1,0:T(8,128)(2,1)S(1)} %collective-permute-done.1.other_ref, f32[1,256]{1,0:T(1,128)S(1)} %bitcast.6, ...), custom_call_target="tpu_custom_call" | custom-call | tf_op jit(solution)/shard_map/pallas_call | solution.py:421
  (1 shorter events, 0.0 us)
Async XLA Ops:
  2.9 13.3 %all-to-all-start = ((bf16[16,4,256]{2,1,0:T(4,128)(2,1)}), bf16[16,4,256]{2,1,0:T(4,128)(2,1)S(1)}, u32[]{:S(2)}, u32[]{:S(2)}) async-start(bf16[16,4,256]{2,1,0:T(4,128)(2,1)} %get-tuple-element.28), calls=%async_computation | async-start | bytes 65536 | tf_op jit(solution)/shard_map/all_to_all | solution.py:380
  10.2 1.2 %copy-start = (bf16[7,256,256]{2,1,0:T(8,128)(2,1)S(1)}, bf16[7,256,256]{2,1,0:T(8,128)(2,1)}, u32[]{:S(2)}) copy-start(bf16[7,256,256]{2,1,0:T(8,128)(2,1)} %get-tuple-element.27.pack_ref.square_ref) | copy-start | bytes 2752516
  11.4 4.7 %copy-start.1 = (bf16[7,256,256]{2,1,0:T(8,128)(2,1)S(1)}, bf16[7,256,256]{2,1,0:T(8,128)(2,1)}, u32[]{:S(2)}) copy-start(bf16[7,256,256]{2,1,0:T(8,128)(2,1)} %get-tuple-element.27.pack_ref.square_ref) | copy-start | bytes 2752516
  22.3 2.1 %collective-permute-start = (bf16[8,72,256]{2,1,0:T(8,128)(2,1)S(1)}, bf16[8,72,256]{2,1,0:T(8,128)(2,1)S(1)}, u32[]{:S(2)}, u32[]{:S(2)}) collective-permute-start(bf16[8,72,256]{2,1,0:T(8,128)(2,1)S(1)} %get-tuple-element.38), channel_id=1, source_target_pairs={{0,1},{1,0},{2,3},{3,2},{4,5},{5,4},{6,7},{7,6},{8,9},{9,8},{10,11... | collective-permute-start | bytes 884744 | tf_op jit(solution)/shard_map/ppermute | solution.py:401
  35.8 14.0 %copy-start.6 = (s32[1,16,4]{1,2,0:T(4,128)S(1)}, s32[1,16,4]{1,2,0:T(4,128)}, u32[]{:S(2)}) copy-start(s32[1,16,4]{1,2,0:T(4,128)} %param.21) | copy-start | bytes 772
  47.1 4.2 %copy-start.2 = (bf16[256,256]{1,0:T(8,128)(2,1)S(1)}, bf16[256,256]{1,0:T(8,128)(2,1)}, u32[]{:S(2)}) copy-start(bf16[256,256]{1,0:T(8,128)(2,1)} %wq_ref.1) | copy-start | bytes 393220
  47.1 4.2 %copy-start.3 = (bf16[256,256]{1,0:T(8,128)(2,1)S(1)}, bf16[256,256]{1,0:T(8,128)(2,1)}, u32[]{:S(2)}) copy-start(bf16[256,256]{1,0:T(8,128)(2,1)} %wk_ref.1) | copy-start | bytes 393220
  47.1 4.2 %copy-start.4 = (bf16[256,256]{1,0:T(8,128)(2,1)S(1)}, bf16[256,256]{1,0:T(8,128)(2,1)}, u32[]{:S(2)}) copy-start(bf16[256,256]{1,0:T(8,128)(2,1)} %wv_ref.1) | copy-start | bytes 393220
  47.1 4.2 %copy-start.5 = (f32[256]{0:T(256)S(1)}, f32[256]{0:T(256)}, u32[]{:S(2)}) copy-start(f32[256]{0:T(256)} %param.12) | copy-start | bytes 3076
  47.2 4.2 %collective-permute-start.1 = (bf16[8,64,256]{2,1,0:T(8,128)(2,1)S(1)}, bf16[8,64,256]{2,1,0:T(8,128)(2,1)S(1)}, u32[]{:S(2)}, u32[]{:S(2)}) collective-permute-start(bf16[8,64,256]{2,1,0:T(8,128)(2,1)S(1)} %all_to_all.16.mine_ref), channel_id=1, source_target_pairs={{0,1},{1,0},{2,3},{3,2},{4,5},{5,4},{6,7},{7,6},{8,9},{9,8},{10,11... | collective-permute-start | bytes 786440 | tf_op jit(solution)/shard_map/ppermute | solution.py:417

commit v5 on v4

--- a/solution.py
+++ b/solution.py
@@ -15,7 +15,6 @@
 BF16 = jnp.bfloat16
 VMEM = pl.BlockSpec(memory_space=pltpu.VMEM)
 SMEM = pl.BlockSpec(memory_space=pltpu.SMEM)
-HBM = pl.BlockSpec(memory_space=pltpu.HBM)
 MIB = 1024 * 1024
 FULL = 60
 
@@ -44,38 +43,17 @@
     return rstd * (g - mean_g - xhat * mean_gx)
 
 
-def begin(sources, targets, sems):
-    copies = [
-        pltpu.make_async_copy(source, target, sems.at[i])
-        for i, (source, target) in enumerate(zip(sources, targets))
-    ]
-    for copy in copies:
-        copy.start()
-    return copies
-
-
-def finish_all(copies):
-    for copy in copies:
-        copy.wait()
-
-
-def pick_kernel(send_hbm, *refs):
+def pick_kernel(send_ref, *refs):
     squares = refs[:6]
-    small = refs[6:10]
-    out_ref, pack_ref, send, wide, dst_ref, src_ref, mask_ref, gain_ref, sems = refs[10:]
-    copies = begin(
-        (send_hbm,) + squares + small,
-        [send] + [pack_ref.at[i] for i in range(6)] + [dst_ref, src_ref, mask_ref, gain_ref],
-        sems,
-    )
-    finish_all(copies[:2])
-    slots, peers = send.shape
+    dst_ref, src_ref, mask_ref, gain_ref, out_ref, pack_ref, wide = refs[6:]
+    slots, peers = send_ref.shape
     rows, feats = wide.shape
-    wide[...] = pack_ref[0].astype(F32)
+    wide[...] = squares[0][...].astype(F32)
+    for i, square in enumerate(squares):
+        pack_ref[i] = square[...]
     for peer in range(peers):
-        picked = [wide[pl.ds(send[slot, peer], 1), :] for slot in range(slots)]
+        picked = [wide[pl.ds(send_ref[slot, peer], 1), :] for slot in range(slots)]
         out_ref[peer] = jnp.concatenate(picked, axis=0).astype(BF16)
-    finish_all(copies[7:])
     src = jnp.where(mask_ref[...] > 0, src_ref[...], -1)
     parts = [dst_ref[...].astype(F32)]
     for base in range(0, rows + up(slots * peers, 128), rows):
@@ -91,7 +69,6 @@
     used = sum(t.shape[0] for t in tall)
     blank = jnp.zeros((rows - used - 3, feats), F32)
     pack_ref[6] = jnp.concatenate(tall + gains + [blank], axis=0).astype(BF16)
-    finish_all(copies[2:7])
 
 
 def gain_row(edge_rows, rows, width):
@@ -113,8 +90,8 @@
 
 def weigh(queries, keys, count, head):
     t = jnp.tanh(dot_t(queries, keys) * (0.2 / math.sqrt(head)))
-    w = count * jnp.exp(5.0 * t)
-    return w.astype(BF16), (w * (1.0 - t * t) * (1.0 / math.sqrt(head))).astype(BF16)
+    w = count * jnp.exp2(t * (5.0 / math.log(2.0)))
+    return w.astype(BF16), (w * (1.0 - t * t)).astype(BF16)
 
 
 def local_kernel(edge_rows, pack_ref, low_ref, far_count, near_count, w_ref, g_ref):
@@ -181,16 +158,17 @@
 
 def attend_kernel(
     edge_rows, far_ref, pack_ref, low_ref, far_count, near_count, near_w, near_g,
-    att_ref, near_ref, keep_ref, give_ref,
-    w_scr, g_scr, dkt_scr, dvt_scr, grad_scr,
+    tail_ref, keep_ref, give_ref,
+    w_scr, g_scr, far_w, far_g, dkt_scr, dvt_scr,
 ):
     _, wq_ref, wk_ref, wv_ref, _, cot_ref = [pack_ref.at[i] for i in range(6)]
     _, rows, feats = low_ref.shape
-    q_ref, k_ref, v_ref, qt_ref, normt_ref, datt_ref = [low_ref.at[i] for i in range(6)]
+    queries, keys, values, qt, norm_t, datt = [low_ref[i] for i in range(6)]
     peers, slots, _ = far_ref.shape
     far = peers * slots
     width = far_count.shape[1]
     head = feats // HEADS
+    pairs = HEADS // 2
     chips, block, _ = keep_ref.shape
     pad = width - far
     far_x = jnp.concatenate([far_ref[p].astype(F32) for p in range(peers)], axis=0)
@@ -201,74 +179,117 @@
     far_normed = (far_hat * gain).astype(BF16)
     far_keys = dot(far_normed, wk_ref[...]).astype(BF16)
     far_values = dot(far_normed, wv_ref[...]).astype(BF16)
-    keys = jnp.concatenate([k_ref[...], far_keys], axis=0)
-    values = jnp.concatenate([v_ref[...], far_values], axis=0)
     masks, hots = head_hots(feats)
-    queries = q_ref[...]
-    count = far_count[...]
-    both_count = jnp.concatenate([near_count[...], count], axis=1)
-    num = jnp.zeros((rows, feats), F32)
-    den = jnp.zeros((rows, feats), F32)
-    for h in range(HEADS):
-        q_head = queries * hots[h]
-        if h < EARLY:
-            w, g = weigh(q_head, far_keys, count, head)
-            w = jnp.concatenate([near_w[h], w], axis=1)
-            g = jnp.concatenate([near_g[h], g], axis=1)
-        else:
-            w, g = weigh(q_head, keys, both_count, head)
-        w_scr[h] = w
-        g_scr[h] = g
-        num = num + dot(w, values * hots[h])
-        den = den + dot(w, jnp.broadcast_to(hots[h], (rows + width, feats)))
+    lane = lax.broadcasted_iota(jnp.int32, (1, feats), 1)
+    even = lax.rem(lane // (2 * head), 2) == 0
+
+    def both(x, j):
+        return jnp.concatenate([x * hots[2 * j], x * hots[2 * j + 1]], axis=0)
+
+    def summed(h):
+        return hots[h + 2] if h // 2 % 2 == 0 else hots[h - 2]
+
+    count = jnp.concatenate([far_count[...]] * 2, axis=1)
+    near = near_count[...]
+    seen = [[], []]
+    for j in range(pairs):
+        w, far_g[j] = weigh(queries, both(far_keys, j), count, head)
+        far_w[j] = w
+        side = j % 2
+        far_ones = jnp.concatenate(
+            [jnp.broadcast_to(summed(h), (width, feats)) for h in (2 * j, 2 * j + 1)], axis=0
+        )
+        seen[side].append((w, both(far_values, j) + far_ones))
+        for h in (2 * j, 2 * j + 1):
+            if h < EARLY:
+                w = near_w[h]
+            else:
+                w, g_scr[h - EARLY] = weigh(queries * hots[h], keys, near, head)
+                w_scr[h - EARLY] = w
+            seen[side].append((w, values * hots[h] + summed(h)))
+    total = [
+        dot(
+            jnp.concatenate([w for w, _ in side], axis=1),
+            jnp.concatenate([v for _, v in side], axis=0),
+        )
+        for side in seen
+    ]
+    num = jnp.where(even, total[0], total[1])
+    crossed = jnp.where(even, total[1], total[0])
+    den = jnp.concatenate(
+        [pltpu.roll(crossed[:, i : i + 4 * head], 2 * head, 1) for i in range(0, feats, 4 * head)],
+        axis=1,
+    )
     rden = 1.0 / den
     att32 = num * rden
     att = att32.astype(BF16)
-    att_ref[...] = att
+    tail_ref[0] = att
     grad_out = dot(att.T, cot_ref[...])
-    dnum = (datt_ref[...].astype(F32) * rden).astype(BF16)
+    dnum = (datt.astype(F32) * rden).astype(BF16)
     dnum_t = dnum.T
     prod = dnum.astype(F32) * att32
-    qt = qt_ref[...]
     dq = jnp.zeros((rows, feats), F32)
+    slopes, weights, far_slopes = [], [], []
+    for j in range(pairs):
+        z = [
+            jnp.sum(jnp.where(masks[h], prod, 0.0), axis=1, keepdims=True)
+            for h in (2 * j, 2 * j + 1)
+        ]
+        far_z = jnp.concatenate([jnp.broadcast_to(x, (rows, width)) for x in z], axis=1)
+        dw = dot_t(dnum, both(far_values, j)) - far_z
+        ds = (far_g[j].astype(F32) * dw).astype(BF16)
+        dq = dq + dot(ds, both(far_keys, j))
+        far_slopes.append(ds)
+        for i, h in enumerate((2 * j, 2 * j + 1)):
+            w, g = (near_w[h], near_g[h]) if h < EARLY else (w_scr[h - EARLY], g_scr[h - EARLY])
+            dw = dot_t(dnum * hots[h], values) - z[i]
+            ds = (g.astype(F32) * dw).astype(BF16)
+            dq = dq + dot(ds, keys * hots[h])
+            slopes.append(ds)
+            weights.append(w)
     for h in range(HEADS):
-        z = jnp.sum(jnp.where(masks[h], prod, 0.0), axis=1, keepdims=True)
-        dw = dot_t(dnum * hots[h], values) - z
-        ds = (g_scr[h].astype(F32) * dw).astype(BF16)
-        dq = dq + dot(ds, keys * hots[h])
         at = slice(h * head, (h + 1) * head)
-        dkt_scr[at, :] = dot(qt[at, :], ds)
-        dvt_scr[at, :] = dot(dnum_t[at, :], w_scr[h])
-    dq = dq.astype(BF16)
-    dkt = dkt_scr[...].astype(BF16)
+        dkt_scr[at, :rows] = dot(qt[at, :], slopes[h])
+        dvt_scr[at, :rows] = dot(dnum_t[at, :], weights[h])
+    for j in range(pairs):
+        at = slice(2 * j * head, (2 * j + 2) * head)
+        dk = dot(qt[at, :], far_slopes[j])
+        dv = dot(dnum_t[at, :], far_w[j])
+        for i in range(2):
+            at = slice((2 * j + i) * head, (2 * j + i + 1) * head)
+            part = slice(i * head, (i + 1) * head)
+            cols = slice(i * width, (i + 1) * width)
+            dkt_scr[at, rows:] = dk[part, cols]
+            dvt_scr[at, rows:] = dv[part, cols]
+    slope = 1.0 / math.sqrt(head)
+    dq = (dq * slope).astype(BF16)
+    dkt = (dkt_scr[...] * slope).astype(BF16)
     dvt = dvt_scr[...].astype(BF16)
-    norm_t = jnp.concatenate([normt_ref[...], far_normed.T], axis=1)
-    grad_query = dot(normt_ref[...], dq)
-    grad_key = dot_t(norm_t, dkt)
-    grad_value = dot_t(norm_t, dvt)
-    d_normed = (dot(wk_ref[...], dkt) + dot(wv_ref[...], dvt)).T
-    near = d_normed[:rows] + dot_t(dq, wq_ref[...])
-    near_ref[...] = near
-    away = d_normed[rows:]
+    tail_ref[1] = dq
+    tail_ref[2] = dkt[:, :rows]
+    tail_ref[3] = dvt[:, :rows]
+    all_t = jnp.concatenate([norm_t, far_normed.T], axis=1)
+    grad_query = dot(norm_t, dq)
+    grad_key = dot_t(all_t, dkt)
+    grad_value = dot_t(all_t, dvt)
+    away = (dot(wk_ref[...], dkt[:, rows:]) + dot(wv_ref[...], dvt[:, rows:])).T
     away_dx = pull(away * gain, far_hat, far_rstd)
-    grad_scr[...] = jnp.concatenate([grad_query, grad_key, grad_value, grad_out], axis=0)
-    half = grad_scr.shape[0] // 2
-    share = half // chips
-    blank = jnp.zeros((block - share - slots, feats), F32)
-    core = lax.rem(lax.axis_index("nodes"), 2)
+    share = 2 * feats // chips
+    blank = [jnp.zeros((block - share - slots, feats), F32)] * (block > share + slots)
+    first = lax.rem(lax.axis_index("nodes"), 2) == 0
+    low = jnp.concatenate([grad_query, grad_key], axis=0)
+    high = jnp.concatenate([grad_value, grad_out], axis=0)
+    keep = jnp.where(first, low, high)
+    give = jnp.where(first, high, low)
     for c in range(chips):
-        for own in (True, False):
-            which = core if own else 1 - core
-            start = pl.multiple_of(which * half + c * share, 8)
-            dx = [away_dx[(2 * c + i) * slots : (2 * c + i + 1) * slots] for i in range(2)]
-            part = jnp.concatenate(
-                [grad_scr[pl.ds(start, share), :], jnp.where(which == 0, dx[0], dx[1]), blank],
-                axis=0,
-            )
-            if own:
-                keep_ref[c] = part
-            else:
-                give_ref[c] = part.astype(BF16)
+        dx = [away_dx[(2 * c + i) * slots : (2 * c + i + 1) * slots] for i in range(2)]
+        at = slice(c * share, (c + 1) * share)
+        keep_ref[c] = jnp.concatenate(
+            [keep[at], jnp.where(first, dx[0], dx[1])] + blank, axis=0
+        )
+        give_ref[c] = jnp.concatenate(
+            [give[at], jnp.where(first, dx[1], dx[0])] + blank, axis=0
+        ).astype(BF16)
 
 
 def pair_kernel(share, slots, keep_ref, got_ref, out_ref):
@@ -291,12 +312,14 @@
     share_ref[...] = jnp.broadcast_to(total.astype(BF16)[None], share_ref.shape)
 
 
-def own_kernel(gain_at, square_ref, near_ref, att_ref, out_ref, feats_ref):
-    x = square_ref[0].astype(F32)
-    out_ref[...] = (x + dot(att_ref[...], square_ref[4])).astype(BF16)
-    gain = packed_gain(square_ref, gain_at)
-    dx = pull(near_ref[...] * gain, *standardize(x))
-    feats_ref[...] = square_ref[5].astype(F32) + dx
+def own_kernel(gain_at, pack_ref, tail_ref, out_ref, feats_ref):
+    x_ref, wq_ref, wk_ref, wv_ref, wo_ref, cot_ref = [pack_ref.at[i] for i in range(6)]
+    x = x_ref[...].astype(F32)
+    out_ref[...] = (x + dot(tail_ref[0], wo_ref[...])).astype(BF16)
+    d_normed = (dot(wk_ref[...], tail_ref[2]) + dot(wv_ref[...], tail_ref[3])).T
+    d_normed = d_normed + dot_t(tail_ref[1], wq_ref[...])
+    gain = packed_gain(pack_ref, gain_at)
+    feats_ref[...] = cot_ref[...].astype(F32) + pull(d_normed * gain, *standardize(x))
 
 
 def finish_kernel(share, send_ref, got_ref, own_ref, feats_ref):
@@ -367,13 +390,11 @@
     square = like((rows, feats), BF16)
     wide = like((rows, feats), F32)
     edges = edge_dst.shape
-    ints = pltpu.VMEM(edges, jnp.int32)
     picked, pack = call(
         pick_kernel,
         (like((peers, slots, feats), BF16), like((7, rows, feats), BF16)),
-        [HBM] * 11,
-        (pltpu.SMEM((slots, peers), jnp.int32), pltpu.VMEM((rows, feats), F32), ints, ints, ints,
-         pltpu.VMEM((1, feats), F32), pltpu.SemaphoreType.DMA((11,))),
+        [SMEM] + [VMEM] * 10,
+        (pltpu.VMEM((rows, feats), F32),),
         mib=FULL,
     )(send, node_feats, w_query, w_key, w_value, w_out, cotangent, edge_dst, edge_src, edge_mask,
       gain)
@@ -386,25 +407,23 @@
         [VMEM],
         cost=cost,
     )(pack)
-    att, near, keep, give = call(
+    late = pltpu.VMEM((max(HEADS - EARLY, 1), rows, rows), BF16)
+    far_heads = pltpu.VMEM((HEADS // 2, rows, 2 * width), BF16)
+    turned = pltpu.VMEM((feats, rows + width), F32)
+    tail, keep, give = call(
         functools.partial(attend_kernel, edges[0]),
-        (square, wide, like((chips, block, feats), F32), like((chips, block, feats), BF16)),
+        (like((4, rows, feats), BF16), like((chips, block, feats), F32),
+         like((chips, block, feats), BF16)),
         [VMEM] * 7,
-        [
-            pltpu.VMEM((HEADS, rows, rows + width), BF16),
-            pltpu.VMEM((HEADS, rows, rows + width), BF16),
-            pltpu.VMEM((feats, rows + width), F32),
-            pltpu.VMEM((feats, rows + width), F32),
-            pltpu.VMEM((4 * feats, feats), F32),
-        ],
+        [late, late, far_heads, far_heads, turned, turned],
     )(arrived, pack, low, far_count, near_count, w, g)
     given = lax.ppermute(give, "nodes", swap)
     output, own = call(
         functools.partial(own_kernel, gain_row(edges[0], rows, width)),
         (square, wide),
-        [VMEM] * 3,
+        [VMEM] * 2,
         cost=cost,
-    )(pack, near, att)
+    )(pack, tail)
     given, own = lax.optimization_barrier((given, own))
     paired = call(
         functools.partial(pair_kernel, share, slots),

time: 52.8 us -> 50.1 us (0.949)
  Pallas kernels: 14.4 us -> 11.8 us
    pallas_call x1, Pallas kernels: 6.14 us -> 3.48 us  [on_device(): call(functools.partial(attend_kernel, edges[0]), (like((4, rows, feats),...]
  transfers between devices with their start and end apart: 3 -> 3, of which waited for: 2 -> 2; matrix products, arithmetic and copies ran while one was open for 0% -> 0% of each run, Pallas kernels for 9% -> 10%
where the time goes in v5:
time: 50.1 us; the launch traced here: 49.8 us
  blocking collectives  22.6 us (45%)
  Pallas kernels  11.8 us (24%)
  starting transfers between devices  10.9 us (22%)
  waiting for transfers between devices  2.68 us (5%)
  local copies, waits for them, and re-layouts  1.2 us (2%)
  between operations  0.7 us (1%)
    all_to_all x2, blocking collectives, across(): return lax.all_to_all(x, 'nodes', 0, 0, axis_index_groups=sides, tiled=True)  22.6 us
    all_to_all x1, starting transfers between devices, on_device(): lax.all_to_all(picked, 'nodes', split_axis=0, concat_axis=0, tiled=True)  7.35 us
    pallas_call x1, Pallas kernels, on_device(): call(functools.partial(attend_kernel, edges[0]), (like((4, rows, feats),...  3.48 us
    ppermute x1, starting transfers between devices, on_device(): other = lax.ppermute(mine, 'nodes', swap)  2.67 us
    all_to_all x1, waiting for transfers between devices, on_device(): lax.all_to_all(picked, 'nodes', split_axis=0, concat_axis=0, tiled=True)  2.37 us
    pallas_call x1, Pallas kernels, on_device(): call(functools.partial(local_kernel, edges[0]), (like((6, rows, feats), B...  2.36 us
    pallas_call x1, Pallas kernels, on_device(): call(pick_kernel, (like((peers, slots, feats), BF16), like((7, rows, feat...  2.3 us
    pallas_call x1, Pallas kernels, on_device(): call(functools.partial(finish_kernel, share), wide, [SMEM] + [VMEM] * 2,...  1.54 us
  transfers between devices with their start and end apart: 3, of which 2 were waited for; matrix products, arithmetic and copies ran while one was open for 0% of the time, Pallas kernels for 10%

profile of v5, /device:TPU:1, one launch (start us, length us, event | category | flops | bytes accessed | tf_op | source)
XLA Modules:
  0.0 49.8 jit_solution(11058275577597292168)
XLA Ops:
  0.6 2.3 %shard_map.162 = (bf16[16,4,256]{2,1,0:T(4,128)(2,1)}, bf16[7,256,256]{2,1,0:T(8,128)(2,1)}) custom-call(s32[4,16]{1,0:T(4,128)} %bitcast.7, bf16[256,256]{1,0:T(8,128)(2,1)} %refs_0_.1, bf16[256,256]{1,0:T(8,128)(2,1)} %wq_ref.1, bf16[256,256]{1,0:T(8,128)(2,1)} %wk_ref.1, bf16[256,256]{1,0:T(8,128)(2,1)} %wv_ref.1, bf16[256,256]{1,0:T(8,128)(2,1)} %refs_4_.1, ...), custom_call_target="tpu_custom_call" | custom-call | tf_op jit(solution)/shard_map/pallas_call | solution.py:393
  2.9 7.3 %all-to-all-start = ((bf16[16,4,256]{2,1,0:T(4,128)(2,1)}), bf16[16,4,256]{2,1,0:T(4,128)(2,1)S(1)}, u32[]{:S(2)}, u32[]{:S(2)}) async-start(bf16[16,4,256]{2,1,0:T(4,128)(2,1)} %get-tuple-element.27), calls=%async_computation | async-start | bytes 65536 | tf_op jit(solution)/shard_map/all_to_all | solution.py:401
  10.3 0.0 copy-start
  10.3 1.2 %copy-done = bf16[7,256,256]{2,1,0:T(8,128)(2,1)S(1)} copy-done((bf16[7,256,256]{2,1,0:T(8,128)(2,1)S(1)}, bf16[7,256,256]{2,1,0:T(8,128)(2,1)}, u32[]{:S(2)}) %copy-start) | copy-done | bytes 917528
  11.5 0.0 copy-start.1
  11.5 2.4 %shard_map.163 = (bf16[6,256,256]{2,1,0:T(8,128)(2,1)S(1)}, f32[256,128]{1,0:T(8,128)S(1)}, f32[256,256]{1,0:T(8,128)S(1)}, bf16[4,256,256]{2,1,0:T(8,128)(2,1)S(1)}, bf16[4,256,256]{2,1,0:T(8,128)(2,1)S(1)}) custom-call(bf16[7,256,256]{2,1,0:T(8,128)(2,1)S(1)} %copy-done), custom_call_target="tpu_custom_call" | custom-call | flops 8000000000 | bytes 2000000 | tf_op jit(solution)/shard_map/pallas_call | solution.py:403
  13.8 2.4 %all-to-all-done.far_ref = bf16[16,4,256]{2,1,0:T(4,128)(2,1)S(1)} async-done(((bf16[16,4,256]{2,1,0:T(4,128)(2,1)}), bf16[16,4,256]{2,1,0:T(4,128)(2,1)S(1)}, u32[]{:S(2)}, u32[]{:S(2)}) %all-to-all-start) | async-done | bytes 32800 | tf_op jit(solution)/shard_map/all_to_all | solution.py:401
  16.2 0.0 copy-done.1
  16.2 3.5 %shard_map.164 = (bf16[4,256,256]{2,1,0:T(8,128)(2,1)S(1)}, f32[8,72,256]{2,1,0:T(8,128)S(1)}, bf16[8,72,256]{2,1,0:T(8,128)(2,1)S(1)}) custom-call(bf16[16,4,256]{2,1,0:T(4,128)(2,1)S(1)} %all-to-all-done.far_ref, bf16[7,256,256]{2,1,0:T(8,128)(2,1)S(1)} %copy-done.1, bf16[6,256,256]{2,1,0:T(8,128)(2,1)S(1)} %get-tuple-element.28.low_ref, ...), custom_call_target="tpu_custom_call" | custom-call | tf_op jit(solution)/shard_map/pallas_call | solution.py:413
  19.7 0.9 %collective-permute-start = (bf16[8,72,256]{2,1,0:T(8,128)(2,1)S(1)}, bf16[8,72,256]{2,1,0:T(8,128)(2,1)S(1)}, u32[]{:S(2)}, u32[]{:S(2)}) collective-permute-start(bf16[8,72,256]{2,1,0:T(8,128)(2,1)S(1)} %get-tuple-element.36), channel_id=1, source_target_pairs={{0,1},{1,0},{2,3},{3,2},{4,5},{5,4},{6,7},{7,6},{8,9},{9,8},{10,11... | collective-permute-start | bytes 884744 | tf_op jit(solution)/shard_map/ppermute | solution.py:420
  20.6 0.9 %shard_map.165 = (bf16[256,256]{1,0:T(8,128)(2,1)}, f32[256,256]{1,0:T(8,128)S(1)}) custom-call(bf16[7,256,256]{2,1,0:T(8,128)(2,1)S(1)} %copy-done.1, bf16[4,256,256]{2,1,0:T(8,128)(2,1)S(1)} %get-tuple-element.33.tail_ref), custom_call_target="tpu_custom_call" | custom-call | flops 8000000000 | bytes 2000000 | tf_op jit(solution)/shard_map/pallas_call | solution.py:421
  21.5 0.3 collective-permute-done.got_ref
  21.8 0.1 shard_map.166
  21.8 11.3 %all_to_all.15.got_ref = bf16[8,72,256]{2,1,0:T(8,128)(2,1)S(1)} all-to-all(bf16[8,72,256]{2,1,0:T(8,128)(2,1)S(1)} %shard_map.166), channel_id=1, replica_groups={{0,2,4,6,8,10,12,14},{1,3,5,7,9,11,13,15},{16,18,20,22,24,26,28,30},{17..., dimensions={0} | all-to-all | bytes 589824 | tf_op jit(solution)/shard_map/all_to_all | solution.py:387
  33.1 0.0 copy-start.6
  33.2 11.3 %all_to_all.16.mine_ref = bf16[8,64,256]{2,1,0:T(8,128)(2,1)S(1)} all-to-all(bf16[8,64,256]{2,1,0:T(8,128)(2,1)S(1)} %shard_map.168), channel_id=1, replica_groups={{0,2,4,6,8,10,12,14},{1,3,5,7,9,11,13,15},{16,18,20,22,24,26,28,30},{17..., dimensions={0} | all-to-all | bytes 524288 | tf_op jit(solution)/shard_map/all_to_all | solution.py:387
  44.5 0.0 copy-start.2
  44.5 0.0 copy-start.3
  44.5 0.0 copy-start.4
  44.5 0.0 copy-start.5
  44.5 2.7 %collective-permute-start.1 = (bf16[8,64,256]{2,1,0:T(8,128)(2,1)S(1)}, bf16[8,64,256]{2,1,0:T(8,128)(2,1)S(1)}, u32[]{:S(2)}, u32[]{:S(2)}) collective-permute-start(bf16[8,64,256]{2,1,0:T(8,128)(2,1)S(1)} %all_to_all.16.mine_ref), channel_id=1, source_target_pairs={{0,1},{1,0},{2,3},{3,2},{4,5},{5,4},{6,7},{7,6},{8,9},{9,8},{10,11... | collective-permute-start | bytes 786440 | tf_op jit(solution)/shard_map/ppermute | solution.py:436
  47.1 0.0 copy-done.6
  47.1 1.5 %shard_map.167 = f32[256,256]{1,0:T(8,128)} custom-call(s32[4,16]{1,0:T(4,128)S(1)} %bitcast.8, bf16[8,72,256]{2,1,0:T(8,128)(2,1)S(1)} %all_to_all.15.got_ref, f32[256,256]{1,0:T(8,128)S(1)} %get-tuple-element.39.own_ref), custom_call_target="tpu_custom_call" | custom-call | flops 8000000000 | bytes 2000000 | tf_op jit(solution)/shard_map/pallas_call | solution.py:437
  48.7 0.0 collective-permute-done.1.other_ref
  48.7 0.0 copy-done.2
  48.7 0.0 copy-done.3
  48.7 0.0 copy-done.4
  48.7 0.0 copy-done.5
  48.7 1.1 %shard_map.169 = (f32[256,256]{1,0:T(8,128)}, f32[256,256]{1,0:T(8,128)}, f32[256,256]{1,0:T(8,128)}, f32[256,256]{1,0:T(8,128)}, f32[1,256]{1,0:T(1,128)}) custom-call(bf16[8,64,256]{2,1,0:T(8,128)(2,1)S(1)} %all_to_all.16.mine_ref, bf16[8,64,256]{2,1,0:T(8,128)(2,1)S(1)} %collective-permute-done.1.other_ref, f32[1,256]{1,0:T(1,128)S(1)} %bitcast.6, ...), custom_call_target="tpu_custom_call" | custom-call | tf_op jit(solution)/shard_map/pallas_call | solution.py:440
  (1 shorter events, 0.0 us)
Async XLA Ops:
  2.9 13.3 %all-to-all-start = ((bf16[16,4,256]{2,1,0:T(4,128)(2,1)}), bf16[16,4,256]{2,1,0:T(4,128)(2,1)S(1)}, u32[]{:S(2)}, u32[]{:S(2)}) async-start(bf16[16,4,256]{2,1,0:T(4,128)(2,1)} %get-tuple-element.27), calls=%async_computation | async-start | bytes 65536 | tf_op jit(solution)/shard_map/all_to_all | solution.py:401
  10.3 1.2 %copy-start = (bf16[7,256,256]{2,1,0:T(8,128)(2,1)S(1)}, bf16[7,256,256]{2,1,0:T(8,128)(2,1)}, u32[]{:S(2)}) copy-start(bf16[7,256,256]{2,1,0:T(8,128)(2,1)} %get-tuple-element.26.pack_ref) | copy-start | bytes 2752516
  11.5 4.7 %copy-start.1 = (bf16[7,256,256]{2,1,0:T(8,128)(2,1)S(1)}, bf16[7,256,256]{2,1,0:T(8,128)(2,1)}, u32[]{:S(2)}) copy-start(bf16[7,256,256]{2,1,0:T(8,128)(2,1)} %get-tuple-element.26.pack_ref) | copy-start | bytes 2752516
  19.7 2.1 %collective-permute-start = (bf16[8,72,256]{2,1,0:T(8,128)(2,1)S(1)}, bf16[8,72,256]{2,1,0:T(8,128)(2,1)S(1)}, u32[]{:S(2)}, u32[]{:S(2)}) collective-permute-start(bf16[8,72,256]{2,1,0:T(8,128)(2,1)S(1)} %get-tuple-element.36), channel_id=1, source_target_pairs={{0,1},{1,0},{2,3},{3,2},{4,5},{5,4},{6,7},{7,6},{8,9},{9,8},{10,11... | collective-permute-start | bytes 884744 | tf_op jit(solution)/shard_map/ppermute | solution.py:420
  33.1 14.0 %copy-start.6 = (s32[1,16,4]{1,2,0:T(4,128)S(1)}, s32[1,16,4]{1,2,0:T(4,128)}, u32[]{:S(2)}) copy-start(s32[1,16,4]{1,2,0:T(4,128)} %param.21) | copy-start | bytes 772
  44.5 4.2 %copy-start.2 = (bf16[256,256]{1,0:T(8,128)(2,1)S(1)}, bf16[256,256]{1,0:T(8,128)(2,1)}, u32[]{:S(2)}) copy-start(bf16[256,256]{1,0:T(8,128)(2,1)} %wq_ref.1) | copy-start | bytes 393220
  44.5 4.2 %copy-start.3 = (bf16[256,256]{1,0:T(8,128)(2,1)S(1)}, bf16[256,256]{1,0:T(8,128)(2,1)}, u32[]{:S(2)}) copy-start(bf16[256,256]{1,0:T(8,128)(2,1)} %wk_ref.1) | copy-start | bytes 393220
  44.5 4.2 %copy-start.4 = (bf16[256,256]{1,0:T(8,128)(2,1)S(1)}, bf16[256,256]{1,0:T(8,128)(2,1)}, u32[]{:S(2)}) copy-start(bf16[256,256]{1,0:T(8,128)(2,1)} %wv_ref.1) | copy-start | bytes 393220
  44.5 4.2 %copy-start.5 = (f32[256]{0:T(256)S(1)}, f32[256]{0:T(256)}, u32[]{:S(2)}) copy-start(f32[256]{0:T(256)} %param.12) | copy-start | bytes 3076
  44.5 4.2 %collective-permute-start.1 = (bf16[8,64,256]{2,1,0:T(8,128)(2,1)S(1)}, bf16[8,64,256]{2,1,0:T(8,128)(2,1)S(1)}, u32[]{:S(2)}, u32[]{:S(2)}) collective-permute-start(bf16[8,64,256]{2,1,0:T(8,128)(2,1)S(1)} %all_to_all.16.mine_ref), channel_id=1, source_target_pairs={{0,1},{1,0},{2,3},{3,2},{4,5},{5,4},{6,7},{7,6},{8,9},{9,8},{10,11... | collective-permute-start | bytes 786440 | tf_op jit(solution)/shard_map/ppermute | solution.py:436

commit v6 on v5

--- a/solution.py
+++ b/solution.py
@@ -9,7 +9,7 @@
 from jax.sharding import PartitionSpec as P
 
 HEADS = 8
-EARLY = 4
+EARLY = 5
 EPS = 1e-05
 F32 = jnp.float32
 BF16 = jnp.bfloat16
@@ -44,8 +44,8 @@
 
 
 def pick_kernel(send_ref, *refs):
-    squares = refs[:6]
-    dst_ref, src_ref, mask_ref, gain_ref, out_ref, pack_ref, wide = refs[6:]
+    squares = refs[:4]
+    dst_ref, src_ref, mask_ref, gain_ref, out_ref, pack_ref, wide = refs[4:]
     slots, peers = send_ref.shape
     rows, feats = wide.shape
     wide[...] = squares[0][...].astype(F32)
@@ -68,7 +68,7 @@
     gains = [first, second, gain - first - second]
     used = sum(t.shape[0] for t in tall)
     blank = jnp.zeros((rows - used - 3, feats), F32)
-    pack_ref[6] = jnp.concatenate(tall + gains + [blank], axis=0).astype(BF16)
+    pack_ref[4] = jnp.concatenate(tall + gains + [blank], axis=0).astype(BF16)
 
 
 def gain_row(edge_rows, rows, width):
@@ -77,7 +77,7 @@
 
 
 def packed_gain(pack_ref, at):
-    parts = pack_ref[6].astype(F32)[at : at + 3]
+    parts = pack_ref[4].astype(F32)[at : at + 3]
     return parts[0:1] + parts[1:2] + parts[2:3]
 
 
@@ -95,11 +95,11 @@
 
 
 def local_kernel(edge_rows, pack_ref, low_ref, far_count, near_count, w_ref, g_ref):
-    x_ref, wq_ref, wk_ref, wv_ref, wo_ref, cot_ref = [pack_ref.at[i] for i in range(6)]
+    x_ref, wq_ref, wk_ref, wv_ref = [pack_ref.at[i] for i in range(4)]
     rows, width = far_count.shape
     gain = packed_gain(pack_ref, gain_row(edge_rows, rows, width))
     queries, keys = local_project(
-        x_ref, gain, wq_ref, wk_ref, wv_ref, wo_ref, cot_ref, low_ref
+        x_ref, gain, wq_ref, wk_ref, wv_ref, low_ref
     )
     feats = queries.shape[1]
     local_count(edge_rows, pack_ref, far_count, near_count)
@@ -108,7 +108,7 @@
         w_ref[h], g_ref[h] = weigh(queries * hots[h], keys, near_count[...], feats // HEADS)
 
 
-def local_project(x_ref, gain, wq_ref, wk_ref, wv_ref, wo_ref, cot_ref, low_ref):
+def local_project(x_ref, gain, wq_ref, wk_ref, wv_ref, low_ref):
     xhat, _ = standardize(x_ref[...].astype(F32))
     normed = (xhat * gain).astype(BF16)
     queries = dot(normed, wq_ref[...]).astype(BF16)
@@ -118,7 +118,6 @@
     low_ref[2] = dot(normed, wv_ref[...]).astype(BF16)
     low_ref[3] = queries.T
     low_ref[4] = normed.T
-    low_ref[5] = dot_t(cot_ref[...], wo_ref[...]).astype(BF16)
     return queries, keys
 
 
@@ -126,7 +125,7 @@
     rows, far = far_count.shape
     edge = 128
     group = 8
-    table = pack_ref[6].astype(F32)
+    table = pack_ref[4].astype(F32)
 
     def part(i):
         at = i // 2 * edge_rows
@@ -157,13 +156,14 @@
 
 
 def attend_kernel(
-    edge_rows, far_ref, pack_ref, low_ref, far_count, near_count, near_w, near_g,
+    edge_rows, far_ref, pack_ref, wo_ref, cot_ref, low_ref, far_count, near_count, near_w, near_g,
     tail_ref, keep_ref, give_ref,
     w_scr, g_scr, far_w, far_g, dkt_scr, dvt_scr,
 ):
-    _, wq_ref, wk_ref, wv_ref, _, cot_ref = [pack_ref.at[i] for i in range(6)]
+    _, wq_ref, wk_ref, wv_ref = [pack_ref.at[i] for i in range(4)]
     _, rows, feats = low_ref.shape
-    queries, keys, values, qt, norm_t, datt = [low_ref[i] for i in range(6)]
+    queries, keys, values, qt, norm_t = [low_ref[i] for i in range(5)]
+    datt = dot_t(cot_ref[...], wo_ref[...]).astype(BF16)
     peers, slots, _ = far_ref.shape
     far = peers * slots
     width = far_count.shape[1]
@@ -312,8 +312,8 @@
     share_ref[...] = jnp.broadcast_to(total.astype(BF16)[None], share_ref.shape)
 
 
-def own_kernel(gain_at, pack_ref, tail_ref, out_ref, feats_ref):
-    x_ref, wq_ref, wk_ref, wv_ref, wo_ref, cot_ref = [pack_ref.at[i] for i in range(6)]
+def own_kernel(gain_at, pack_ref, wo_ref, cot_ref, tail_ref, out_ref, feats_ref):
+    x_ref, wq_ref, wk_ref, wv_ref = [pack_ref.at[i] for i in range(4)]
     x = x_ref[...].astype(F32)
     out_ref[...] = (x + dot(tail_ref[0], wo_ref[...])).astype(BF16)
     d_normed = (dot(wk_ref[...], tail_ref[2]) + dot(wv_ref[...], tail_ref[3])).T
@@ -392,17 +392,16 @@
     edges = edge_dst.shape
     picked, pack = call(
         pick_kernel,
-        (like((peers, slots, feats), BF16), like((7, rows, feats), BF16)),
-        [SMEM] + [VMEM] * 10,
+        (like((peers, slots, feats), BF16), like((5, rows, feats), BF16)),
+        [SMEM] + [VMEM] * 8,
         (pltpu.VMEM((rows, feats), F32),),
         mib=FULL,
-    )(send, node_feats, w_query, w_key, w_value, w_out, cotangent, edge_dst, edge_src, edge_mask,
-      gain)
+    )(send, node_feats, w_query, w_key, w_value, edge_dst, edge_src, edge_mask, gain)
     arrived = lax.all_to_all(picked, "nodes", split_axis=0, concat_axis=0, tiled=True)
     heads = like((EARLY, rows, rows), BF16)
     low, far_count, near_count, w, g = call(
         functools.partial(local_kernel, edges[0]),
-        (like((6, rows, feats), BF16), like((rows, width), F32), like((rows, rows), F32),
+        (like((5, rows, feats), BF16), like((rows, width), F32), like((rows, rows), F32),
          heads, heads),
         [VMEM],
         cost=cost,
@@ -414,16 +413,16 @@
         functools.partial(attend_kernel, edges[0]),
         (like((4, rows, feats), BF16), like((chips, block, feats), F32),
          like((chips, block, feats), BF16)),
-        [VMEM] * 7,
+        [VMEM] * 9,
         [late, late, far_heads, far_heads, turned, turned],
-    )(arrived, pack, low, far_count, near_count, w, g)
+    )(arrived, pack, w_out, cotangent, low, far_count, near_count, w, g)
     given = lax.ppermute(give, "nodes", swap)
     output, own = call(
         functools.partial(own_kernel, gain_row(edges[0], rows, width)),
         (square, wide),
-        [VMEM] * 2,
+        [VMEM] * 4,
         cost=cost,
-    )(pack, tail)
+    )(pack, w_out, cotangent, tail)
     given, own = lax.optimization_barrier((given, own))
     paired = call(
         functools.partial(pair_kernel, share, slots),

time: 50.1 us -> 49.8 us (level)
    unnamed x14 -> x18, local copies, waits for them, and re-layouts: 1.2 us -> 1.12 us
where the time goes in v6:
time: 49.8 us; the launch traced here: 49.4 us
  blocking collectives  22.6 us (45%)
  Pallas kernels  11.4 us (23%)
  starting transfers between devices  10.9 us (22%)
  waiting for transfers between devices  2.74 us (6%)
  local copies, waits for them, and re-layouts  1.12 us (2%)
  between operations  0.7 us (1%)
    all_to_all x2, blocking collectives, across(): return lax.all_to_all(x, 'nodes', 0, 0, axis_index_groups=sides, tiled=True)  22.6 us
    all_to_all x1, starting transfers between devices, on_device(): lax.all_to_all(picked, 'nodes', split_axis=0, concat_axis=0, tiled=True)  7.35 us
    pallas_call x1, Pallas kernels, on_device(): call(functools.partial(attend_kernel, edges[0]), (like((4, rows, feats),...  3.33 us
    ppermute x1, starting transfers between devices, on_device(): other = lax.ppermute(mine, 'nodes', swap)  2.66 us
    all_to_all x1, waiting for transfers between devices, on_device(): lax.all_to_all(picked, 'nodes', split_axis=0, concat_axis=0, tiled=True)  2.43 us
    pallas_call x1, Pallas kernels, on_device(): call(functools.partial(local_kernel, edges[0]), (like((5, rows, feats), B...  2.39 us
    pallas_call x1, Pallas kernels, on_device(): call(pick_kernel, (like((peers, slots, feats), BF16), like((5, rows, feat...  2.09 us
    pallas_call x1, Pallas kernels, on_device(): call(functools.partial(finish_kernel, share), wide, [SMEM] + [VMEM] * 2,...  1.54 us
  transfers between devices with their start and end apart: 3, of which 2 were waited for; matrix products, arithmetic and copies ran while one was open for 0% of the time, Pallas kernels for 10%

profile of v6, /device:TPU:1, one launch (start us, length us, event | category | flops | bytes accessed | tf_op | source)
XLA Modules:
  0.0 49.4 jit_solution(12765164543718213130)
XLA Ops:
  0.6 2.1 %shard_map.162 = (bf16[16,4,256]{2,1,0:T(4,128)(2,1)}, bf16[5,256,256]{2,1,0:T(8,128)(2,1)}) custom-call(s32[4,16]{1,0:T(4,128)} %bitcast.7, bf16[256,256]{1,0:T(8,128)(2,1)} %refs_0_.1, bf16[256,256]{1,0:T(8,128)(2,1)} %wq_ref.1, bf16[256,256]{1,0:T(8,128)(2,1)} %wk_ref.1, bf16[256,256]{1,0:T(8,128)(2,1)} %wv_ref.1, s32[48,128]{1,0:T(8,128)} %refs_4_.1, ...), custom_call_target="tpu_custom_call" | custom-call | tf_op jit(solution)/shard_map/pallas_call | solution.py:393
  2.7 7.3 %all-to-all-start = ((bf16[16,4,256]{2,1,0:T(4,128)(2,1)}), bf16[16,4,256]{2,1,0:T(4,128)(2,1)S(1)}, u32[]{:S(2)}, u32[]{:S(2)}) async-start(bf16[16,4,256]{2,1,0:T(4,128)(2,1)} %get-tuple-element.27), calls=%async_computation | async-start | bytes 65536 | tf_op jit(solution)/shard_map/all_to_all | solution.py:400
  10.1 0.0 copy-start
  10.1 1.1 %copy-done = bf16[5,256,256]{2,1,0:T(8,128)(2,1)S(1)} copy-done((bf16[5,256,256]{2,1,0:T(8,128)(2,1)S(1)}, bf16[5,256,256]{2,1,0:T(8,128)(2,1)}, u32[]{:S(2)}) %copy-start) | copy-done | bytes 655384
  11.2 0.0 copy-start.1
  11.2 0.0 copy-start.5
  11.2 0.0 copy-start.6
  11.2 2.4 %shard_map.163 = (bf16[5,256,256]{2,1,0:T(8,128)(2,1)S(1)}, f32[256,128]{1,0:T(8,128)S(1)}, f32[256,256]{1,0:T(8,128)S(1)}, bf16[5,256,256]{2,1,0:T(8,128)(2,1)S(1)}, bf16[5,256,256]{2,1,0:T(8,128)(2,1)S(1)}) custom-call(bf16[5,256,256]{2,1,0:T(8,128)(2,1)S(1)} %copy-done), custom_call_target="tpu_custom_call" | custom-call | flops 8000000000 | bytes 2000000 | tf_op jit(solution)/shard_map/pallas_call | solution.py:402
  13.6 2.4 %all-to-all-done.far_ref = bf16[16,4,256]{2,1,0:T(4,128)(2,1)S(1)} async-done(((bf16[16,4,256]{2,1,0:T(4,128)(2,1)}), bf16[16,4,256]{2,1,0:T(4,128)(2,1)S(1)}, u32[]{:S(2)}, u32[]{:S(2)}) %all-to-all-start) | async-done | bytes 32800 | tf_op jit(solution)/shard_map/all_to_all | solution.py:400
  16.0 0.0 copy-done.1
  16.0 0.0 copy-done.5
  16.0 0.0 copy-done.6
  16.0 3.3 %shard_map.164 = (bf16[4,256,256]{2,1,0:T(8,128)(2,1)S(1)}, f32[8,72,256]{2,1,0:T(8,128)S(1)}, bf16[8,72,256]{2,1,0:T(8,128)(2,1)S(1)}) custom-call(bf16[16,4,256]{2,1,0:T(4,128)(2,1)S(1)} %all-to-all-done.far_ref, bf16[5,256,256]{2,1,0:T(8,128)(2,1)S(1)} %copy-done.1, bf16[256,256]{1,0:T(8,128)(2,1)S(1)} %copy-done.5, bf16[256,256]{1,0:T(8,128)(2,1)S(1)} %copy-done.6, ...), custom_call_target="tpu_custom_call" | custom-call | tf_op jit(solution)/shard_map/pallas_call | solution.py:412
  19.3 0.9 %collective-permute-start = (bf16[8,72,256]{2,1,0:T(8,128)(2,1)S(1)}, bf16[8,72,256]{2,1,0:T(8,128)(2,1)S(1)}, u32[]{:S(2)}, u32[]{:S(2)}) collective-permute-start(bf16[8,72,256]{2,1,0:T(8,128)(2,1)S(1)} %get-tuple-element.36), channel_id=1, source_target_pairs={{0,1},{1,0},{2,3},{3,2},{4,5},{5,4},{6,7},{7,6},{8,9},{9,8},{10,11... | collective-permute-start | bytes 884744 | tf_op jit(solution)/shard_map/ppermute | solution.py:419
  20.2 0.9 %shard_map.165 = (bf16[256,256]{1,0:T(8,128)(2,1)}, f32[256,256]{1,0:T(8,128)S(1)}) custom-call(bf16[5,256,256]{2,1,0:T(8,128)(2,1)S(1)} %copy-done.1, bf16[256,256]{1,0:T(8,128)(2,1)S(1)} %copy-done.5, bf16[256,256]{1,0:T(8,128)(2,1)S(1)} %copy-done.6, bf16[4,256,256]{2,1,0:T(8,128)(2,1)S(1)} %get-tuple-element.33.tail_ref), custom_call_target="tpu_custom_call" | custom-call | flops 8000000000 | bytes 2000000 | tf_op jit(solution)/shard_map/pallas_call | solution.py:420
  21.1 0.3 collective-permute-done.got_ref
  21.4 0.1 shard_map.166
  21.5 11.3 %all_to_all.15.got_ref = bf16[8,72,256]{2,1,0:T(8,128)(2,1)S(1)} all-to-all(bf16[8,72,256]{2,1,0:T(8,128)(2,1)S(1)} %shard_map.166), channel_id=1, replica_groups={{0,2,4,6,8,10,12,14},{1,3,5,7,9,11,13,15},{16,18,20,22,24,26,28,30},{17..., dimensions={0} | all-to-all | bytes 589824 | tf_op jit(solution)/shard_map/all_to_all | solution.py:387
  32.8 0.0 copy-start.8
  32.8 11.3 %all_to_all.16.mine_ref = bf16[8,64,256]{2,1,0:T(8,128)(2,1)S(1)} all-to-all(bf16[8,64,256]{2,1,0:T(8,128)(2,1)S(1)} %shard_map.168), channel_id=1, replica_groups={{0,2,4,6,8,10,12,14},{1,3,5,7,9,11,13,15},{16,18,20,22,24,26,28,30},{17..., dimensions={0} | all-to-all | bytes 524288 | tf_op jit(solution)/shard_map/all_to_all | solution.py:387
  44.1 0.0 copy-start.2
  44.1 0.0 copy-start.3
  44.1 0.0 copy-start.4
  44.1 2.7 %collective-permute-start.1 = (bf16[8,64,256]{2,1,0:T(8,128)(2,1)S(1)}, bf16[8,64,256]{2,1,0:T(8,128)(2,1)S(1)}, u32[]{:S(2)}, u32[]{:S(2)}) collective-permute-start(bf16[8,64,256]{2,1,0:T(8,128)(2,1)S(1)} %all_to_all.16.mine_ref), channel_id=1, source_target_pairs={{0,1},{1,0},{2,3},{3,2},{4,5},{5,4},{6,7},{7,6},{8,9},{9,8},{10,11... | collective-permute-start | bytes 786440 | tf_op jit(solution)/shard_map/ppermute | solution.py:435
  46.8 0.0 copy-done.8
  46.8 1.5 %shard_map.167 = f32[256,256]{1,0:T(8,128)} custom-call(s32[4,16]{1,0:T(4,128)S(1)} %bitcast.8, bf16[8,72,256]{2,1,0:T(8,128)(2,1)S(1)} %all_to_all.15.got_ref, f32[256,256]{1,0:T(8,128)S(1)} %get-tuple-element.39.own_ref), custom_call_target="tpu_custom_call" | custom-call | flops 8000000000 | bytes 2000000 | tf_op jit(solution)/shard_map/pallas_call | solution.py:436
  48.3 0.0 collective-permute-done.1.other_ref
  48.3 0.0 copy-done.2
  48.3 0.0 copy-done.3
  48.3 0.0 copy-done.4
  48.3 0.0 copy-done.7
  48.4 1.1 %shard_map.169 = (f32[256,256]{1,0:T(8,128)}, f32[256,256]{1,0:T(8,128)}, f32[256,256]{1,0:T(8,128)}, f32[256,256]{1,0:T(8,128)}, f32[1,256]{1,0:T(1,128)}) custom-call(bf16[8,64,256]{2,1,0:T(8,128)(2,1)S(1)} %all_to_all.16.mine_ref, bf16[8,64,256]{2,1,0:T(8,128)(2,1)S(1)} %collective-permute-done.1.other_ref, f32[1,256]{1,0:T(1,128)S(1)} %bitcast.6, ...), custom_call_target="tpu_custom_call" | custom-call | tf_op jit(solution)/shard_map/pallas_call | solution.py:439
  (2 shorter events, 0.0 us)
Async XLA Ops:
  2.7 13.3 %all-to-all-start = ((bf16[16,4,256]{2,1,0:T(4,128)(2,1)}), bf16[16,4,256]{2,1,0:T(4,128)(2,1)S(1)}, u32[]{:S(2)}, u32[]{:S(2)}) async-start(bf16[16,4,256]{2,1,0:T(4,128)(2,1)} %get-tuple-element.27), calls=%async_computation | async-start | bytes 65536 | tf_op jit(solution)/shard_map/all_to_all | solution.py:400
  10.1 1.1 %copy-start = (bf16[5,256,256]{2,1,0:T(8,128)(2,1)S(1)}, bf16[5,256,256]{2,1,0:T(8,128)(2,1)}, u32[]{:S(2)}) copy-start(bf16[5,256,256]{2,1,0:T(8,128)(2,1)} %get-tuple-element.26.pack_ref) | copy-start | bytes 1966084
  11.2 4.8 %copy-start.1 = (bf16[5,256,256]{2,1,0:T(8,128)(2,1)S(1)}, bf16[5,256,256]{2,1,0:T(8,128)(2,1)}, u32[]{:S(2)}) copy-start(bf16[5,256,256]{2,1,0:T(8,128)(2,1)} %get-tuple-element.26.pack_ref) | copy-start | bytes 1966084
  11.2 4.8 %copy-start.5 = (bf16[256,256]{1,0:T(8,128)(2,1)S(1)}, bf16[256,256]{1,0:T(8,128)(2,1)}, u32[]{:S(2)}) copy-start(bf16[256,256]{1,0:T(8,128)(2,1)} %wo_ref.3) | copy-start | bytes 393220
  11.2 4.8 %copy-start.6 = (bf16[256,256]{1,0:T(8,128)(2,1)S(1)}, bf16[256,256]{1,0:T(8,128)(2,1)}, u32[]{:S(2)}) copy-start(bf16[256,256]{1,0:T(8,128)(2,1)} %cot_ref.3) | copy-start | bytes 393220
  19.3 2.1 %collective-permute-start = (bf16[8,72,256]{2,1,0:T(8,128)(2,1)S(1)}, bf16[8,72,256]{2,1,0:T(8,128)(2,1)S(1)}, u32[]{:S(2)}, u32[]{:S(2)}) collective-permute-start(bf16[8,72,256]{2,1,0:T(8,128)(2,1)S(1)} %get-tuple-element.36), channel_id=1, source_target_pairs={{0,1},{1,0},{2,3},{3,2},{4,5},{5,4},{6,7},{7,6},{8,9},{9,8},{10,11... | collective-permute-start | bytes 884744 | tf_op jit(solution)/shard_map/ppermute | solution.py:419
  32.8 14.0 %copy-start.8 = (s32[1,16,4]{1,2,0:T(4,128)S(1)}, s32[1,16,4]{1,2,0:T(4,128)}, u32[]{:S(2)}) copy-start(s32[1,16,4]{1,2,0:T(4,128)} %param.21) | copy-start | bytes 772
  44.1 4.2 %copy-start.2 = (bf16[256,256]{1,0:T(8,128)(2,1)S(1)}, bf16[256,256]{1,0:T(8,128)(2,1)}, u32[]{:S(2)}) copy-start(bf16[256,256]{1,0:T(8,128)(2,1)} %wq_ref.1) | copy-start | bytes 393220
  44.1 4.2 %copy-start.3 = (bf16[256,256]{1,0:T(8,128)(2,1)S(1)}, bf16[256,256]{1,0:T(8,128)(2,1)}, u32[]{:S(2)}) copy-start(bf16[256,256]{1,0:T(8,128)(2,1)} %wk_ref.1) | copy-start | bytes 393220
  44.1 4.2 %copy-start.4 = (bf16[256,256]{1,0:T(8,128)(2,1)S(1)}, bf16[256,256]{1,0:T(8,128)(2,1)}, u32[]{:S(2)}) copy-start(bf16[256,256]{1,0:T(8,128)(2,1)} %wv_ref.1) | copy-start | bytes 393220
  44.1 4.2 %copy-start.7 = (f32[256]{0:T(256)S(1)}, f32[256]{0:T(256)}, u32[]{:S(2)}) copy-start(f32[256]{0:T(256)} %param.12) | copy-start | bytes 3076
  44.1 4.2 %collective-permute-start.1 = (bf16[8,64,256]{2,1,0:T(8,128)(2,1)S(1)}, bf16[8,64,256]{2,1,0:T(8,128)(2,1)S(1)}, u32[]{:S(2)}, u32[]{:S(2)}) collective-permute-start(bf16[8,64,256]{2,1,0:T(8,128)(2,1)S(1)} %all_to_all.16.mine_ref), channel_id=1, source_target_pairs={{0,1},{1,0},{2,3},{3,2},{4,5},{5,4},{6,7},{7,6},{8,9},{9,8},{10,11... | collective-permute-start | bytes 786440 | tf_op jit(solution)/shard_map/ppermute | solution.py:435
